TPU v7x, 128 devices: a whole 4x4x4 slice. The times are simulated.
128 devices in a mesh: dp: 4 (over y), seq: 32 (over z, x, core).
Axes of the slice: x: 4, y: 4, z: 4, core: 2. Of those that a mesh axis runs over, the one named last changes fastest.
Arguments:
- byte_keys: bfloat16 [4, 65536, 1024], P('dp', 'seq')
- byte_values: bfloat16 [4, 65536, 1024], P('dp', 'seq'), may hold values from -6 to 6
- doc_ids: int32 [4, 65536], P('dp', 'seq'), may hold values from 0 to 255, as said below
- queries: bfloat16 [4, 16384, 1024], P('dp', 'seq')
- patch_end: int32 [4, 16384], P('dp', 'seq'), may hold values from 1 to 65536, as said below
- cotangent: bfloat16 [4, 16384, 4096], P('dp', 'seq'), may hold values from -6 to 6
- proj_weight: bfloat16 [4096, 1024], P('seq'), may hold values from -0.1875 to 0.1875
- norm_gain: float32 [4096], replicated, may hold values from 0.25 to 1.75
Outputs:
- d_queries: bfloat16 [4, 16384, 1024], P('dp', 'seq')
- d_keys: bfloat16 [4, 65536, 1024], P('dp', 'seq')
- d_values: bfloat16 [4, 65536, 1024], P('dp', 'seq')
- d_proj: float32 [4096, 1024], P('seq')
- d_gain: float32 [4096], replicated
Inputs may be any that keep to these rules, and one draw needn't show every extreme that they name: `patch_end`: within a stream the ends rise strictly, each patch has 1 to 7 bytes, the last end is 65536; for every rank d from 1 to the seq size less 1, patch d * 512 - 1 ends at d * 2048 + e with -256 <= e <= 256, and in every stream e = -256 occurs at some rank and e = 256 at another; some patch has 7 bytes in every stream. `doc_ids`: within a stream the numbers never fall, start at 0, change only at bytes where a patch begins, and rise by one at each change; every stream holds exactly 256 documents.
All inputs are finite; a program needn't handle non-finite values.
Results may differ from a plain program's by a relative error of at most 0.024.
Values may be sent and summed in bfloat16 or wider, within the bound.
No kernel may reach another device: no remote copies, remote signals or barrier semaphores. Data moves between devices by JAX's collectives and lax.ppermute only.
A program may use at most 192 MiB of HBM per device.

v0:
```python
import math

import jax
import jax.numpy as jnp
from jax import lax
from jax.sharding import PartitionSpec as P

HEADS = 8
HD = 128
WIN = 128
PG = 64
HALO = 384
SLAB = 576


masked_score = -1e30
epsilon = 1e-05


def padded(block, sides, width):
    for axis, dim in sides:
        count = lax.axis_size(axis)
        forward = [(i, i + 1) for i in range(count - 1)]
        backward = [(target, source) for source, target in forward]
        low = lax.ppermute(
            lax.slice_in_dim(block, block.shape[dim] - width, None, axis=dim), axis, forward
        )
        high = lax.ppermute(lax.slice_in_dim(block, 0, width, axis=dim), axis, backward)
        block = jnp.concatenate([low, block, high], axis=dim)
    return block


def shifted(block, axis, distance):
    devices = range(lax.axis_size(axis))
    route = [(i - distance, i) for i in devices if i - distance in devices]
    return lax.ppermute(block, axis, route)


def block_probs(query_group, key_slab, visible):
    score_scale = 1.0 / math.sqrt(HD)
    scores = (
        jnp.einsum("phd,jhd->hpj", query_group, key_slab, preferred_element_type=jnp.float32)
        * score_scale
    )
    scores = jnp.where(visible[None], scores, masked_score)
    top_score = jnp.max(scores, axis=2, keepdims=True)
    expo = jnp.exp(scores - top_score)
    return expo / jnp.sum(expo, axis=2, keepdims=True)


def on_device(
    byte_keys, byte_values, doc_ids, queries, patch_end, cotangent, proj_weight, norm_gain
):
    score_scale = 1.0 / math.sqrt(HD)
    byte_dev = byte_keys.shape[1]
    attn_width = byte_keys.shape[2]
    patch_dev = queries.shape[1]
    seq_count = lax.axis_size("seq")
    seq_rank = lax.axis_index("seq")
    total_bytes = byte_dev * seq_count
    rim_rows = HALO
    byte_pair = jnp.concatenate([byte_keys[0], byte_values[0]], axis=1)
    wide_pair, wide_doc = (
        padded(byte_pair, (("seq", 0),), rim_rows),
        padded(doc_ids[0], (("seq", 0),), rim_rows),
    )
    ext_rows = wide_pair.shape[0]
    first_byte = seq_rank * byte_dev - rim_rows
    patch_ends = patch_end[0]
    last_doc = jnp.take(wide_doc, patch_ends - 1 - first_byte)
    groups = patch_dev // PG
    local_queries = queries[0]

    def setup(index):
        ends_here = lax.dynamic_slice_in_dim(patch_ends, index * PG, PG)
        docs_here = lax.dynamic_slice_in_dim(last_doc, index * PG, PG)
        offset = jnp.clip(ends_here[0] - WIN - first_byte, 0, ext_rows - SLAB)
        slab = lax.dynamic_slice_in_dim(wide_pair, offset, SLAB, 0)
        slab_doc = lax.dynamic_slice_in_dim(wide_doc, offset, SLAB, 0)
        position = first_byte + offset + jnp.arange(SLAB, dtype=jnp.int32)
        visible = (position[None, :] >= ends_here[:, None] - WIN) & (
            position[None, :] < ends_here[:, None]
        )
        visible = visible & (position[None, :] >= 0) & (position[None, :] < total_bytes)
        visible = visible & (slab_doc[None, :] == docs_here[:, None])
        key_slab = slab[:, :attn_width].reshape(SLAB, HEADS, HD)
        value_slab = slab[:, attn_width:].reshape(SLAB, HEADS, HD)
        query_group = lax.dynamic_slice_in_dim(local_queries, index * PG, PG, 0).reshape(
            PG, HEADS, HD
        )
        return (offset, visible, key_slab, value_slab, query_group)

    def forward_group(index):
        offset, visible, key_slab, value_slab, query_group = setup(index)
        probs = block_probs(query_group, key_slab, visible).astype(jnp.bfloat16)
        attended = jnp.einsum("hpj,jhd->phd", probs, value_slab, preferred_element_type=jnp.float32)
        return attended.reshape(PG, attn_width).astype(jnp.bfloat16)

    attended_all = lax.map(forward_group, jnp.arange(groups, dtype=jnp.int32)).reshape(
        patch_dev, attn_width
    )
    full_weight = lax.all_gather(proj_weight, "seq", axis=0, tiled=True)
    latent = lax.dot_general(
        attended_all, full_weight, (((1,), (1,)), ((), ())), preferred_element_type=jnp.float32
    )
    upstream = cotangent[0].astype(jnp.float32) * norm_gain
    inverse = lax.rsqrt(jnp.mean(latent * latent, axis=1, keepdims=True) + epsilon)
    gain_terms = jnp.sum(cotangent[0].astype(jnp.float32) * latent * inverse, axis=0)
    mixed_dot = jnp.mean(upstream * latent, axis=1, keepdims=True)
    d_latent = (inverse * upstream - latent * inverse * inverse * inverse * mixed_dot).astype(
        jnp.bfloat16
    )
    d_attended = jnp.dot(d_latent, full_weight, preferred_element_type=jnp.float32)
    d_attended = d_attended.astype(jnp.bfloat16)
    grad_part = lax.psum_scatter(
        lax.dot_general(
            d_latent, attended_all, (((0,), (0,)), ((), ())), preferred_element_type=jnp.float32
        ).astype(jnp.bfloat16),
        "seq",
        scatter_dimension=0,
        tiled=True,
    )
    d_proj = lax.psum(grad_part, "dp").astype(jnp.float32)
    d_gain = lax.psum(gain_terms, ("dp", "seq"))

    def backward_group(grad_bytes, index):
        offset, visible, key_slab, value_slab, query_group = setup(index)
        probs = block_probs(query_group, key_slab, visible)
        d_out = lax.dynamic_slice_in_dim(d_attended, index * PG, PG, 0).reshape(PG, HEADS, HD)
        out_group = lax.dynamic_slice_in_dim(attended_all, index * PG, PG, 0).reshape(PG, HEADS, HD)
        row_dot = jnp.transpose(
            jnp.sum(d_out.astype(jnp.float32) * out_group.astype(jnp.float32), axis=2)
        )[:, :, None]
        d_probs = jnp.einsum("phd,jhd->hpj", d_out, value_slab, preferred_element_type=jnp.float32)
        d_scores = (probs * (d_probs - row_dot) * score_scale).astype(jnp.bfloat16)
        d_query = jnp.einsum("hpj,jhd->phd", d_scores, key_slab, preferred_element_type=jnp.float32)
        d_query = d_query.reshape(PG, attn_width).astype(jnp.bfloat16)
        d_key = jnp.einsum(
            "hpj,phd->jhd", d_scores, query_group, preferred_element_type=jnp.float32
        ).reshape(SLAB, attn_width)
        d_value = jnp.einsum(
            "hpj,phd->jhd", probs.astype(jnp.bfloat16), d_out, preferred_element_type=jnp.float32
        ).reshape(SLAB, attn_width)
        current = lax.dynamic_slice_in_dim(grad_bytes, offset, SLAB, 0)
        grad_bytes = lax.dynamic_update_slice_in_dim(
            grad_bytes, current + jnp.concatenate([d_key, d_value], axis=1), offset, 0
        )
        return (grad_bytes, d_query)

    start_grad = jnp.zeros((ext_rows, 2 * attn_width), jnp.float32)
    grad_bytes, d_query_groups = lax.scan(
        backward_group, start_grad, jnp.arange(groups, dtype=jnp.int32)
    )
    lower_rim = grad_bytes[:rim_rows]
    upper_rim = grad_bytes[ext_rows - rim_rows :]
    from_above = shifted(lower_rim.astype(jnp.bfloat16), "seq", -1).astype(lower_rim.dtype)
    from_below = shifted(upper_rim.astype(jnp.bfloat16), "seq", 1).astype(upper_rim.dtype)
    own_rows = grad_bytes[rim_rows : rim_rows + byte_dev]
    own_rows = own_rows.at[byte_dev - rim_rows :].add(from_above)
    own_rows = own_rows.at[:rim_rows].add(from_below)
    d_queries = d_query_groups.reshape(1, patch_dev, attn_width)
    d_keys = own_rows[:, :attn_width].astype(jnp.bfloat16)[None]
    d_values = own_rows[:, attn_width:].astype(jnp.bfloat16)[None]
    return (d_queries, d_keys, d_values, d_proj, d_gain)


def solution(mesh):
    in_specs = (
        P("dp", "seq", None),
        P("dp", "seq", None),
        P("dp", "seq"),
        P("dp", "seq", None),
        P("dp", "seq"),
        P("dp", "seq", None),
        P("seq", None),
        P(),
    )
    out_specs = (
        P("dp", "seq", None),
        P("dp", "seq", None),
        P("dp", "seq", None),
        P("seq", None),
        P(),
    )
    return jax.shard_map(
        on_device, mesh=mesh, in_specs=in_specs, out_specs=out_specs, check_vma=False
    )
```

profile of v0, /device:TPU:0, one launch (start us, length us, event | category | flops | bytes accessed | tf_op | source)
XLA Modules:
  0.0 620.4 jit_solution(3840407877987545097)
XLA Ops:
  8.0 3.9 pad_maximum_fusion.2
  14.6 4.7 collective-permute-start
  20.7 2.9 collective-permute-done.1
  23.6 3.1 gather_fusion
  26.8 18.9 %pad_maximum_fusion = bf16[2816,2048]{1,0:T(8,128)(2,1)} fusion(bf16[384,2048]{1,0:T(8,128)(2,1)S(1)} %collective-permute-done.3, bf16[2048,1024]{1,0:T(8,128)(2,1)} %bitcast.187, bf16[2048,1024]{1,0:T(8,128)(2,1)} %bitcast.189, bf16[384,2048]{1,0:T(8,128)(2,1)S(1)} %collective-permute-done.2), kind=kLoop, calls=%fused_computation.73 | loop fusion | flops 46137344 | bytes 23068672 | tf_op jit(solution)/shard_map/concatenate | solution.py:29
  46.8 63.9 %while.30 = (s32[]{:T(128)}, bf16[8,64,1024]{2,1,0:T(8,128)(2,1)}, s32[8]{0:T(128)S(1)}, s32[512]{0:T(512)S(1)}, s32[]{:T(128)}, /*index=5*/bf16[2816,2048]{1,0:...) while((s32[]{:T(128)}, bf16[8,64,1024]{2,1,0:T(8,128)(2,1)}, ...), condition=%wide.region_3.4_spmd, body=%wide.region_0.3_spmd.sunk | while | flops 153386944 | bytes 11759427 | solution.py:99
  64.4 2.6 dynamic-slice_bitcast_fusion.15
  72.4 2.6 dynamic-slice_bitcast_fusion.15
  110.7 7.6 %multiply_reduce_fusion.1 = (f32[512]{0:T(512)S(1)}, f32[512,4096]{1,0:T(8,128)S(1)}) fusion(bf16[512,1024]{1,0:T(8,128)(2,1)} %bitcast.192, bf16[4096,1024]{1,0:T(8,128)(2,1)} %all-gather.2.cloned.1.call-done), kind=kOutput, calls=%fused_computation.83 | convolution fusion | flops 4299161088 | bytes 17827840 | tf_op jit(solution)/shard_map/dot_general | solution.py:103
  118.3 4.7 fusion.58
  123.0 3.3 fusion.55
  128.3 6.9 %convolution_convert_fusion = bf16[4096,1024]{1,0:T(8,128)(2,1)} fusion(bf16[512,4096]{1,0:T(8,128)(2,1)S(1)} %fusion.55, bf16[512,1024]{1,0:T(8,128)(2,1)S(1)} %bitcast.193), kind=kOutput, calls=%fused_computation.84 | convolution fusion | flops 4299161600 | bytes 13631488 | tf_op jit(solution)/shard_map/dot_general | solution.py:116
  135.3 9.1 %convolution_convert_fusion.1 = bf16[512,1024]{1,0:T(8,128)(2,1)S(1)} fusion(bf16[512,4096]{1,0:T(8,128)(2,1)} %copy-done.2, bf16[4096,1024]{1,0:T(8,128)(2,1)} %all-gather.2.cloned.1.call-done), kind=kOutput, calls=%fused_computation.92 | convolution fusion | flops 4295491584 | bytes 13631488 | tf_op jit(solution)/shard_map/dot_general | solution.py:113
  145.6 10.6 %broadcast_in_dim.82 = f32[2816,2048]{1,0:T(8,128)} broadcast(f32[]{:T(128)} %constant.244.clone.1), dimensions={} | broadcast | bytes 23068676 | tf_op jit(solution)/shard_map/broadcast_in_dim | solution.py:150
  156.2 281.2 %while.31 = (s32[]{:T(128)}, f32[2816,2048]{1,0:T(8,128)}, bf16[8,64,1024]{2,1,0:T(8,128)(2,1)}, s32[8]{0:T(128)S(1)}, s32[512]{0:T(512)S(1)}, /*index=5*/s32[]{...) while((s32[]{:T(128)}, f32[2816,2048]{1,0:T(8,128)}, ...), condition=%wide.region_10.11_spmd, body=%wide.region_6.10_spmd.sunk | while | flops 383974848 | bytes 65853712 | solution.py:151
  165.8 2.8 convolution_bitcast_fusion.4
  172.3 6.0 maximum_add_fusion.2
  178.3 13.7 %dynamic_update_slice.29 = f32[2816,2048]{1,0:T(8,128)} dynamic-update-slice(f32[2816,2048]{1,0:T(8,128)} %get-tuple-element.653, f32[576,2048]{1,0:T(8,128)} %maximum_add_fusion.2, s32[]{:T(128)S(6)} %min.18, s32[]{:T(128)} %constant.243.clone.1..sunk.1) | dynamic-update-slice | bytes 9437188 | tf_op jit(solution)/shard_map/while/body/eval_jaxpr/dynamic_update_slice | solution.py:145
  201.7 2.8 convolution_bitcast_fusion.4
  208.0 5.7 maximum_add_fusion.2
  213.8 13.5 %dynamic_update_slice.29 = f32[2816,2048]{1,0:T(8,128)} dynamic-update-slice(f32[2816,2048]{1,0:T(8,128)} %get-tuple-element.653, f32[576,2048]{1,0:T(8,128)} %maximum_add_fusion.2, s32[]{:T(128)S(6)} %min.18, s32[]{:T(128)} %constant.243.clone.1..sunk.1) | dynamic-update-slice | bytes 9437188 | tf_op jit(solution)/shard_map/while/body/eval_jaxpr/dynamic_update_slice | solution.py:145
  236.9 2.8 convolution_bitcast_fusion.4
  243.3 5.7 maximum_add_fusion.2
  249.0 13.4 %dynamic_update_slice.29 = f32[2816,2048]{1,0:T(8,128)} dynamic-update-slice(f32[2816,2048]{1,0:T(8,128)} %get-tuple-element.653, f32[576,2048]{1,0:T(8,128)} %maximum_add_fusion.2, s32[]{:T(128)S(6)} %min.18, s32[]{:T(128)} %constant.243.clone.1..sunk.1) | dynamic-update-slice | bytes 9437188 | tf_op jit(solution)/shard_map/while/body/eval_jaxpr/dynamic_update_slice | solution.py:145
  272.1 2.8 convolution_bitcast_fusion.4
  278.4 5.7 maximum_add_fusion.2
  284.2 13.4 %dynamic_update_slice.29 = f32[2816,2048]{1,0:T(8,128)} dynamic-update-slice(f32[2816,2048]{1,0:T(8,128)} %get-tuple-element.653, f32[576,2048]{1,0:T(8,128)} %maximum_add_fusion.2, s32[]{:T(128)S(6)} %min.18, s32[]{:T(128)} %constant.243.clone.1..sunk.1) | dynamic-update-slice | bytes 9437188 | tf_op jit(solution)/shard_map/while/body/eval_jaxpr/dynamic_update_slice | solution.py:145
  307.2 2.8 convolution_bitcast_fusion.4
  313.6 5.7 maximum_add_fusion.2
  319.3 13.4 %dynamic_update_slice.29 = f32[2816,2048]{1,0:T(8,128)} dynamic-update-slice(f32[2816,2048]{1,0:T(8,128)} %get-tuple-element.653, f32[576,2048]{1,0:T(8,128)} %maximum_add_fusion.2, s32[]{:T(128)S(6)} %min.18, s32[]{:T(128)} %constant.243.clone.1..sunk.1) | dynamic-update-slice | bytes 9437188 | tf_op jit(solution)/shard_map/while/body/eval_jaxpr/dynamic_update_slice | solution.py:145
  342.3 2.8 convolution_bitcast_fusion.4
  348.7 5.7 maximum_add_fusion.2
  354.4 13.3 %dynamic_update_slice.29 = f32[2816,2048]{1,0:T(8,128)} dynamic-update-slice(f32[2816,2048]{1,0:T(8,128)} %get-tuple-element.653, f32[576,2048]{1,0:T(8,128)} %maximum_add_fusion.2, s32[]{:T(128)S(6)} %min.18, s32[]{:T(128)} %constant.243.clone.1..sunk.1) | dynamic-update-slice | bytes 9437188 | tf_op jit(solution)/shard_map/while/body/eval_jaxpr/dynamic_update_slice | solution.py:145
  377.5 2.8 convolution_bitcast_fusion.4
  383.8 5.7 maximum_add_fusion.2
  389.6 13.3 %dynamic_update_slice.29 = f32[2816,2048]{1,0:T(8,128)} dynamic-update-slice(f32[2816,2048]{1,0:T(8,128)} %get-tuple-element.653, f32[576,2048]{1,0:T(8,128)} %maximum_add_fusion.2, s32[]{:T(128)S(6)} %min.18, s32[]{:T(128)} %constant.243.clone.1..sunk.1) | dynamic-update-slice | bytes 9437188 | tf_op jit(solution)/shard_map/while/body/eval_jaxpr/dynamic_update_slice | solution.py:145
  412.6 2.8 convolution_bitcast_fusion.4
  418.9 5.7 maximum_add_fusion.2
  424.7 12.7 %dynamic_update_slice.29 = f32[2816,2048]{1,0:T(8,128)} dynamic-update-slice(f32[2816,2048]{1,0:T(8,128)} %get-tuple-element.653, f32[576,2048]{1,0:T(8,128)} %maximum_add_fusion.2, s32[]{:T(128)S(6)} %min.18, s32[]{:T(128)} %constant.243.clone.1..sunk.1) | dynamic-update-slice | bytes 9437188 | tf_op jit(solution)/shard_map/while/body/eval_jaxpr/dynamic_update_slice | solution.py:145
  437.4 9.5 %convert.10 = bf16[2816,2048]{1,0:T(8,128)(2,1)S(1)} convert(f32[2816,2048]{1,0:T(8,128)} %get-tuple-element.348) | non-fusion elementwise | flops 5767168 | bytes 34603008 | tf_op jit(solution)/shard_map/convert.5
  448.9 24.1 %collective-permute-start.5 = (bf16[384,2048]{1,0:T(8,128)(2,1)S(1)}, bf16[384,2048]{1,0:T(8,128)(2,1)}, u32[]{:S(2)}, u32[]{:S(2)}) collective-permute-start(bf16[384,2048]{1,0:T(8,128)(2,1)S(1)} %get-tuple-element.413), channel_id=1, source_target_pairs={{0,1},{1,2},{2,3},{3,4},{4,5},{5,6},{6,7},{7,8},{8,9},{9,10},{10,1... | collective-permute-start | bytes 4718600 | tf_op jit(solution)/shard_map/ppermute | solution.py:36
  473.0 6.0 slice.124
  479.0 75.7 %psum.15 = f32[4096]{0:T(1024)} all-reduce(f32[4096]{0:T(1024)S(1)} %copy-done.6), channel_id=1, replica_groups=mesh['dp'=4,'seq'=32] {'dp','seq'}, use_global_device_ids=true, to_apply=%region_14.15 | all-reduce | flops 4096 | bytes 32768 | tf_op jit(solution)/shard_map/psum | solution.py:124
  554.8 4.6 add_dynamic-update-slice_fusion
  559.4 4.7 fusion.59
  564.1 9.1 %convert.11 = bf16[2048,2048]{1,0:T(8,128)(2,1)} convert(f32[2048,2048]{1,0:T(8,128)} %fusion.59) | non-fusion elementwise | flops 4194304 | bytes 25165824 | tf_op jit(solution)/shard_map/convert.3
  573.2 6.0 slice_bitcast_fusion
  579.3 32.8 %all-reduce.2.cloned.1.call-done = bf16[128,1024]{1,0:T(8,128)(2,1)} async-done(((bf16[128,1024]{1,0:T(8,128)(2,1)}), bf16[128,1024]{1,0:T(8,128)(2,1)}) %all-reduce.2.cloned.1.call-update) | async-done | bytes 262160 | tf_op jit(solution)/shard_map/psum | solution.py:123
  (446 shorter events, 164.0 us)
Async XLA Ops:
  7.2 103.5 %all-gather.2.cloned.1.call-start = ((), (), s32[]{:S(2)}) async-start(), calls=%async_computation.1 | async-start | bytes 8650752 | tf_op jit(solution)/shard_map/all_gather | solution.py:102
  7.9 565.3 %reduce-scatter.2.cloned.1.call-start = ((), (), s32[]{:S(2)}) async-start(), calls=%async_computation.2 | async-start | bytes 8650752 | tf_op jit(solution)/shard_map/reduce_scatter | solution.py:115
  7.9 6.6 %copy-start.11 = (s32[1,2048]{1,0:T(1,128)S(1)}, s32[1,2048]{1,0:T(1,128)}, u32[]{:S(2)}) copy-start(s32[1,2048]{1,0:T(1,128)} %param.18) | copy-start | bytes 24580
  8.0 12.7 %copy-start.8 = (s32[1,512]{1,0:T(1,128)S(1)}, s32[1,512]{1,0:T(1,128)}, u32[]{:S(2)}) copy-start(s32[1,512]{1,0:T(1,128)} %param.20) | copy-start | bytes 6148
  11.8 14.9 %collective-permute-start.2 = (bf16[384,2048]{1,0:T(8,128)(2,1)}, bf16[384,2048]{1,0:T(8,128)(2,1)S(1)}, u32[]{:S(2)}, u32[]{:S(2)}) collective-permute-start(bf16[384,2048]{1,0:T(8,128)(2,1)} %get-tuple-element.417), channel_id=1, source_target_pairs={{0,1},{1,2},{2,3},{3,4},{4,5},{5,6},{6,7},{7,8},{8,9},{9,10},{10,1... | collective-permute-start | bytes 4718600 | tf_op jit(solution)/shard_map/ppermute | solution.py:25
  13.2 13.5 %collective-permute-start.3 = (bf16[384,2048]{1,0:T(8,128)(2,1)}, bf16[384,2048]{1,0:T(8,128)(2,1)S(1)}, u32[]{:S(2)}, u32[]{:S(2)}) collective-permute-start(bf16[384,2048]{1,0:T(8,128)(2,1)} %get-tuple-element.418), channel_id=1, source_target_pairs={{1,0},{2,1},{3,2},{4,3},{5,4},{6,5},{7,6},{8,7},{9,8},{10,9},{11,1... | collective-permute-start | bytes 4718600 | tf_op jit(solution)/shard_map/ppermute | solution.py:28
  14.6 6.1 collective-permute-start
  19.3 4.3 collective-permute-start.1
  110.7 7.6 %copy-start.12 = (s32[512]{0:T(512)}, s32[512]{0:T(512)S(1)}, u32[]{:S(2)}) copy-start(s32[512]{0:T(512)S(1)} %get-tuple-element.712) | copy-start | bytes 6148
  110.7 7.6 %copy-start.1 = (bf16[1,512,4096]{2,1,0:T(8,128)(2,1)S(1)}, bf16[1,512,4096]{2,1,0:T(8,128)(2,1)}, u32[]{:S(2)}) copy-start(bf16[1,512,4096]{2,1,0:T(8,128)(2,1)} %param.21) | copy-start | bytes 12582916
  110.7 7.6 %copy-start.7 = (f32[4096]{0:T(1024)S(1)}, f32[4096]{0:T(1024)}, u32[]{:S(2)}) copy-start(f32[4096]{0:T(1024)} %param.23) | copy-start | bytes 49156
  135.3 476.8 %all-reduce.2.cloned.1.call-start = ((), (), s32[]{:S(2)}) async-start(), calls=%async_computation.3 | async-start | bytes 524288 | tf_op jit(solution)/shard_map/psum | solution.py:123
  178.3 13.7 %copy-start.5 = (bf16[512,1024]{1,0:T(8,128)(2,1)S(1)}, bf16[512,1024]{1,0:T(8,128)(2,1)}, u32[]{:S(2)}) copy-start(bf16[512,1024]{1,0:T(8,128)(2,1)} %copy-done.4) | copy-start | bytes 3145732 | tf_op jit(solution)/shard_map/while
  178.3 13.7 %copy-start.10 = (s32[512]{0:T(512)S(1)}, s32[512]{0:T(512)}, u32[]{:S(2)}) copy-start(s32[512]{0:T(512)} %copy-done.9) | copy-start | bytes 6148 | tf_op jit(solution)/shard_map/while
  178.3 13.7 %copy-start.14 = (s32[8]{0:T(128)S(1)}, s32[8]{0:T(128)}, u32[]{:S(2)}) copy-start(s32[8]{0:T(128)} %copy-done.13) | copy-start | bytes 100 | tf_op jit(solution)/shard_map/while
  192.0 6.4 %copy-start.4 = (bf16[512,1024]{1,0:T(8,128)(2,1)}, bf16[512,1024]{1,0:T(8,128)(2,1)S(1)}, u32[]{:S(2)}) copy-start(bf16[512,1024]{1,0:T(8,128)(2,1)S(1)} %get-tuple-element.681) | copy-start | bytes 3145732 | tf_op jit(solution)/shard_map/while
  192.0 6.4 %copy-start.9 = (s32[512]{0:T(512)}, s32[512]{0:T(512)S(1)}, u32[]{:S(2)}) copy-start(s32[512]{0:T(512)S(1)} %get-tuple-element.675) | copy-start | bytes 6148 | tf_op jit(solution)/shard_map/while
  213.8 13.5 %copy-start.5 = (bf16[512,1024]{1,0:T(8,128)(2,1)S(1)}, bf16[512,1024]{1,0:T(8,128)(2,1)}, u32[]{:S(2)}) copy-start(bf16[512,1024]{1,0:T(8,128)(2,1)} %copy-done.4) | copy-start | bytes 3145732 | tf_op jit(solution)/shard_map/while
  213.8 13.5 %copy-start.10 = (s32[512]{0:T(512)S(1)}, s32[512]{0:T(512)}, u32[]{:S(2)}) copy-start(s32[512]{0:T(512)} %copy-done.9) | copy-start | bytes 6148 | tf_op jit(solution)/shard_map/while
  213.8 13.5 %copy-start.14 = (s32[8]{0:T(128)S(1)}, s32[8]{0:T(128)}, u32[]{:S(2)}) copy-start(s32[8]{0:T(128)} %copy-done.13) | copy-start | bytes 100 | tf_op jit(solution)/shard_map/while
  227.3 6.3 %copy-start.4 = (bf16[512,1024]{1,0:T(8,128)(2,1)}, bf16[512,1024]{1,0:T(8,128)(2,1)S(1)}, u32[]{:S(2)}) copy-start(bf16[512,1024]{1,0:T(8,128)(2,1)S(1)} %get-tuple-element.681) | copy-start | bytes 3145732 | tf_op jit(solution)/shard_map/while
  227.3 6.3 %copy-start.9 = (s32[512]{0:T(512)}, s32[512]{0:T(512)S(1)}, u32[]{:S(2)}) copy-start(s32[512]{0:T(512)S(1)} %get-tuple-element.675) | copy-start | bytes 6148 | tf_op jit(solution)/shard_map/while
  249.0 13.4 %copy-start.5 = (bf16[512,1024]{1,0:T(8,128)(2,1)S(1)}, bf16[512,1024]{1,0:T(8,128)(2,1)}, u32[]{:S(2)}) copy-start(bf16[512,1024]{1,0:T(8,128)(2,1)} %copy-done.4) | copy-start | bytes 3145732 | tf_op jit(solution)/shard_map/while
  249.0 13.4 %copy-start.10 = (s32[512]{0:T(512)S(1)}, s32[512]{0:T(512)}, u32[]{:S(2)}) copy-start(s32[512]{0:T(512)} %copy-done.9) | copy-start | bytes 6148 | tf_op jit(solution)/shard_map/while
  249.0 13.4 %copy-start.14 = (s32[8]{0:T(128)S(1)}, s32[8]{0:T(128)}, u32[]{:S(2)}) copy-start(s32[8]{0:T(128)} %copy-done.13) | copy-start | bytes 100 | tf_op jit(solution)/shard_map/while
  262.4 6.3 %copy-start.4 = (bf16[512,1024]{1,0:T(8,128)(2,1)}, bf16[512,1024]{1,0:T(8,128)(2,1)S(1)}, u32[]{:S(2)}) copy-start(bf16[512,1024]{1,0:T(8,128)(2,1)S(1)} %get-tuple-element.681) | copy-start | bytes 3145732 | tf_op jit(solution)/shard_map/while
  284.2 13.4 %copy-start.5 = (bf16[512,1024]{1,0:T(8,128)(2,1)S(1)}, bf16[512,1024]{1,0:T(8,128)(2,1)}, u32[]{:S(2)}) copy-start(bf16[512,1024]{1,0:T(8,128)(2,1)} %copy-done.4) | copy-start | bytes 3145732 | tf_op jit(solution)/shard_map/while
  284.2 13.4 %copy-start.10 = (s32[512]{0:T(512)S(1)}, s32[512]{0:T(512)}, u32[]{:S(2)}) copy-start(s32[512]{0:T(512)} %copy-done.9) | copy-start | bytes 6148 | tf_op jit(solution)/shard_map/while
  284.2 13.4 %copy-start.14 = (s32[8]{0:T(128)S(1)}, s32[8]{0:T(128)}, u32[]{:S(2)}) copy-start(s32[8]{0:T(128)} %copy-done.13) | copy-start | bytes 100 | tf_op jit(solution)/shard_map/while
  297.6 6.3 %copy-start.4 = (bf16[512,1024]{1,0:T(8,128)(2,1)}, bf16[512,1024]{1,0:T(8,128)(2,1)S(1)}, u32[]{:S(2)}) copy-start(bf16[512,1024]{1,0:T(8,128)(2,1)S(1)} %get-tuple-element.681) | copy-start | bytes 3145732 | tf_op jit(solution)/shard_map/while
  319.3 13.4 %copy-start.5 = (bf16[512,1024]{1,0:T(8,128)(2,1)S(1)}, bf16[512,1024]{1,0:T(8,128)(2,1)}, u32[]{:S(2)}) copy-start(bf16[512,1024]{1,0:T(8,128)(2,1)} %copy-done.4) | copy-start | bytes 3145732 | tf_op jit(solution)/shard_map/while
  319.3 13.4 %copy-start.10 = (s32[512]{0:T(512)S(1)}, s32[512]{0:T(512)}, u32[]{:S(2)}) copy-start(s32[512]{0:T(512)} %copy-done.9) | copy-start | bytes 6148 | tf_op jit(solution)/shard_map/while
  319.3 13.4 %copy-start.14 = (s32[8]{0:T(128)S(1)}, s32[8]{0:T(128)}, u32[]{:S(2)}) copy-start(s32[8]{0:T(128)} %copy-done.13) | copy-start | bytes 100 | tf_op jit(solution)/shard_map/while
  332.7 6.3 %copy-start.4 = (bf16[512,1024]{1,0:T(8,128)(2,1)}, bf16[512,1024]{1,0:T(8,128)(2,1)S(1)}, u32[]{:S(2)}) copy-start(bf16[512,1024]{1,0:T(8,128)(2,1)S(1)} %get-tuple-element.681) | copy-start | bytes 3145732 | tf_op jit(solution)/shard_map/while
  354.4 13.4 %copy-start.5 = (bf16[512,1024]{1,0:T(8,128)(2,1)S(1)}, bf16[512,1024]{1,0:T(8,128)(2,1)}, u32[]{:S(2)}) copy-start(bf16[512,1024]{1,0:T(8,128)(2,1)} %copy-done.4) | copy-start | bytes 3145732 | tf_op jit(solution)/shard_map/while
  354.4 13.4 %copy-start.10 = (s32[512]{0:T(512)S(1)}, s32[512]{0:T(512)}, u32[]{:S(2)}) copy-start(s32[512]{0:T(512)} %copy-done.9) | copy-start | bytes 6148 | tf_op jit(solution)/shard_map/while
  354.4 13.4 %copy-start.14 = (s32[8]{0:T(128)S(1)}, s32[8]{0:T(128)}, u32[]{:S(2)}) copy-start(s32[8]{0:T(128)} %copy-done.13) | copy-start | bytes 100 | tf_op jit(solution)/shard_map/while
  367.8 6.3 %copy-start.4 = (bf16[512,1024]{1,0:T(8,128)(2,1)}, bf16[512,1024]{1,0:T(8,128)(2,1)S(1)}, u32[]{:S(2)}) copy-start(bf16[512,1024]{1,0:T(8,128)(2,1)S(1)} %get-tuple-element.681) | copy-start | bytes 3145732 | tf_op jit(solution)/shard_map/while
  389.6 13.4 %copy-start.5 = (bf16[512,1024]{1,0:T(8,128)(2,1)S(1)}, bf16[512,1024]{1,0:T(8,128)(2,1)}, u32[]{:S(2)}) copy-start(bf16[512,1024]{1,0:T(8,128)(2,1)} %copy-done.4) | copy-start | bytes 3145732 | tf_op jit(solution)/shard_map/while
  389.6 13.4 %copy-start.10 = (s32[512]{0:T(512)S(1)}, s32[512]{0:T(512)}, u32[]{:S(2)}) copy-start(s32[512]{0:T(512)} %copy-done.9) | copy-start | bytes 6148 | tf_op jit(solution)/shard_map/while
  389.6 13.4 %copy-start.14 = (s32[8]{0:T(128)S(1)}, s32[8]{0:T(128)}, u32[]{:S(2)}) copy-start(s32[8]{0:T(128)} %copy-done.13) | copy-start | bytes 100 | tf_op jit(solution)/shard_map/while
  424.6 12.7 %copy-start.5 = (bf16[512,1024]{1,0:T(8,128)(2,1)S(1)}, bf16[512,1024]{1,0:T(8,128)(2,1)}, u32[]{:S(2)}) copy-start(bf16[512,1024]{1,0:T(8,128)(2,1)} %copy-done.4) | copy-start | bytes 3145732 | tf_op jit(solution)/shard_map/while
  424.6 12.7 %copy-start.10 = (s32[512]{0:T(512)S(1)}, s32[512]{0:T(512)}, u32[]{:S(2)}) copy-start(s32[512]{0:T(512)} %copy-done.9) | copy-start | bytes 6148 | tf_op jit(solution)/shard_map/while
  424.7 12.7 %copy-start.14 = (s32[8]{0:T(128)S(1)}, s32[8]{0:T(128)}, u32[]{:S(2)}) copy-start(s32[8]{0:T(128)} %copy-done.13) | copy-start | bytes 100 | tf_op jit(solution)/shard_map/while
  437.4 35.6 %copy-start = (f32[2816,2048]{1,0:T(8,128)S(1)}, f32[2816,2048]{1,0:T(8,128)}, u32[]{:S(2)}) copy-start(f32[2816,2048]{1,0:T(8,128)} %get-tuple-element.348) | copy-start | bytes 69206016
  447.3 107.5 %collective-permute-start.4 = (bf16[384,2048]{1,0:T(8,128)(2,1)S(1)}, bf16[384,2048]{1,0:T(8,128)(2,1)}, u32[]{:S(2)}, u32[]{:S(2)}) collective-permute-start(bf16[384,2048]{1,0:T(8,128)(2,1)S(1)} %get-tuple-element.414), channel_id=1, source_target_pairs={{1,0},{2,1},{3,2},{4,3},{5,4},{6,5},{7,6},{8,7},{9,8},{10,9},{11,1... | collective-permute-start | bytes 4718600 | tf_op jit(solution)/shard_map/ppermute | solution.py:36
  448.9 30.1 %copy-start.6 = (f32[4096]{0:T(1024)S(1)}, f32[4096]{0:T(1024)}, u32[]{:S(2)}) copy-start(f32[4096]{0:T(1024)} %get-tuple-element.349) | copy-start | bytes 49156
  448.9 110.5 %collective-permute-start.5 = (bf16[384,2048]{1,0:T(8,128)(2,1)S(1)}, bf16[384,2048]{1,0:T(8,128)(2,1)}, u32[]{:S(2)}, u32[]{:S(2)}) collective-permute-start(bf16[384,2048]{1,0:T(8,128)(2,1)S(1)} %get-tuple-element.413), channel_id=1, source_target_pairs={{0,1},{1,2},{2,3},{3,4},{4,5},{5,6},{6,7},{7,8},{8,9},{9,10},{10,1... | collective-permute-start | bytes 4718600 | tf_op jit(solution)/shard_map/ppermute | solution.py:36
  (18 other events, 76.0 us)
Sparse Core Ops, SparseCore 0:
  10.3 66.1 all-gather.1
  135.4 114.4 reduce-scatter.1
  573.3 38.7 all-reduce.1
where the time goes:
time: 625 us; the launch traced here: 620 us
  local copies, waits for them, and re-layouts  229 us (37%)
  other arithmetic  134 us (21%)
  matrix products  83.5 us (13%)
  blocking collectives  75.7 us (12%)
  waiting for transfers between devices  36.5 us (6%)
  starting transfers between devices  34.5 us (6%)
  between operations  14 us (2%)
  loops' own time  13.3 us (2%)
    dynamic_update_slice x8, local copies, waits for them, and re-layouts, backward_group(): lax.dynamic_update_slice_in_dim(grad_bytes, current + jnp.concatenate([d_...  107 us
    psum x1, blocking collectives, on_device(): d_gain = lax.psum(gain_terms, ('dp', 'seq'))  75.7 us
    add x8, other arithmetic, backward_group(): current + jnp.concatenate([d_key, d_value], axis=1)  46.1 us
    while x136, local copies, waits for them, and re-layouts  42 us
    psum x1, waiting for transfers between devices, on_device(): d_proj = lax.psum(grad_part, 'dp').astype(jnp.float32)  32.8 us
    ppermute x2, starting transfers between devices, shifted(): return lax.ppermute(block, axis, route)  25.7 us
    dot_general x8, matrix products, backward_group(): jnp.einsum('hpj,phd->jhd', probs.astype(jnp.bfloat16), d_out, preferred_e...  22.7 us
    concatenate x2, other arithmetic, padded(): block = jnp.concatenate([low, block, high], axis=dim)  18.9 us
  transfers between devices with their start and end apart: 9, of which 2 were waited for; matrix products, arithmetic and copies ran while one was open for 68% of the time, Pallas kernels for 0%

commit v1 on v0

v1 whole, which is shorter than its diff:
```python
import math

import jax
import jax.numpy as jnp
from jax import lax
from jax.experimental import pallas as pl
from jax.experimental.pallas import tpu as pltpu
from jax.sharding import PartitionSpec as P

HEADS = 8
HD = 128
WIN = 128
LOW = 384
HIGH = 256
PG = 32
SLAB = 384
RING = 4
LANES = 128

masked_score = -1e30
epsilon = 1e-05
score_scale = 1.0 / math.sqrt(HD)
bf16, f32 = jnp.bfloat16, jnp.float32
MIB = 1024 * 1024
VMEM_GRANT = 60 * MIB


def dot(a, b):
    return jnp.dot(a, b, preferred_element_type=f32)


def dot_rows(a, b):
    return lax.dot_general(a, b, (((1,), (1,)), ((), ())), preferred_element_type=f32)


def dot_columns(a, b):
    return lax.dot_general(a, b, (((0,), (0,)), ((), ())), preferred_element_type=f32)


def of_head(head):
    return slice(head * HD, (head + 1) * HD)


def fetch_bytes(low_ref, high_ref, keys_ref, values_ref, key_ext, value_ext, sems):
    own = keys_ref.shape[0]
    copies = []
    for which, (own_ref, ext) in enumerate(((keys_ref, key_ext), (values_ref, value_ext))):
        parts = (
            (low_ref.at[pl.ds(which * LOW, LOW)], pl.ds(0, LOW)),
            (own_ref, pl.ds(LOW, own)),
            (high_ref.at[pl.ds(which * HIGH, HIGH)], pl.ds(LOW + own, HIGH)),
        )
        for part, (source, rows) in enumerate(parts):
            copies.append(
                pltpu.make_async_copy(source, ext.at[rows], sems.at[which * 3 + part])
            )
    return copies


def visible_bias(offset, span_ref, rows):
    position = offset + lax.broadcasted_iota(jnp.int32, (PG, SLAB), 1)
    visible = (position >= span_ref[rows, 0:1]) & (position < span_ref[rows, 1:2])
    return jnp.where(visible, 0.0, masked_score)


def forward_kernel(
    offset_ref, span_ref, low_ref, high_ref, keys_ref, values_ref, query_ref,
    attended_ref, level_ref, key_ext, value_ext, sems,
):
    step = pl.program_id(0)

    @pl.when(step == 0)
    def _():
        copies = fetch_bytes(low_ref, high_ref, keys_ref, values_ref, key_ext, value_ext, sems)
        for copy in copies:
            copy.start()
        for copy in copies:
            copy.wait()

    groups = query_ref.shape[0] // PG

    def one_group(group, carry):
        rows = pl.ds(pl.multiple_of(group * PG, PG), PG)
        offset = pl.multiple_of(offset_ref[step * groups + group], 16)
        slab = pl.ds(offset, SLAB)
        bias = visible_bias(offset, span_ref, rows)
        heads = [of_head(head) for head in range(HEADS)]
        scores = [dot_rows(query_ref[rows, h], key_ext[slab, h]) for h in heads]
        scores = [x * score_scale + bias for x in scores]
        top = [jnp.max(x, axis=1, keepdims=True) for x in scores]
        expo = [jnp.exp(x - y) for x, y in zip(scores, top)]
        total = [jnp.sum(x, axis=1, keepdims=True) for x in expo]
        probs = [(x * (1.0 / y)).astype(bf16) for x, y in zip(expo, total)]
        attended = [dot(x, value_ext[slab, h]) for x, h in zip(probs, heads)]
        for h, x, y, z in zip(heads, attended, top, total):
            attended_ref[rows, h] = x.astype(bf16)
            level_ref[rows, h] = jnp.broadcast_to(y + jnp.log(z), (PG, HD))
        return carry

    lax.fori_loop(0, groups, one_group, 0)


def backward_kernel(
    offset_ref, span_ref, low_ref, high_ref, keys_ref, values_ref, query_ref,
    attended_ref, level_ref, d_attended_ref, after_ref,
    d_query_ref, d_key_ref, d_value_ref, d_low_ref, d_high_ref,
    key_ext, value_ext, sems, d_key, d_value,
):
    step = pl.program_id(0)
    own = keys_ref.shape[0]

    @pl.when(step == 0)
    def _():
        copies = fetch_bytes(low_ref, high_ref, keys_ref, values_ref, key_ext, value_ext, sems)
        for copy in copies:
            copy.start()
        d_key[...] = jnp.zeros_like(d_key)
        d_value[...] = jnp.zeros_like(d_value)
        for copy in copies:
            copy.wait()

    groups = query_ref.shape[0] // PG

    def one_group(group, carry):
        rows = pl.ds(pl.multiple_of(group * PG, PG), PG)
        offset = pl.multiple_of(offset_ref[step * groups + group], 16)
        slab = pl.ds(offset, SLAB)
        bias = visible_bias(offset, span_ref, rows)
        heads = [of_head(head) for head in range(HEADS)]
        scores = [dot_rows(query_ref[rows, h], key_ext[slab, h]) for h in heads]
        d_probs = [dot_rows(d_attended_ref[rows, h], value_ext[slab, h]) for h in heads]
        row_dot = [
            jnp.sum(
                d_attended_ref[rows, h].astype(f32) * attended_ref[rows, h].astype(f32),
                axis=1, keepdims=True,
            )
            for h in heads
        ]
        level = [jnp.concatenate([level_ref[rows, h]] * (SLAB // HD), axis=1) for h in heads]
        probs = [jnp.exp(x * score_scale + bias - y) for x, y in zip(scores, level)]
        d_scores = [
            (x * (y - z) * score_scale).astype(bf16) for x, y, z in zip(probs, d_probs, row_dot)
        ]
        probs = [x.astype(bf16) for x in probs]
        d_query = [dot(x, key_ext[slab, h]) for x, h in zip(d_scores, heads)]
        key_part = [dot_columns(x, query_ref[rows, h]) for x, h in zip(d_scores, heads)]
        value_part = [dot_columns(x, d_attended_ref[rows, h]) for x, h in zip(probs, heads)]
        for h, x, y, z in zip(heads, d_query, key_part, value_part):
            d_query_ref[rows, h] = x.astype(bf16)
            d_key[slab, h] += y
            d_value[slab, h] += z
        return carry

    lax.fori_loop(0, groups, one_group, 0)

    @pl.when(step == pl.num_programs(0) - 1)
    def _():
        for which, (total, own_ref) in enumerate(((d_key, d_key_ref), (d_value, d_value_ref))):
            d_low_ref[which * LOW : (which + 1) * LOW, :] = total[:LOW, :].astype(bf16)
            own_ref[...] = total[LOW : LOW + own, :].astype(bf16)
            d_high_ref[which * HIGH : (which + 1) * HIGH, :] = total[LOW + own :, :].astype(bf16)


def forward_call(inputs):
    own, width = inputs[4].shape
    patches = inputs[6].shape[0]
    steps = 4
    ext_rows = LOW + own + HIGH

    def per_step(columns):
        return pl.BlockSpec((patches // steps, columns), lambda step, offset: (step, 0))

    return pl.pallas_call(
        forward_kernel,
        out_shape=[
            jax.ShapeDtypeStruct((patches, width), bf16),
            jax.ShapeDtypeStruct((patches, width), f32),
        ],
        grid_spec=pltpu.PrefetchScalarGridSpec(
            num_scalar_prefetch=1,
            grid=(steps,),
            in_specs=[per_step(2)] + [pl.BlockSpec(memory_space=pl.ANY)] * 4 + [per_step(width)],
            out_specs=[per_step(width)] * 2,
            scratch_shapes=[pltpu.VMEM((ext_rows, width), bf16)] * 2
            + [pltpu.SemaphoreType.DMA((6,))],
        ),
        compiler_params=pltpu.CompilerParams(vmem_limit_bytes=VMEM_GRANT),
        cost_estimate=pl.CostEstimate(
            flops=4 * HEADS * patches * SLAB * HD,
            bytes_accessed=20 * MIB,
            transcendentals=HEADS * patches * SLAB,
        ),
        name="attention_forward",
    )(*inputs)


def backward_call(inputs, after):
    own, width = inputs[4].shape
    patches = inputs[6].shape[0]
    steps = 4
    ext_rows = LOW + own + HIGH
    step_block = pl.BlockSpec((patches // steps, width), lambda step, offset: (step, 0))
    anywhere = pl.BlockSpec(memory_space=pl.ANY)

    def kept(rows):
        return pl.BlockSpec(
            (rows, width), lambda step, offset: (0, 0), pipeline_mode=pl.Buffered(1)
        )

    rows = (own, own, 2 * LOW, 2 * HIGH)
    return pl.pallas_call(
        backward_kernel,
        out_shape=[jax.ShapeDtypeStruct((count, width), bf16) for count in (patches,) + rows],
        grid_spec=pltpu.PrefetchScalarGridSpec(
            num_scalar_prefetch=1,
            grid=(steps,),
            in_specs=[pl.BlockSpec((patches // steps, 2), lambda step, offset: (step, 0))]
            + [anywhere] * 4
            + [step_block] * 4
            + [anywhere],
            out_specs=[step_block] + [kept(count) for count in rows],
            scratch_shapes=[pltpu.VMEM((ext_rows, width), bf16)] * 2
            + [pltpu.SemaphoreType.DMA((6,))]
            + [pltpu.VMEM((ext_rows, width), f32)] * 2,
        ),
        compiler_params=pltpu.CompilerParams(vmem_limit_bytes=VMEM_GRANT),
        cost_estimate=pl.CostEstimate(
            flops=14 * HEADS * patches * SLAB * HD,
            bytes_accessed=40 * MIB,
            transcendentals=HEADS * patches * SLAB,
        ),
        name="attention_backward",
    )(*inputs, after)


def chip_block(place_ref, chunk):
    side, first, second = chunk // 16, chunk // 4 % 4, chunk % 4
    core = (place_ref[2] + side) % 2
    z = (place_ref[0] - jnp.where(core == 0, first, second) + RING) % RING
    x = (place_ref[1] - jnp.where(core == 0, second, first) + RING) % RING
    return (z * RING + x) * 2 + core


def fetch_weights(place_ref, weights_ref, weight, sems):
    copies = []
    for chunk in range(32):
        start = pl.multiple_of(chip_block(place_ref, chunk) * LANES, LANES)
        copies.append(
            pltpu.make_async_copy(
                weights_ref.at[pl.ds(start, LANES)],
                weight.at[pl.ds(chunk * LANES, LANES)],
                sems.at[chunk],
            )
        )
    return [copies[start : start + 4] for start in range(0, 32, 4)]


def latent_kernel(
    place_ref, attended_ref, norm_ref, cotangent_ref, weights_ref,
    mine_ref, other_ref, gain_ref, weight, cotangent, latent, square, mixed, sems,
):
    pieces = fetch_weights(place_ref, weights_ref, weight, sems)
    cotangent_copy = pltpu.make_async_copy(cotangent_ref, cotangent, sems.at[32])
    for slab, copies in enumerate(pieces):
        for copy in copies:
            copy.start()
        if slab == 0:
            cotangent_copy.start()
    square[...] = jnp.zeros_like(square)
    mixed[...] = jnp.zeros_like(mixed)

    def columns_of(chunk):
        return pl.ds(pl.multiple_of(chip_block(place_ref, chunk) * LANES, LANES), LANES)

    for slab in range(8):
        for copy in pieces[slab]:
            copy.wait()
        for half in range(2):
            start = slab * 512 + half * 256
            block = dot_rows(attended_ref[...], weight[start : start + 256, :])
            if slab == 0 and half == 0:
                cotangent_copy.wait()
            for side in range(2):
                chunk = slab * 4 + half * 2 + side
                columns = columns_of(chunk)
                here = block[:, side * LANES : (side + 1) * LANES]
                latent[chunk] = here
                square[...] += here * here
                mixed[...] += here * (cotangent[:, columns].astype(f32) * norm_ref[:, columns])

    count = cotangent.shape[1]
    inverse = lax.rsqrt(jnp.sum(square[...], axis=1, keepdims=True) / count + epsilon)
    back = inverse * inverse * inverse * (jnp.sum(mixed[...], axis=1, keepdims=True) / count)
    square[...] = jnp.broadcast_to(inverse, square.shape)
    mixed[...] = jnp.broadcast_to(back, mixed.shape)

    def finish(chunk, out_ref):
        columns = columns_of(chunk)
        here = latent[chunk]
        arriving = cotangent[:, columns].astype(f32)
        scaled = arriving * square[...]
        gain = jnp.sum(scaled * here, axis=0, keepdims=True)
        spot = pl.ds(pl.multiple_of(chip_block(place_ref, chunk) * 8, 8), 8)
        gain_ref[spot, :] = jnp.broadcast_to(gain, (8, LANES))
        d_latent = scaled * norm_ref[:, columns] - here * mixed[...]
        place = pl.ds(pl.multiple_of(chunk % 16 * LANES, LANES), LANES)
        out_ref[:, place] = d_latent.astype(bf16)

    lax.fori_loop(0, 16, lambda chunk, carry: (finish(chunk, mine_ref), carry)[1], 0)
    lax.fori_loop(16, 32, lambda chunk, carry: (finish(chunk, other_ref), carry)[1], 0)


def latent_call(place, attended, norm_gain, cotangent, weights):
    patches, count = cotangent.shape
    return pl.pallas_call(
        latent_kernel,
        out_shape=[
            jax.ShapeDtypeStruct((patches, count // 2), bf16),
            jax.ShapeDtypeStruct((patches, count // 2), bf16),
            jax.ShapeDtypeStruct((count // LANES * 8, LANES), f32),
        ],
        in_specs=[pl.BlockSpec(memory_space=pltpu.SMEM)]
        + [pl.BlockSpec(memory_space=pltpu.VMEM)] * 2
        + [pl.BlockSpec(memory_space=pl.ANY)] * 2,
        out_specs=[pl.BlockSpec(memory_space=pltpu.VMEM)] * 3,
        scratch_shapes=[
            pltpu.VMEM(weights.shape, bf16),
            pltpu.VMEM((patches, count), bf16),
            pltpu.VMEM((32, patches, LANES), f32),
            pltpu.VMEM((patches, LANES), f32),
            pltpu.VMEM((patches, LANES), f32),
            pltpu.SemaphoreType.DMA((33,)),
        ],
        compiler_params=pltpu.CompilerParams(vmem_limit_bytes=VMEM_GRANT),
        cost_estimate=pl.CostEstimate(
            flops=2 * patches * count * 1024, bytes_accessed=18 * MIB, transcendentals=patches
        ),
        name="latent",
    )(place, attended, norm_gain, cotangent, weights)


def d_attended_kernel(place_ref, mine_ref, other_ref, weights_ref, out_ref, weight, total, sems):
    pieces = fetch_weights(place_ref, weights_ref, weight, sems)
    for copies in pieces:
        for copy in copies:
            copy.start()
    for slab in range(8):
        source = mine_ref if slab < 4 else other_ref
        d_latent = source[:, slab % 4 * 512 : slab % 4 * 512 + 512]
        for copy in pieces[slab]:
            copy.wait()
        part = dot(d_latent, weight[slab * 512 : slab * 512 + 512, :])
        if slab == 0:
            total[...] = part
        elif slab < 7:
            total[...] += part
        else:
            out_ref[...] = (total[...] + part).astype(bf16)


def d_attended_call(place, mine, other, weights):
    patches, width = mine.shape[0], weights.shape[1]
    return pl.pallas_call(
        d_attended_kernel,
        out_shape=jax.ShapeDtypeStruct((patches, width), bf16),
        in_specs=[pl.BlockSpec(memory_space=pltpu.SMEM)]
        + [pl.BlockSpec(memory_space=pltpu.VMEM)] * 2
        + [pl.BlockSpec(memory_space=pl.ANY)],
        out_specs=pl.BlockSpec(memory_space=pltpu.VMEM),
        scratch_shapes=[
            pltpu.VMEM(weights.shape, bf16),
            pltpu.VMEM((patches, width), f32),
            pltpu.SemaphoreType.DMA((32,)),
        ],
        compiler_params=pltpu.CompilerParams(vmem_limit_bytes=VMEM_GRANT),
        cost_estimate=pl.CostEstimate(
            flops=4 * patches * mine.shape[1] * width, bytes_accessed=14 * MIB, transcendentals=0
        ),
        name="d_attended",
    )(place, mine, other, weights)


def d_proj_kernel(
    mine_ref, peer_ref, attended_ref, peer_attended_ref, gain_ref, after_ref, *refs
):
    outs, (turned, peer_turned) = refs[:4], refs[4:]
    turned[...] = attended_ref[...].T
    peer_turned[...] = peer_attended_ref[...].T
    width = turned.shape[0]
    for k in range(RING):
        distance = (RING - k) % RING
        columns = slice(distance * 512, distance * 512 + 512)
        part = dot(turned[...], mine_ref[:, columns])
        part += dot(peer_turned[...], peer_ref[:, columns])
        outs[k][:width, :] = part.astype(bf16)
        outs[k][width:, :] = gain_ref[...]


def d_proj_call(mine, peer, attended, peer_attended, gain, after):
    patches, width = attended.shape
    return pl.pallas_call(
        d_proj_kernel,
        out_shape=[jax.ShapeDtypeStruct((width + 16, 512), bf16)] * 4,
        in_specs=[pl.BlockSpec(memory_space=pltpu.VMEM)] * 5
        + [pl.BlockSpec(memory_space=pl.ANY)],
        out_specs=[pl.BlockSpec(memory_space=pltpu.VMEM)] * 4,
        scratch_shapes=[pltpu.VMEM((width, patches), bf16)] * 2,
        compiler_params=pltpu.CompilerParams(vmem_limit_bytes=VMEM_GRANT),
        cost_estimate=pl.CostEstimate(
            flops=4 * patches * mine.shape[1] * width, bytes_accessed=12 * MIB, transcendentals=0
        ),
        name="d_proj",
    )(mine, peer, attended, peer_attended, gain, after)


def rim_kernel(
    key_in, value_in, below_ref, above_ref, key_out, value_out, key_rim, value_rim, sems
):
    own = key_in.shape[0]
    places = ((pl.ds(0, HIGH), pl.ds(0, HIGH)), (pl.ds(own - LOW, LOW), pl.ds(HIGH, LOW)))

    def copies(outward):
        found = []
        for which, (source, out, rim) in enumerate(
            ((key_in, key_out, key_rim), (value_in, value_out, value_rim))
        ):
            for side, (far, near) in enumerate(places):
                sem = sems.at[4 * outward + 2 * which + side]
                if outward:
                    found.append(pltpu.make_async_copy(rim.at[near], out.at[far], sem))
                else:
                    found.append(pltpu.make_async_copy(source.at[far], rim.at[near], sem))
        return found

    inward, outward = copies(0), copies(1)
    for copy in inward:
        copy.start()
    for which, rim in enumerate((key_rim, value_rim)):
        inward[2 * which].wait()
        below = below_ref[which * HIGH : (which + 1) * HIGH, :].astype(f32)
        rim[:HIGH, :] = (rim[:HIGH, :].astype(f32) + below).astype(bf16)
        outward[2 * which].start()
        inward[2 * which + 1].wait()
        above = above_ref[which * LOW : (which + 1) * LOW, :].astype(f32)
        rim[HIGH:, :] = (rim[HIGH:, :].astype(f32) + above).astype(bf16)
        outward[2 * which + 1].start()
    for copy in outward:
        copy.wait()


def rim_call(d_key, d_value, from_below, from_above):
    width = from_below.shape[1]
    anywhere = pl.BlockSpec(memory_space=pl.ANY)
    vmem = pl.BlockSpec(memory_space=pltpu.VMEM)
    return pl.pallas_call(
        rim_kernel,
        out_shape=[jax.ShapeDtypeStruct(d_key.shape, bf16)] * 2,
        in_specs=[anywhere, anywhere, vmem, vmem],
        out_specs=[anywhere, anywhere],
        scratch_shapes=[pltpu.VMEM((HIGH + LOW, width), bf16)] * 2
        + [pltpu.SemaphoreType.DMA((8,))],
        input_output_aliases={0: 0, 1: 1},
        compiler_params=pltpu.CompilerParams(vmem_limit_bytes=VMEM_GRANT),
        name="rims",
    )(d_key, d_value, from_below, from_above)


def along(which, distance):
    pairs = []
    for z in range(RING):
        for x in range(RING):
            for core in range(2):
                on_z = (which == "first") == (core == 0)
                to_z = (z + distance) % RING if on_z else z
                to_x = x if on_z else (x + distance) % RING
                pairs.append(((z * RING + x) * 2 + core, (to_z * RING + to_x) * 2 + core))
    return pairs


def to_peer(value):
    return lax.ppermute(value, "seq", [(i, i ^ 1) for i in range(lax.axis_size("seq"))])


def ring(values, which):
    return [values[0]] + [
        lax.ppermute(values[k], "seq", along(which, k)) for k in range(1, RING)
    ]


def total_of(parts):
    parts = [part.astype(f32) for part in parts]
    return (parts[0] + parts[2]) + (parts[1] + parts[3])


def halves(value):
    upper = value.astype(bf16)
    lower = (value - upper.astype(f32)).astype(bf16)
    return jnp.concatenate([upper, lower])


def joined(value):
    rows = value.shape[0] // 2
    return value[:rows] + value[rows:]


def first_sum_kernel(*refs):
    parts, outs = refs[:4], refs[4:]
    width = parts[0].shape[0] - 16
    gain = joined(total_of([ref[width:, :] for ref in parts]))
    gain = halves(
        jnp.concatenate([gain[:, k * LANES : (k + 1) * LANES] for k in range(RING)])
    )
    for k in range(RING):
        start = (RING - k) % RING * LANES
        columns = slice(start, start + LANES)
        outs[k][:width, :] = total_of([ref[:width, columns] for ref in parts]).astype(bf16)
        outs[k][width:, :] = gain


def first_sum(parts):
    width = parts[0].shape[0] - 16
    vmem = pl.BlockSpec(memory_space=pltpu.VMEM)
    return pl.pallas_call(
        first_sum_kernel,
        out_shape=[jax.ShapeDtypeStruct((width + 64, LANES), bf16)] * RING,
        in_specs=[vmem] * 4,
        out_specs=[vmem] * 4,
        compiler_params=pltpu.CompilerParams(vmem_limit_bytes=VMEM_GRANT),
        name="first_sum",
    )(*parts)


def second_sum_kernel(place_ref, *refs):
    parts, outs, total = refs[:4], refs[4:8], refs[8]
    width = total.shape[0]
    quarter = width // RING
    total[...] = total_of([ref[:width, :] for ref in parts])
    gain = halves(joined(total_of([ref[width:, :] for ref in parts])))
    for k in range(RING):
        start = pl.multiple_of((place_ref[3] + k) % RING * quarter, quarter)
        outs[k][:quarter, :] = total[pl.ds(start, quarter), :].astype(bf16)
        outs[k][quarter:, :] = gain


def second_sum(place, parts):
    width = parts[0].shape[0] - 64
    vmem = pl.BlockSpec(memory_space=pltpu.VMEM)
    return pl.pallas_call(
        second_sum_kernel,
        out_shape=[jax.ShapeDtypeStruct((width // RING + 64, LANES), bf16)] * RING,
        in_specs=[pl.BlockSpec(memory_space=pltpu.SMEM)]
        + [vmem] * 4,
        out_specs=[vmem] * RING,
        scratch_shapes=[pltpu.VMEM((width, LANES), f32)],
        name="second_sum",
    )(place, *parts)


def stream_sum_kernel(*refs):
    parts, part_ref, gain_ref = refs[:4], refs[4], refs[5]
    quarter = part_ref.shape[0]
    total = total_of([ref[...] for ref in parts])
    part_ref[...] = total[:quarter, :].astype(bf16)
    gain_ref[...] = joined(total[quarter:, :])


def stream_sum(parts):
    quarter = parts[0].shape[0] - 64
    vmem = pl.BlockSpec(memory_space=pltpu.VMEM)
    return pl.pallas_call(
        stream_sum_kernel,
        out_shape=[
            jax.ShapeDtypeStruct((quarter, LANES), bf16),
            jax.ShapeDtypeStruct((32, LANES), f32),
        ],
        in_specs=[vmem] * 4,
        out_specs=[vmem] * 2,
        name="stream_sum",
    )(*parts)


def finish_kernel(place_ref, *refs):
    parts, out_ref = refs[:4], refs[4]
    quarter = parts[0].shape[0]
    for k in range(RING):
        start = pl.multiple_of((place_ref[3] - k + RING) % RING * quarter, quarter)
        out_ref[:, pl.ds(start, quarter)] = parts[k][...].astype(f32).T


def finish_call(place, parts):
    quarter = parts[0].shape[0]
    vmem = pl.BlockSpec(memory_space=pltpu.VMEM)
    return pl.pallas_call(
        finish_kernel,
        out_shape=jax.ShapeDtypeStruct((LANES, RING * quarter), f32),
        in_specs=[pl.BlockSpec(memory_space=pltpu.SMEM)] + [vmem] * 4,
        out_specs=vmem,
        name="d_proj_rows",
    )(place, *parts)


def stream_ring(values):
    count = lax.axis_size("dp")
    return [values[0]] + [
        lax.ppermute(values[k], "dp", [(i, (i + k) % count) for i in range(count)])
        for k in range(1, RING)
    ]


def on_device(
    byte_keys, byte_values, doc_ids, queries, patch_end, cotangent, proj_weight, norm_gain
):
    own, width = byte_keys.shape[1:]
    patches = queries.shape[1]
    seq_count = lax.axis_size("seq")
    seq_rank = lax.axis_index("seq")
    upward = [(i, i + 1) for i in range(seq_count - 1)]
    downward = [(i + 1, i) for i in range(seq_count - 1)]
    keys, values, docs = byte_keys[0], byte_values[0], doc_ids[0]
    place = jnp.stack([seq_rank // (2 * RING), seq_rank // 2 % RING, seq_rank % 2, lax.axis_index("dp")])

    low_docs = lax.ppermute(docs[own - LOW :], "seq", upward)
    high_docs = lax.ppermute(docs[:HIGH], "seq", downward)
    low = jnp.concatenate([keys[own - LOW :], values[own - LOW :]])
    high = jnp.concatenate([keys[:HIGH], values[:HIGH]])
    low, high = lax.ppermute(low, "seq", upward), lax.ppermute(high, "seq", downward)
    weights = lax.all_gather(proj_weight, "seq", axis=0, tiled=True)

    ext_docs = jnp.concatenate([low_docs, docs, high_docs])
    ends = patch_end[0] - (seq_rank * own - LOW)
    position = jnp.arange(ext_docs.shape[0], dtype=jnp.int32)
    last_doc = jnp.sum(
        jnp.where(position[None, :] == ends[:, None] - 1, ext_docs[None, :], 0), axis=1
    )
    earlier = (ext_docs[None, :] < last_doc[:, None]) & (position[None, :] < ends[:, None])
    doc_start = jnp.sum(earlier.astype(jnp.int32), axis=1)
    first = jnp.maximum(jnp.maximum(ends - WIN, doc_start), jnp.where(seq_rank == 0, LOW, 0))
    span = jnp.stack([first, ends], axis=1)
    offsets = jnp.clip(ends[::PG] - WIN, 0, LOW + own + HIGH - SLAB) // 16 * 16

    common = (offsets, span, low, high, keys, values, queries[0])
    attended, level = forward_call(common)
    peer_attended = to_peer(attended)

    mine, other, gain = latent_call(place, attended, norm_gain[None], cotangent[0], weights)
    peer_mine = to_peer(other)
    gain = gain.reshape(RING, 8, 8, LANES)[:, :, 0].transpose(1, 0, 2).reshape(8, 512)
    gain = gain + to_peer(gain)
    d_attended = d_attended_call(place, mine, other, weights)
    to_send = d_proj_call(mine, peer_mine, attended, peer_attended, halves(gain), d_attended)
    from_ring = ring(to_send, "first")

    inputs = common + (attended, level, d_attended)
    d_query, d_keys, d_values, d_low, d_high = backward_call(inputs, to_send[0])
    from_ring, d_low, d_high = lax.optimization_barrier((from_ring, d_low, d_high))
    from_above = lax.ppermute(d_low, "seq", downward)
    from_below = lax.ppermute(d_high, "seq", upward)
    from_ring = ring(first_sum(from_ring), "second")
    to_send = second_sum(place, from_ring)
    part, gain = stream_sum(stream_ring(to_send))
    d_proj = finish_call(place, stream_ring([part] * RING))
    d_gain = gain.reshape(-1)

    d_keys, d_values = rim_call(d_keys, d_values, from_below, from_above)
    return (d_query[None], d_keys[None], d_values[None], d_proj, d_gain)


def solution(mesh):
    in_specs = (
        P("dp", "seq", None),
        P("dp", "seq", None),
        P("dp", "seq"),
        P("dp", "seq", None),
        P("dp", "seq"),
        P("dp", "seq", None),
        P("seq", None),
        P(),
    )
    out_specs = (
        P("dp", "seq", None),
        P("dp", "seq", None),
        P("dp", "seq", None),
        P("seq", None),
        P(),
    )
    return jax.shard_map(
        on_device, mesh=mesh, in_specs=in_specs, out_specs=out_specs, check_vma=False
    )
```

time: 625 us -> 220 us (0.35)
  local copies, waits for them, and re-layouts: 229 us -> 13.7 us
  other arithmetic: 134 us -> 6.35 us
  Pallas kernels: 0 us -> 101 us
  matrix products: 83.5 us -> 0 us
  blocking collectives: 75.7 us -> 0 us
  waiting for transfers between devices: 36.5 us -> 50.6 us
  loops' own time: 13.3 us -> 0 us
    dynamic_update_slice x24 -> x0, local copies, waits for them, and re-layouts: 117 us -> none  [the longest x8 107 us: backward_group(): lax.dynamic_update_slice_in_dim(grad_bytes, current + jnp.concatenate([d_...]
    pallas_call x0 -> x10, Pallas kernels: none -> 101 us  [the longest x1 32.2 us: backward_call(): pl.pallas_call(backward_kernel, out_shape=[jax.ShapeDtypeStruct((count, w...]
    dot_general x59 -> x0, matrix products: 83.5 us -> none  [the longest x8 22.7 us: backward_group(): jnp.einsum('hpj,phd->jhd', probs.astype(jnp.bfloat16), d_out, preferred_e...]
    psum x1 -> x0, blocking collectives: 75.7 us -> none  [on_device(): d_gain = lax.psum(gain_terms, ('dp', 'seq'))]
    add x24 -> x0, other arithmetic: 46.2 us -> none  [the longest x8 46.1 us: backward_group(): current + jnp.concatenate([d_key, d_value], axis=1)]
    while x136 -> x0, local copies, waits for them, and re-layouts: 42 us -> none
    psum x1 -> x0, waiting for transfers between devices: 32.8 us -> none  [on_device(): d_proj = lax.psum(grad_part, 'dp').astype(jnp.float32)]
    all_gather x1, waiting for transfers between devices: 0.01 us -> 25.4 us  [on_device(): weights = lax.all_gather(proj_weight, 'seq', axis=0, tiled=True)]
  transfers between devices with their start and end apart: 9 -> 22, of which waited for: 2 -> 10; matrix products, arithmetic and copies ran while one was open for 68% -> 6% of each run, Pallas kernels for 0% -> 32%
where the time goes in v1:
time: 220 us
  Pallas kernels  101 us (46%)
  waiting for transfers between devices  50.6 us (23%)
  starting transfers between devices  33.8 us (15%)
  between operations  14.3 us (6%)
  local copies, waits for them, and re-layouts  13.7 us (6%)
  other arithmetic  6.35 us (3%)
    pallas_call x1, Pallas kernels, backward_call(): pl.pallas_call(backward_kernel, out_shape=[jax.ShapeDtypeStruct((count, w...  32.2 us
    all_gather x1, waiting for transfers between devices, on_device(): weights = lax.all_gather(proj_weight, 'seq', axis=0, tiled=True)  25.4 us
    pallas_call x1, Pallas kernels, forward_call(): pl.pallas_call(forward_kernel, out_shape=[jax.ShapeDtypeStruct((patches,...  18 us
    pallas_call x1, Pallas kernels, latent_call(): pl.pallas_call(latent_kernel, out_shape=[jax.ShapeDtypeStruct((patches, c...  17.7 us
    ppermute x6, waiting for transfers between devices, ring(): lax.ppermute(values[k], 'seq', along(which, k))  15.7 us
    pallas_call x1, Pallas kernels, d_attended_call(): pl.pallas_call(d_attended_kernel, out_shape=jax.ShapeDtypeStruct((patches...  9.94 us
    pallas_call x1, Pallas kernels, d_proj_call(): pl.pallas_call(d_proj_kernel, out_shape=[jax.ShapeDtypeStruct((width + 16...  9.27 us
    ppermute x6, starting transfers between devices, stream_ring(): lax.ppermute(values[k], 'dp', [(i, (i + k) % count) for i in range(count)])  9.17 us
  transfers between devices with their start and end apart: 22, of which 10 were waited for; matrix products, arithmetic and copies ran while one was open for 6% of the time, Pallas kernels for 32%

profile of v1, /device:TPU:0, one launch (start us, length us, event | category | flops | bytes accessed | tf_op | source)
XLA Modules:
  0.0 219.7 jit_solution(7994617828744612307)
XLA Ops:
  7.9 0.7 slice.45
  8.6 1.3 collective-permute-start.1
  9.9 0.7 slice_reduce_fusion
  10.6 3.0 %collective-permute-start = (s32[384]{0:T(512)S(1)}, s32[384]{0:T(512)S(1)}, u32[]{:S(2)}, u32[]{:S(2)}) collective-permute-start(s32[384]{0:T(512)S(1)} %slice_reduce_fusion), channel_id=1, source_target_pairs={{0,1},{1,2},{2,3},{3,4},{4,5},{5,6},{6,7},{7,8},{8,9},{9,10},{10,1... | collective-permute-start | bytes 4616 | tf_op jit(solution)/shard_map/ppermute | solution.py:622
  13.6 1.3 slice_bitcast_fusion.2
  14.9 1.0 pad_maximum_fusion.1
  15.9 1.4 collective-permute-start.3
  17.3 1.5 slice_bitcast_fusion
  18.8 1.3 pad_maximum_fusion
  20.1 3.8 %collective-permute-start.2 = (bf16[768,1024]{1,0:T(8,128)(2,1)}, bf16[768,1024]{1,0:T(8,128)(2,1)S(1)}, u32[]{:S(2)}, u32[]{:S(2)}) collective-permute-start(bf16[768,1024]{1,0:T(8,128)(2,1)} %pad_maximum_fusion), channel_id=1, source_target_pairs={{0,1},{1,2},{2,3},{3,4},{4,5},{5,6},{6,7},{7,8},{8,9},{9,10},{10,1... | collective-permute-start | bytes 4718600 | tf_op jit(solution)/shard_map/ppermute | solution.py:626
  25.3 0.9 select_reduce_fusion
  26.1 1.3 convert_reduce_fusion
  27.5 0.9 copy.25.span_ref
  28.4 1.0 copy-done.1
  30.0 18.0 %attention_forward.1 = (bf16[512,1024]{1,0:T(8,128)(2,1)}, f32[512,1024]{1,0:T(8,128)}) custom-call(s32[16]{0:T(128)} %fusion.1.offset_ref, s32[512,2]{1,0:T(8,128)} %copy.25.span_ref, bf16[768,1024]{1,0:T(8,128)(2,1)} %copy-done, bf16[512,1024]{1,0:T(8,128)(2,1)} %copy-done.1, bf16[2048,1024]{1,0:T(8,128)(2,1)} %bitcast.38, bf16[2048,1024]{1,0:T(8,128)(2,1)} %bitcast.36, ...), custom_call_target="tpu_custom_call" | custom-call | flops 805306368 | bytes 20971520 | tf_op jit(solution)/shard_map/attention_forward/pallas_call | solution.py:173
  48.0 25.4 %all-gather.2.cloned.1.call-done.weights_ref = bf16[4096,1024]{1,0:T(8,128)(2,1)} async-done(((bf16[128,1024]{1,0:T(8,128)(2,1)}), bf16[4096,1024]{1,0:T(8,128)(2,1)}) %all-gather.2.cloned.1.call-update) | async-done | bytes 8388624 | tf_op jit(solution)/shard_map/all_gather | solution.py:627
  73.4 17.7 %latent.1 = (bf16[512,2048]{1,0:T(8,128)(2,1)}, bf16[512,2048]{1,0:T(8,128)(2,1)}, f32[256,128]{1,0:T(8,128)}) custom-call(s32[4]{0:T(128)} %pad_add_fusion.2.place_ref, bf16[512,1024]{1,0:T(8,128)(2,1)} %get-tuple-element.37.attended_ref, f32[1,4096]{1,0:T(1,128)} %bitcast.55, bf16[512,4096]{1,0:T(8,128)(2,1)} %bitcast.53, ...), custom_call_target="tpu_custom_call" | custom-call | flops 4294967296 | bytes 18874368 | tf_op jit(solution)/shard_map/latent/pallas_call | solution.py:315
  91.7 0.9 slice.56
  93.1 9.9 %d_attended.1.after_ref.d_attended_ref = bf16[512,1024]{1,0:T(8,128)(2,1)} custom-call(s32[4]{0:T(128)} %pad_add_fusion.2.place_ref, bf16[512,2048]{1,0:T(8,128)(2,1)} %get-tuple-element.39.mine_ref, bf16[512,2048]{1,0:T(8,128)(2,1)} %get-tuple-element.40.other_ref, bf16[4096,1024]{1,0:T(8,128)(2,1)} %all-gather.2.cloned.1.call-done.weights_ref), custom_call_target="tpu_custom_call" | custom-call | flops 4294967296 | bytes 14680064 | tf_op jit(solution)/shard_map/d_attended/pallas_call | solution.py:363
  103.7 1.3 copy-done.18
  105.0 9.3 %d_proj.1 = (bf16[1040,512]{1,0:T(8,128)(2,1)}, bf16[1040,512]{1,0:T(8,128)(2,1)}, bf16[1040,512]{1,0:T(8,128)(2,1)}, bf16[1040,512]{1,0:T(8,128)(2,1)}) custom-call(bf16[512,2048]{1,0:T(8,128)(2,1)} %get-tuple-element.39.mine_ref, bf16[512,2048]{1,0:T(8,128)(2,1)} %copy-done.18, bf16[512,1024]{1,0:T(8,128)(2,1)} %get-tuple-element.37.attended_ref, ...), custom_call_target="tpu_custom_call" | custom-call | flops 4294967296 | bytes 12582912 | tf_op jit(solution)/shard_map/d_proj/pallas_call | solution.py:401
  114.3 1.1 collective-permute-start.7
  115.5 2.8 %collective-permute-start.8 = (bf16[1040,512]{1,0:T(8,128)(2,1)}, bf16[1040,512]{1,0:T(8,128)(2,1)S(1)}, u32[]{:S(2)}, u32[]{:S(2)}) collective-permute-start(bf16[1040,512]{1,0:T(8,128)(2,1)} %get-tuple-element.47), channel_id=1, source_target_pairs={{0,16},{1,5},{2,18},{3,7},{4,20},{5,1},{6,22},{7,3},{8,24},{9,13},... | collective-permute-start | bytes 3194888 | tf_op jit(solution)/shard_map/ppermute | solution.py:486
  118.3 1.4 collective-permute-start.9
  119.7 32.2 %attention_backward.1 = (bf16[512,1024]{1,0:T(8,128)(2,1)}, bf16[2048,1024]{1,0:T(8,128)(2,1)}, bf16[2048,1024]{1,0:T(8,128)(2,1)}, bf16[768,1024]{1,0:T(8,128)(2,1)}, bf16[512,1024]{1,0:T(8,128)(2,1)}) custom-call(s32[16]{0:T(128)} %fusion.1.offset_ref, s32[512,2]{1,0:T(8,128)} %copy.25.span_ref, bf16[768,1024]{1,0:T(8,128)(2,1)} %copy-done, ...), custom_call_target="tpu_custom_call" | custom-call | flops 2818572288 | bytes 41943040 | tf_op jit(solution)/shard_map/attention_backward/pallas_call | solution.py:211
  152.0 1.0 copy-done.4
  153.4 1.3 collective-permute-start.11
  154.7 4.1 %collective-permute-start.10 = (bf16[512,1024]{1,0:T(8,128)(2,1)}, bf16[512,1024]{1,0:T(8,128)(2,1)}, u32[]{:S(2)}, u32[]{:S(2)}) collective-permute-start(bf16[512,1024]{1,0:T(8,128)(2,1)} %get-tuple-element.51), channel_id=1, source_target_pairs={{0,1},{1,2},{2,3},{3,4},{4,5},{5,6},{6,7},{7,8},{8,9},{9,10},{10,1... | collective-permute-start | bytes 3145736 | tf_op jit(solution)/shard_map/ppermute | solution.py:657
  158.8 3.5 %first_sum.1 = (bf16[1088,128]{1,0:T(8,128)(2,1)}, bf16[1088,128]{1,0:T(8,128)(2,1)}, bf16[1088,128]{1,0:T(8,128)(2,1)}, bf16[1088,128]{1,0:T(8,128)(2,1)}) custom-call(bf16[1040,512]{1,0:T(8,128)(2,1)} %get-tuple-element.55.after_ref.refs_0_, bf16[1040,512]{1,0:T(8,128)(2,1)} %copy-done.3, bf16[1040,512]{1,0:T(8,128)(2,1)} %copy-done.4, ...), custom_call_target="tpu_custom_call" | custom-call | tf_op jit(solution)/shard_map/first_sum/pallas_call | solution.py:523
  162.2 1.8 collective-permute-start.13
  164.0 1.4 collective-permute-start.14
  165.5 9.2 %collective-permute-done.12.refs_1_ = bf16[1088,128]{1,0:T(8,128)(2,1)S(1)} collective-permute-done((bf16[1088,128]{1,0:T(8,128)(2,1)}, bf16[1088,128]{1,0:T(8,128)(2,1)S(1)}, u32[]{:S(2)}, u32[]{:S(2)}) %collective-permute-start.12) | collective-permute-done | bytes 278560 | tf_op jit(solution)/shard_map/ppermute | solution.py:486
  174.7 3.1 %collective-permute-done.13.refs_2_ = bf16[1088,128]{1,0:T(8,128)(2,1)S(1)} collective-permute-done((bf16[1088,128]{1,0:T(8,128)(2,1)}, bf16[1088,128]{1,0:T(8,128)(2,1)S(1)}, u32[]{:S(2)}, u32[]{:S(2)}) %collective-permute-start.13) | collective-permute-done | bytes 278560 | tf_op jit(solution)/shard_map/ppermute | solution.py:486
  177.8 3.3 %collective-permute-done.14.refs_3_ = bf16[1088,128]{1,0:T(8,128)(2,1)S(1)} collective-permute-done((bf16[1088,128]{1,0:T(8,128)(2,1)}, bf16[1088,128]{1,0:T(8,128)(2,1)S(1)}, u32[]{:S(2)}, u32[]{:S(2)}) %collective-permute-start.14) | collective-permute-done | bytes 278560 | tf_op jit(solution)/shard_map/ppermute | solution.py:486
  181.1 0.7 copy-done.9
  181.9 2.2 %second_sum.1 = (bf16[320,128]{1,0:T(8,128)(2,1)}, bf16[320,128]{1,0:T(8,128)(2,1)}, bf16[320,128]{1,0:T(8,128)(2,1)}, bf16[320,128]{1,0:T(8,128)(2,1)}) custom-call(s32[4]{0:T(128)} %pad_add_fusion.2.place_ref, bf16[1088,128]{1,0:T(8,128)(2,1)} %get-tuple-element.59.refs_0_, bf16[1088,128]{1,0:T(8,128)(2,1)} %copy-done.7, bf16[1088,128]{1,0:T(8,128)(2,1)} %copy-done.8, ...), custom_call_target="tpu_custom_call" | custom-call | tf_op jit(solution)/shard_map/second_sum/pallas_call | solution.py:548
  184.1 1.5 collective-permute-start.15
  185.6 2.7 %collective-permute-start.16 = (bf16[320,128]{1,0:T(8,128)(2,1)}, bf16[320,128]{1,0:T(8,128)(2,1)S(1)}, u32[]{:S(2)}, u32[]{:S(2)}) collective-permute-start(bf16[320,128]{1,0:T(8,128)(2,1)} %get-tuple-element.65), channel_id=1, source_target_pairs={{0,64},{32,96},{64,0},{96,32},{1,65},{33,97},{65,1},{97,33},{2,66}... | collective-permute-start | bytes 245768 | tf_op jit(solution)/shard_map/ppermute | solution.py:605
  188.3 1.4 collective-permute-start.17
  189.9 1.8 collective-permute-done.16.refs_2_
  191.8 1.1 collective-permute-done.17.refs_3_
  193.6 1.7 stream_sum.1
  195.2 2.7 %collective-permute-start.20 = (bf16[256,128]{1,0:T(8,128)(2,1)}, bf16[256,128]{1,0:T(8,128)(2,1)S(1)}, u32[]{:S(2)}, u32[]{:S(2)}) collective-permute-start(bf16[256,128]{1,0:T(8,128)(2,1)} %get-tuple-element.67.refs_0_), channel_id=1, source_target_pairs={{0,96},{32,0},{64,32},{96,64},{1,97},{33,1},{65,33},{97,65},{2,98}... | collective-permute-start | bytes 196616 | tf_op jit(solution)/shard_map/ppermute | solution.py:605
  198.8 2.0 collective-permute-done.20.refs_3_
  200.7 3.3 %collective-permute-done.19.refs_2_ = bf16[256,128]{1,0:T(8,128)(2,1)S(1)} collective-permute-done((bf16[256,128]{1,0:T(8,128)(2,1)}, bf16[256,128]{1,0:T(8,128)(2,1)S(1)}, u32[]{:S(2)}, u32[]{:S(2)}) %collective-permute-start.19) | collective-permute-done | bytes 65568 | tf_op jit(solution)/shard_map/ppermute | solution.py:605
  205.2 1.9 d_proj_rows.1
  207.1 1.2 copy-done.2
  208.3 4.6 %rims.1 = (bf16[2048,1024]{1,0:T(8,128)(2,1)}, bf16[2048,1024]{1,0:T(8,128)(2,1)}) custom-call(bf16[2048,1024]{1,0:T(8,128)(2,1)} %get-tuple-element.44.key_in, bf16[2048,1024]{1,0:T(8,128)(2,1)} %get-tuple-element.45.value_in, bf16[512,1024]{1,0:T(8,128)(2,1)} %collective-permute-done.10.below_ref, ...), custom_call_target="tpu_custom_call", output_to_operand_aliasing={{0}: (0, {}), {1}: (1, {})} | custom-call | tf_op jit(solution)/shard_map/rims/pallas_call | solution.py:455
  (66 shorter events, 7.7 us)
Async XLA Ops:
  7.2 66.2 %all-gather.2.cloned.1.call-start = ((), (), s32[]{:S(2)}) async-start(), calls=%async_computation | async-start | bytes 8650752 | tf_op jit(solution)/shard_map/all_gather | solution.py:627
  8.6 16.7 %collective-permute-start.1 = (s32[256]{0:T(256)S(1)}, s32[256]{0:T(256)S(1)}, u32[]{:S(2)}, u32[]{:S(2)}) collective-permute-start(s32[256]{0:T(256)S(1)} %bitcast.52), channel_id=1, source_target_pairs={{1,0},{2,1},{3,2},{4,3},{5,4},{6,5},{7,6},{8,7},{9,8},{10,9},{11,1... | collective-permute-start | bytes 3080 | tf_op jit(solution)/shard_map/ppermute | solution.py:623
  10.6 14.7 %collective-permute-start = (s32[384]{0:T(512)S(1)}, s32[384]{0:T(512)S(1)}, u32[]{:S(2)}, u32[]{:S(2)}) collective-permute-start(s32[384]{0:T(512)S(1)} %slice_reduce_fusion), channel_id=1, source_target_pairs={{0,1},{1,2},{2,3},{3,4},{4,5},{5,6},{6,7},{7,8},{8,9},{9,10},{10,1... | collective-permute-start | bytes 4616 | tf_op jit(solution)/shard_map/ppermute | solution.py:622
  15.9 8.0 %copy-start.16 = (s32[1,512]{1,0:T(1,128)S(1)}, s32[1,512]{1,0:T(1,128)}, u32[]{:S(2)}) copy-start(s32[1,512]{1,0:T(1,128)} %param.12) | copy-start | bytes 6148
  15.9 9.3 %copy-start.17 = (s32[1,2048]{1,0:T(1,128)S(1)}, s32[1,2048]{1,0:T(1,128)}, u32[]{:S(2)}) copy-start(s32[1,2048]{1,0:T(1,128)} %param.10) | copy-start | bytes 24580
  15.9 12.5 %collective-permute-start.3 = (bf16[512,1024]{1,0:T(8,128)(2,1)}, bf16[512,1024]{1,0:T(8,128)(2,1)S(1)}, u32[]{:S(2)}, u32[]{:S(2)}) collective-permute-start(bf16[512,1024]{1,0:T(8,128)(2,1)} %pad_maximum_fusion.1), channel_id=1, source_target_pairs={{1,0},{2,1},{3,2},{4,3},{5,4},{6,5},{7,6},{8,7},{9,8},{10,9},{11,1... | collective-permute-start | bytes 3145736 | tf_op jit(solution)/shard_map/ppermute | solution.py:626
  20.1 8.3 %collective-permute-start.2 = (bf16[768,1024]{1,0:T(8,128)(2,1)}, bf16[768,1024]{1,0:T(8,128)(2,1)S(1)}, u32[]{:S(2)}, u32[]{:S(2)}) collective-permute-start(bf16[768,1024]{1,0:T(8,128)(2,1)} %pad_maximum_fusion), channel_id=1, source_target_pairs={{0,1},{1,2},{2,3},{3,4},{4,5},{5,6},{6,7},{7,8},{8,9},{9,10},{10,1... | collective-permute-start | bytes 4718600 | tf_op jit(solution)/shard_map/ppermute | solution.py:626
  28.4 1.1 copy-start.1
  28.4 1.6 copy-start
  73.4 18.1 %copy-start.6 = (bf16[512,1024]{1,0:T(8,128)(2,1)S(1)}, bf16[512,1024]{1,0:T(8,128)(2,1)}, u32[]{:S(2)}) copy-start(bf16[512,1024]{1,0:T(8,128)(2,1)} %get-tuple-element.37.attended_ref) | copy-start | bytes 3145732
  91.1 12.6 %collective-permute-start.4 = (bf16[512,2048]{1,0:T(8,128)(2,1)}, bf16[512,2048]{1,0:T(8,128)(2,1)S(1)}, u32[]{:S(2)}, u32[]{:S(2)}) collective-permute-start(bf16[512,2048]{1,0:T(8,128)(2,1)} %get-tuple-element.40.other_ref), channel_id=1, source_target_pairs={{0,1},{1,0},{2,3},{3,2},{4,5},{5,4},{6,7},{7,6},{8,9},{9,8},{10,11... | collective-permute-start | bytes 6291464 | tf_op jit(solution)/shard_map/ppermute | solution.py:481
  91.4 12.3 %collective-permute-start.5 = (bf16[512,1024]{1,0:T(8,128)(2,1)S(1)}, bf16[512,1024]{1,0:T(8,128)(2,1)}, u32[]{:S(2)}, u32[]{:S(2)}) collective-permute-start(bf16[512,1024]{1,0:T(8,128)(2,1)S(1)} %copy-done.6), channel_id=1, source_target_pairs={{0,1},{1,0},{2,3},{3,2},{4,5},{5,4},{6,7},{7,6},{8,9},{9,8},{10,11... | collective-permute-start | bytes 3145736 | tf_op jit(solution)/shard_map/ppermute | solution.py:481
  92.6 10.4 %collective-permute-start.6 = (f32[8,512]{1,0:T(8,128)S(1)}, f32[8,512]{1,0:T(8,128)S(1)}, u32[]{:S(2)}, u32[]{:S(2)}) collective-permute-start(f32[8,512]{1,0:T(8,128)S(1)} %bitcast.44), channel_id=1, source_target_pairs={{0,1},{1,0},{2,3},{3,2},{4,5},{5,4},{6,7},{7,6},{8,9},{9,8},{10,11... | collective-permute-start | bytes 49160 | tf_op jit(solution)/shard_map/ppermute | solution.py:481
  103.7 1.3 copy-start.18
  114.3 37.6 %collective-permute-start.7 = (bf16[1040,512]{1,0:T(8,128)(2,1)}, bf16[1040,512]{1,0:T(8,128)(2,1)S(1)}, u32[]{:S(2)}, u32[]{:S(2)}) collective-permute-start(bf16[1040,512]{1,0:T(8,128)(2,1)} %get-tuple-element.46), channel_id=1, source_target_pairs={{0,8},{1,3},{2,10},{3,5},{4,12},{5,7},{6,14},{7,1},{8,16},{9,11},{... | collective-permute-start | bytes 3194888 | tf_op jit(solution)/shard_map/ppermute | solution.py:486
  115.5 36.5 %collective-permute-start.8 = (bf16[1040,512]{1,0:T(8,128)(2,1)}, bf16[1040,512]{1,0:T(8,128)(2,1)S(1)}, u32[]{:S(2)}, u32[]{:S(2)}) collective-permute-start(bf16[1040,512]{1,0:T(8,128)(2,1)} %get-tuple-element.47), channel_id=1, source_target_pairs={{0,16},{1,5},{2,18},{3,7},{4,20},{5,1},{6,22},{7,3},{8,24},{9,13},... | collective-permute-start | bytes 3194888 | tf_op jit(solution)/shard_map/ppermute | solution.py:486
  118.3 33.7 %collective-permute-start.9 = (bf16[1040,512]{1,0:T(8,128)(2,1)}, bf16[1040,512]{1,0:T(8,128)(2,1)S(1)}, u32[]{:S(2)}, u32[]{:S(2)}) collective-permute-start(bf16[1040,512]{1,0:T(8,128)(2,1)} %get-tuple-element.48), channel_id=1, source_target_pairs={{0,24},{1,7},{2,26},{3,1},{4,28},{5,3},{6,30},{7,5},{8,0},{9,15},{... | collective-permute-start | bytes 3194888 | tf_op jit(solution)/shard_map/ppermute | solution.py:486
  151.9 6.8 %copy-start.3 = (bf16[1040,512]{1,0:T(8,128)(2,1)}, bf16[1040,512]{1,0:T(8,128)(2,1)S(1)}, u32[]{:S(2)}) copy-start(bf16[1040,512]{1,0:T(8,128)(2,1)S(1)} %collective-permute-done.7.refs_1_) | copy-start | bytes 3194884
  152.0 1.0 copy-start.4
  152.0 1.4 copy-start.5
  153.4 53.7 %collective-permute-start.11 = (bf16[768,1024]{1,0:T(8,128)(2,1)}, bf16[768,1024]{1,0:T(8,128)(2,1)S(1)}, u32[]{:S(2)}, u32[]{:S(2)}) collective-permute-start(bf16[768,1024]{1,0:T(8,128)(2,1)} %get-tuple-element.52), channel_id=1, source_target_pairs={{1,0},{2,1},{3,2},{4,3},{5,4},{6,5},{7,6},{8,7},{9,8},{10,9},{11,1... | collective-permute-start | bytes 4718600 | tf_op jit(solution)/shard_map/ppermute | solution.py:656
  154.7 52.4 %collective-permute-start.10 = (bf16[512,1024]{1,0:T(8,128)(2,1)}, bf16[512,1024]{1,0:T(8,128)(2,1)}, u32[]{:S(2)}, u32[]{:S(2)}) collective-permute-start(bf16[512,1024]{1,0:T(8,128)(2,1)} %get-tuple-element.51), channel_id=1, source_target_pairs={{0,1},{1,2},{2,3},{3,4},{4,5},{5,6},{6,7},{7,8},{8,9},{9,10},{10,1... | collective-permute-start | bytes 3145736 | tf_op jit(solution)/shard_map/ppermute | solution.py:657
  162.2 12.4 %collective-permute-start.12 = (bf16[1088,128]{1,0:T(8,128)(2,1)}, bf16[1088,128]{1,0:T(8,128)(2,1)S(1)}, u32[]{:S(2)}, u32[]{:S(2)}) collective-permute-start(bf16[1088,128]{1,0:T(8,128)(2,1)} %get-tuple-element.60), channel_id=1, source_target_pairs={{0,2},{1,9},{2,4},{3,11},{4,6},{5,13},{6,0},{7,15},{8,10},{9,17},{... | collective-permute-start | bytes 835592 | tf_op jit(solution)/shard_map/ppermute | solution.py:486
  162.2 15.6 %collective-permute-start.13 = (bf16[1088,128]{1,0:T(8,128)(2,1)}, bf16[1088,128]{1,0:T(8,128)(2,1)S(1)}, u32[]{:S(2)}, u32[]{:S(2)}) collective-permute-start(bf16[1088,128]{1,0:T(8,128)(2,1)} %get-tuple-element.61), channel_id=1, source_target_pairs={{0,4},{1,17},{2,6},{3,19},{4,0},{5,21},{6,2},{7,23},{8,12},{9,25},... | collective-permute-start | bytes 835592 | tf_op jit(solution)/shard_map/ppermute | solution.py:486
  164.0 17.1 %collective-permute-start.14 = (bf16[1088,128]{1,0:T(8,128)(2,1)}, bf16[1088,128]{1,0:T(8,128)(2,1)S(1)}, u32[]{:S(2)}, u32[]{:S(2)}) collective-permute-start(bf16[1088,128]{1,0:T(8,128)(2,1)} %get-tuple-element.62), channel_id=1, source_target_pairs={{0,6},{1,25},{2,0},{3,27},{4,2},{5,29},{6,4},{7,31},{8,14},{9,1},{... | collective-permute-start | bytes 835592 | tf_op jit(solution)/shard_map/ppermute | solution.py:486
  174.7 6.5 %copy-start.7 = (bf16[1088,128]{1,0:T(8,128)(2,1)}, bf16[1088,128]{1,0:T(8,128)(2,1)S(1)}, u32[]{:S(2)}) copy-start(bf16[1088,128]{1,0:T(8,128)(2,1)S(1)} %collective-permute-done.12.refs_1_) | copy-start | bytes 835588
  177.8 3.4 %copy-start.8 = (bf16[1088,128]{1,0:T(8,128)(2,1)}, bf16[1088,128]{1,0:T(8,128)(2,1)S(1)}, u32[]{:S(2)}) copy-start(bf16[1088,128]{1,0:T(8,128)(2,1)S(1)} %collective-permute-done.13.refs_2_) | copy-start | bytes 835588
  181.1 0.7 copy-start.9
  184.1 5.9 %collective-permute-start.15 = (bf16[320,128]{1,0:T(8,128)(2,1)}, bf16[320,128]{1,0:T(8,128)(2,1)S(1)}, u32[]{:S(2)}, u32[]{:S(2)}) collective-permute-start(bf16[320,128]{1,0:T(8,128)(2,1)} %get-tuple-element.64), channel_id=1, source_target_pairs={{0,32},{32,64},{64,96},{96,0},{1,33},{33,65},{65,97},{97,1},{2,34}... | collective-permute-start | bytes 245768 | tf_op jit(solution)/shard_map/ppermute | solution.py:605
  185.6 6.2 %collective-permute-start.16 = (bf16[320,128]{1,0:T(8,128)(2,1)}, bf16[320,128]{1,0:T(8,128)(2,1)S(1)}, u32[]{:S(2)}, u32[]{:S(2)}) collective-permute-start(bf16[320,128]{1,0:T(8,128)(2,1)} %get-tuple-element.65), channel_id=1, source_target_pairs={{0,64},{32,96},{64,0},{96,32},{1,65},{33,97},{65,1},{97,33},{2,66}... | collective-permute-start | bytes 245768 | tf_op jit(solution)/shard_map/ppermute | solution.py:605
  188.3 4.7 %collective-permute-start.17 = (bf16[320,128]{1,0:T(8,128)(2,1)}, bf16[320,128]{1,0:T(8,128)(2,1)S(1)}, u32[]{:S(2)}, u32[]{:S(2)}) collective-permute-start(bf16[320,128]{1,0:T(8,128)(2,1)} %get-tuple-element.66), channel_id=1, source_target_pairs={{0,96},{32,0},{64,32},{96,64},{1,97},{33,1},{65,33},{97,65},{2,98}... | collective-permute-start | bytes 245768 | tf_op jit(solution)/shard_map/ppermute | solution.py:605
  189.9 3.0 %copy-start.10 = (bf16[320,128]{1,0:T(8,128)(2,1)}, bf16[320,128]{1,0:T(8,128)(2,1)S(1)}, u32[]{:S(2)}) copy-start(bf16[320,128]{1,0:T(8,128)(2,1)S(1)} %collective-permute-done.15.refs_1_) | copy-start | bytes 245764
  191.8 1.2 copy-start.11
  192.9 0.6 copy-start.12
  195.2 5.5 %collective-permute-start.20 = (bf16[256,128]{1,0:T(8,128)(2,1)}, bf16[256,128]{1,0:T(8,128)(2,1)S(1)}, u32[]{:S(2)}, u32[]{:S(2)}) collective-permute-start(bf16[256,128]{1,0:T(8,128)(2,1)} %get-tuple-element.67.refs_0_), channel_id=1, source_target_pairs={{0,96},{32,0},{64,32},{96,64},{1,97},{33,1},{65,33},{97,65},{2,98}... | collective-permute-start | bytes 196616 | tf_op jit(solution)/shard_map/ppermute | solution.py:605
  197.9 6.1 %collective-permute-start.19 = (bf16[256,128]{1,0:T(8,128)(2,1)}, bf16[256,128]{1,0:T(8,128)(2,1)S(1)}, u32[]{:S(2)}, u32[]{:S(2)}) collective-permute-start(bf16[256,128]{1,0:T(8,128)(2,1)} %get-tuple-element.67.refs_0_), channel_id=1, source_target_pairs={{0,64},{32,96},{64,0},{96,32},{1,65},{33,97},{65,1},{97,33},{2,66}... | collective-permute-start | bytes 196616 | tf_op jit(solution)/shard_map/ppermute | solution.py:605
  198.1 6.4 %collective-permute-start.18 = (bf16[256,128]{1,0:T(8,128)(2,1)}, bf16[256,128]{1,0:T(8,128)(2,1)S(1)}, u32[]{:S(2)}, u32[]{:S(2)}) collective-permute-start(bf16[256,128]{1,0:T(8,128)(2,1)} %get-tuple-element.67.refs_0_), channel_id=1, source_target_pairs={{0,32},{32,64},{64,96},{96,0},{1,33},{33,65},{65,97},{97,1},{2,34}... | collective-permute-start | bytes 196616 | tf_op jit(solution)/shard_map/ppermute | solution.py:605
  200.7 3.7 %copy-start.13 = (bf16[256,128]{1,0:T(8,128)(2,1)}, bf16[256,128]{1,0:T(8,128)(2,1)S(1)}, u32[]{:S(2)}) copy-start(bf16[256,128]{1,0:T(8,128)(2,1)S(1)} %collective-permute-done.20.refs_3_) | copy-start | bytes 196612
  204.0 0.6 copy-start.14
  204.6 0.6 copy-start.15
  207.1 1.2 copy-start.2
Sparse Core Ops, SparseCore 0:
  10.3 63.0 all-gather.1

commit v2 on v1

--- a/solution.py
+++ b/solution.py
@@ -1,3 +1,4 @@
+import functools
 import math
 
 import jax
@@ -12,8 +13,11 @@
 WIN = 128
 LOW = 384
 HIGH = 256
-PG = 32
-SLAB = 384
+PG = 64
+SLAB = 592
+SHORT = 448
+PAD = 400
+PAIR = 2
 RING = 4
 LANES = 128
 
@@ -37,152 +41,205 @@
     return lax.dot_general(a, b, (((0,), (0,)), ((), ())), preferred_element_type=f32)
 
 
-def of_head(head):
-    return slice(head * HD, (head + 1) * HD)
+def of_pair(pair):
+    return slice(pair * PAIR * HD, (pair + 1) * PAIR * HD)
+
+
+def spread(block):
+    column = lax.broadcasted_iota(jnp.int32, block.shape, 1)
+    zero = jnp.zeros_like(block)
+    return jnp.concatenate(
+        [jnp.where(column // HD == head, block, zero) for head in range(PAIR)]
+    )
+
+
+def gathered_heads(block):
+    rows = block.shape[0] // PAIR
+    return jnp.concatenate(
+        [block[h * rows : (h + 1) * rows, h * HD : (h + 1) * HD] for h in range(PAIR)], axis=1
+    )
 
 
 def fetch_bytes(low_ref, high_ref, keys_ref, values_ref, key_ext, value_ext, sems):
     own = keys_ref.shape[0]
     copies = []
     for which, (own_ref, ext) in enumerate(((keys_ref, key_ext), (values_ref, value_ext))):
-        parts = (
+        parts = [
             (low_ref.at[pl.ds(which * LOW, LOW)], pl.ds(0, LOW)),
-            (own_ref, pl.ds(LOW, own)),
             (high_ref.at[pl.ds(which * HIGH, HIGH)], pl.ds(LOW + own, HIGH)),
-        )
-        for part, (source, rows) in enumerate(parts):
+        ]
+        parts += [
+            (own_ref.at[pl.ds(start, 256)], pl.ds(LOW + start, 256))
+            for start in range(0, own, 256)
+        ]
+        for source, rows in parts:
             copies.append(
-                pltpu.make_async_copy(source, ext.at[rows], sems.at[which * 3 + part])
+                pltpu.make_async_copy(source, ext.at[rows], sems.at[len(copies)])
             )
     return copies
 
 
-def visible_bias(offset, span_ref, rows):
-    position = offset + lax.broadcasted_iota(jnp.int32, (PG, SLAB), 1)
-    visible = (position >= span_ref[rows, 0:1]) & (position < span_ref[rows, 1:2])
+def load_bytes(low_ref, high_ref, keys_ref, values_ref, key_ext, value_ext, sems, totals):
+    copies = fetch_bytes(low_ref, high_ref, keys_ref, values_ref, key_ext, value_ext, sems)
+    for copy in copies:
+        copy.start()
+    rows = key_ext.shape[0] - PAD
+    for ext in (key_ext, value_ext):
+        ext[rows:, :] = jnp.zeros((PAD, ext.shape[1]), bf16)
+    for total in totals:
+        total[...] = jnp.zeros_like(total)
+    for copy in copies:
+        copy.wait()
+
+
+def visible_bias(offset, length, span):
+    position = offset + lax.broadcasted_iota(jnp.int32, (length, PAIR * PG), 0)
+    visible = (position >= span[0:1, :]) & (position < span[1:2, :])
     return jnp.where(visible, 0.0, masked_score)
 
 
+def each_group(offset_ref, short_ref, groups, one_group):
+    step = pl.program_id(0)
+
+    def body(group, carry):
+        offset = pl.multiple_of(offset_ref[step * groups + group], 16)
+        short = short_ref[step * groups + group]
+
+        @pl.when(short == 1)
+        def _():
+            one_group(group, offset, SHORT)
+
+        @pl.when(short == 0)
+        def _():
+            one_group(group, offset, SLAB)
+
+        return carry
+
+    lax.fori_loop(0, groups, body, 0)
+
+
 def forward_kernel(
-    offset_ref, span_ref, low_ref, high_ref, keys_ref, values_ref, query_ref,
+    offset_ref, short_ref, span_ref, low_ref, high_ref, keys_ref, values_ref, query_ref,
     attended_ref, level_ref, key_ext, value_ext, sems,
 ):
-    step = pl.program_id(0)
-
-    @pl.when(step == 0)
+    @pl.when(pl.program_id(0) == 0)
     def _():
-        copies = fetch_bytes(low_ref, high_ref, keys_ref, values_ref, key_ext, value_ext, sems)
-        for copy in copies:
-            copy.start()
+        load_bytes(low_ref, high_ref, keys_ref, values_ref, key_ext, value_ext, sems, ())
+
+    def one_group(group, offset, length):
+        rows = pl.ds(pl.multiple_of(group * PG, PG), PG)
+        marks = pl.ds(pl.multiple_of(group * 8, 8), 8)
+        slab = pl.ds(offset, length)
+        bias = visible_bias(offset, length, span_ref[marks, :])
+        pairs = [of_pair(pair) for pair in range(HEADS // PAIR)]
+        scores = [dot_rows(key_ext[slab, c], spread(query_ref[rows, c])) for c in pairs]
+        scores = [x * score_scale + bias for x in scores]
+        top = [jnp.max(x, axis=0, keepdims=True) for x in scores]
+        expo = [jnp.exp(x - y) for x, y in zip(scores, top)]
+        total = [jnp.sum(x, axis=0, keepdims=True) for x in expo]
+        probs = [(x * (1.0 / y)).astype(bf16) for x, y in zip(expo, total)]
+        attended = [dot_columns(x, value_ext[slab, c]) for x, c in zip(probs, pairs)]
+        for x, c in zip(attended, pairs):
+            attended_ref[rows, c] = gathered_heads(x).astype(bf16)
+        level = [x + jnp.log(y) for x, y in zip(top, total)]
+        level.append(jnp.zeros((8 - len(pairs), PAIR * PG), f32))
+        level_ref[marks, :] = jnp.concatenate(level)
+
+    each_group(offset_ref, short_ref, query_ref.shape[0] // PG, one_group)
+
+
+def backward_kernel(
+    offset_ref, short_ref, span_ref, low_ref, high_ref, keys_ref, values_ref, query_ref,
+    attended_ref, level_ref, d_attended_ref, after_ref,
+    d_query_ref, d_key_ref, d_value_ref, d_low_ref, d_high_ref,
+    key_ext, value_ext, sems, d_key, d_value, key_out, value_out, out_sems,
+):
+    own = keys_ref.shape[0]
+
+    @pl.when(pl.program_id(0) == 0)
+    def _():
+        load_bytes(
+            low_ref, high_ref, keys_ref, values_ref, key_ext, value_ext, sems, (d_key, d_value)
+        )
+
+    def one_group(group, offset, length):
+        rows = pl.ds(pl.multiple_of(group * PG, PG), PG)
+        marks = pl.ds(pl.multiple_of(group * 8, 8), 8)
+        slab = pl.ds(offset, length)
+        bias = visible_bias(offset, length, span_ref[marks, :])
+        levels = level_ref[marks, :]
+        for first in range(0, HEADS // PAIR, 2):
+            pairs = [of_pair(pair) for pair in range(first, first + 2)]
+            query = [spread(query_ref[rows, c]) for c in pairs]
+            d_out = [spread(d_attended_ref[rows, c]) for c in pairs]
+            scores = [dot_rows(key_ext[slab, c], x) for x, c in zip(query, pairs)]
+            d_probs = [dot_rows(value_ext[slab, c], x) for x, c in zip(d_out, pairs)]
+            row_dot = []
+            for c in pairs:
+                both = d_attended_ref[rows, c].astype(f32) * attended_ref[rows, c].astype(f32)
+                both = jnp.concatenate([both[:, h * HD : (h + 1) * HD] for h in range(PAIR)])
+                row_dot.append(jnp.sum(both.T, axis=0, keepdims=True))
+            probs = [
+                jnp.exp(x * score_scale + bias - levels[first + i : first + i + 1, :])
+                for i, x in enumerate(scores)
+            ]
+            d_scores = [
+                (x * (y - z) * score_scale).astype(bf16)
+                for x, y, z in zip(probs, d_probs, row_dot)
+            ]
+            probs = [x.astype(bf16) for x in probs]
+            for c, x in zip(pairs, d_scores):
+                d_query = dot_columns(x, key_ext[slab, c])
+                d_query_ref[rows, c] = gathered_heads(d_query).astype(bf16)
+            for c, x, y in zip(pairs, d_scores, query):
+                d_key[slab, c] += dot(x, y)
+            for c, x, y in zip(pairs, probs, d_out):
+                d_value[slab, c] += dot(x, y)
+
+    each_group(offset_ref, short_ref, query_ref.shape[0] // PG, one_group)
+
+    @pl.when(pl.program_id(0) == pl.num_programs(0) - 1)
+    def _():
+        copies = []
+        sources = ((d_key, key_out, d_key_ref), (d_value, value_out, d_value_ref))
+        for which, (total, staged, out_ref) in enumerate(sources):
+            parts = [(0, LOW, d_low_ref, which * LOW), (LOW + own, HIGH, d_high_ref, which * HIGH)]
+            parts += [(LOW + start, 256, out_ref, start) for start in range(0, own, 256)]
+            for start, count, out, place in parts:
+                rows = slice(start, start + count)
+                staged[rows, :] = total[rows, :].astype(bf16)
+                copy = pltpu.make_async_copy(
+                    staged.at[pl.ds(start, count)],
+                    out.at[pl.ds(place, count)],
+                    out_sems.at[len(copies)],
+                )
+                copy.start()
+                copies.append(copy)
         for copy in copies:
             copy.wait()
 
-    groups = query_ref.shape[0] // PG
-
-    def one_group(group, carry):
-        rows = pl.ds(pl.multiple_of(group * PG, PG), PG)
-        offset = pl.multiple_of(offset_ref[step * groups + group], 16)
-        slab = pl.ds(offset, SLAB)
-        bias = visible_bias(offset, span_ref, rows)
-        heads = [of_head(head) for head in range(HEADS)]
-        scores = [dot_rows(query_ref[rows, h], key_ext[slab, h]) for h in heads]
-        scores = [x * score_scale + bias for x in scores]
-        top = [jnp.max(x, axis=1, keepdims=True) for x in scores]
-        expo = [jnp.exp(x - y) for x, y in zip(scores, top)]
-        total = [jnp.sum(x, axis=1, keepdims=True) for x in expo]
-        probs = [(x * (1.0 / y)).astype(bf16) for x, y in zip(expo, total)]
-        attended = [dot(x, value_ext[slab, h]) for x, h in zip(probs, heads)]
-        for h, x, y, z in zip(heads, attended, top, total):
-            attended_ref[rows, h] = x.astype(bf16)
-            level_ref[rows, h] = jnp.broadcast_to(y + jnp.log(z), (PG, HD))
-        return carry
-
-    lax.fori_loop(0, groups, one_group, 0)
-
-
-def backward_kernel(
-    offset_ref, span_ref, low_ref, high_ref, keys_ref, values_ref, query_ref,
-    attended_ref, level_ref, d_attended_ref, after_ref,
-    d_query_ref, d_key_ref, d_value_ref, d_low_ref, d_high_ref,
-    key_ext, value_ext, sems, d_key, d_value,
-):
-    step = pl.program_id(0)
-    own = keys_ref.shape[0]
-
-    @pl.when(step == 0)
-    def _():
-        copies = fetch_bytes(low_ref, high_ref, keys_ref, values_ref, key_ext, value_ext, sems)
-        for copy in copies:
-            copy.start()
-        d_key[...] = jnp.zeros_like(d_key)
-        d_value[...] = jnp.zeros_like(d_value)
-        for copy in copies:
-            copy.wait()
-
-    groups = query_ref.shape[0] // PG
-
-    def one_group(group, carry):
-        rows = pl.ds(pl.multiple_of(group * PG, PG), PG)
-        offset = pl.multiple_of(offset_ref[step * groups + group], 16)
-        slab = pl.ds(offset, SLAB)
-        bias = visible_bias(offset, span_ref, rows)
-        heads = [of_head(head) for head in range(HEADS)]
-        scores = [dot_rows(query_ref[rows, h], key_ext[slab, h]) for h in heads]
-        d_probs = [dot_rows(d_attended_ref[rows, h], value_ext[slab, h]) for h in heads]
-        row_dot = [
-            jnp.sum(
-                d_attended_ref[rows, h].astype(f32) * attended_ref[rows, h].astype(f32),
-                axis=1, keepdims=True,
-            )
-            for h in heads
-        ]
-        level = [jnp.concatenate([level_ref[rows, h]] * (SLAB // HD), axis=1) for h in heads]
-        probs = [jnp.exp(x * score_scale + bias - y) for x, y in zip(scores, level)]
-        d_scores = [
-            (x * (y - z) * score_scale).astype(bf16) for x, y, z in zip(probs, d_probs, row_dot)
-        ]
-        probs = [x.astype(bf16) for x in probs]
-        d_query = [dot(x, key_ext[slab, h]) for x, h in zip(d_scores, heads)]
-        key_part = [dot_columns(x, query_ref[rows, h]) for x, h in zip(d_scores, heads)]
-        value_part = [dot_columns(x, d_attended_ref[rows, h]) for x, h in zip(probs, heads)]
-        for h, x, y, z in zip(heads, d_query, key_part, value_part):
-            d_query_ref[rows, h] = x.astype(bf16)
-            d_key[slab, h] += y
-            d_value[slab, h] += z
-        return carry
-
-    lax.fori_loop(0, groups, one_group, 0)
-
-    @pl.when(step == pl.num_programs(0) - 1)
-    def _():
-        for which, (total, own_ref) in enumerate(((d_key, d_key_ref), (d_value, d_value_ref))):
-            d_low_ref[which * LOW : (which + 1) * LOW, :] = total[:LOW, :].astype(bf16)
-            own_ref[...] = total[LOW : LOW + own, :].astype(bf16)
-            d_high_ref[which * HIGH : (which + 1) * HIGH, :] = total[LOW + own :, :].astype(bf16)
-
 
 def forward_call(inputs):
-    own, width = inputs[4].shape
-    patches = inputs[6].shape[0]
+    own, width = inputs[5].shape
+    patches = inputs[7].shape[0]
     steps = 4
-    ext_rows = LOW + own + HIGH
-
-    def per_step(columns):
-        return pl.BlockSpec((patches // steps, columns), lambda step, offset: (step, 0))
-
+    ext_rows = LOW + own + HIGH + PAD
+    marks = patches // PG * 8
+    block = pl.BlockSpec((patches // steps, width), lambda step, *scalars: (step, 0))
+    mark_block = pl.BlockSpec((marks // steps, PAIR * PG), lambda step, *scalars: (step, 0))
     return pl.pallas_call(
         forward_kernel,
         out_shape=[
             jax.ShapeDtypeStruct((patches, width), bf16),
-            jax.ShapeDtypeStruct((patches, width), f32),
+            jax.ShapeDtypeStruct((marks, PAIR * PG), f32),
         ],
         grid_spec=pltpu.PrefetchScalarGridSpec(
-            num_scalar_prefetch=1,
+            num_scalar_prefetch=2,
             grid=(steps,),
-            in_specs=[per_step(2)] + [pl.BlockSpec(memory_space=pl.ANY)] * 4 + [per_step(width)],
-            out_specs=[per_step(width)] * 2,
+            in_specs=[mark_block] + [pl.BlockSpec(memory_space=pl.ANY)] * 4 + [block],
+            out_specs=[block, mark_block],
             scratch_shapes=[pltpu.VMEM((ext_rows, width), bf16)] * 2
-            + [pltpu.SemaphoreType.DMA((6,))],
+            + [pltpu.SemaphoreType.DMA((2 * (2 + own // 256),))],
         ),
         compiler_params=pltpu.CompilerParams(vmem_limit_bytes=VMEM_GRANT),
         cost_estimate=pl.CostEstimate(
@@ -195,33 +252,31 @@
 
 
 def backward_call(inputs, after):
-    own, width = inputs[4].shape
-    patches = inputs[6].shape[0]
+    own, width = inputs[5].shape
+    patches = inputs[7].shape[0]
     steps = 4
-    ext_rows = LOW + own + HIGH
-    step_block = pl.BlockSpec((patches // steps, width), lambda step, offset: (step, 0))
+    ext_rows = LOW + own + HIGH + PAD
+    marks = patches // PG * 8
+    block = pl.BlockSpec((patches // steps, width), lambda step, *scalars: (step, 0))
+    mark_block = pl.BlockSpec((marks // steps, PAIR * PG), lambda step, *scalars: (step, 0))
     anywhere = pl.BlockSpec(memory_space=pl.ANY)
-
-    def kept(rows):
-        return pl.BlockSpec(
-            (rows, width), lambda step, offset: (0, 0), pipeline_mode=pl.Buffered(1)
-        )
-
-    rows = (own, own, 2 * LOW, 2 * HIGH)
+    rows = (patches, own, own, 2 * LOW, 2 * HIGH)
     return pl.pallas_call(
         backward_kernel,
-        out_shape=[jax.ShapeDtypeStruct((count, width), bf16) for count in (patches,) + rows],
+        out_shape=[jax.ShapeDtypeStruct((count, width), bf16) for count in rows],
         grid_spec=pltpu.PrefetchScalarGridSpec(
-            num_scalar_prefetch=1,
+            num_scalar_prefetch=2,
             grid=(steps,),
-            in_specs=[pl.BlockSpec((patches // steps, 2), lambda step, offset: (step, 0))]
+            in_specs=[mark_block]
             + [anywhere] * 4
-            + [step_block] * 4
+            + [block, block, mark_block, block]
             + [anywhere],
-            out_specs=[step_block] + [kept(count) for count in rows],
+            out_specs=[block] + [anywhere] * 4,
             scratch_shapes=[pltpu.VMEM((ext_rows, width), bf16)] * 2
-            + [pltpu.SemaphoreType.DMA((6,))]
-            + [pltpu.VMEM((ext_rows, width), f32)] * 2,
+            + [pltpu.SemaphoreType.DMA((2 * (2 + own // 256),))]
+            + [pltpu.VMEM((ext_rows, width), f32)] * 2
+            + [pltpu.VMEM((ext_rows - PAD, width), bf16)] * 2
+            + [pltpu.SemaphoreType.DMA((2 * (2 + own // 256),))],
         ),
         compiler_params=pltpu.CompilerParams(vmem_limit_bytes=VMEM_GRANT),
         cost_estimate=pl.CostEstimate(
@@ -257,36 +312,51 @@
 
 def latent_kernel(
     place_ref, attended_ref, norm_ref, cotangent_ref, weights_ref,
-    mine_ref, other_ref, gain_ref, weight, cotangent, latent, square, mixed, sems,
+    mine_ref, other_ref, gain_ref,
+    weight, cotangent, latent, square, mixed, mine, other, sems,
 ):
     pieces = fetch_weights(place_ref, weights_ref, weight, sems)
-    cotangent_copy = pltpu.make_async_copy(cotangent_ref, cotangent, sems.at[32])
+    rows_each = cotangent.shape[0] // 8
+    cotangent_copies = [
+        pltpu.make_async_copy(
+            cotangent_ref.at[pl.ds(part * rows_each, rows_each)],
+            cotangent.at[pl.ds(part * rows_each, rows_each)],
+            sems.at[32 + part],
+        )
+        for part in range(8)
+    ]
     for slab, copies in enumerate(pieces):
         for copy in copies:
             copy.start()
         if slab == 0:
-            cotangent_copy.start()
+            for copy in cotangent_copies:
+                copy.start()
     square[...] = jnp.zeros_like(square)
     mixed[...] = jnp.zeros_like(mixed)
 
     def columns_of(chunk):
         return pl.ds(pl.multiple_of(chip_block(place_ref, chunk) * LANES, LANES), LANES)
 
-    for slab in range(8):
+    def multiply(slab):
         for copy in pieces[slab]:
             copy.wait()
-        for half in range(2):
-            start = slab * 512 + half * 256
-            block = dot_rows(attended_ref[...], weight[start : start + 256, :])
-            if slab == 0 and half == 0:
-                cotangent_copy.wait()
-            for side in range(2):
-                chunk = slab * 4 + half * 2 + side
-                columns = columns_of(chunk)
-                here = block[:, side * LANES : (side + 1) * LANES]
-                latent[chunk] = here
-                square[...] += here * here
-                mixed[...] += here * (cotangent[:, columns].astype(f32) * norm_ref[:, columns])
+        start = slab * 512
+        latent[slab] = dot_rows(attended_ref[...], weight[start : start + 512, :])
+
+    multiply(0)
+    for copy in cotangent_copies:
+        copy.wait()
+    for slab in range(8):
+        if slab < 7:
+            multiply(slab + 1)
+        columns = [columns_of(slab * 4 + part) for part in range(4)]
+        scaled = [norm_ref[:, c] for c in columns]
+        for start in range(0, square.shape[0], 64):
+            rows = slice(start, start + 64)
+            here = [latent[slab, rows, p * LANES : (p + 1) * LANES] for p in range(4)]
+            arriving = [cotangent[rows, c].astype(f32) * g for c, g in zip(columns, scaled)]
+            square[rows, :] += total_of([x * x for x in here])
+            mixed[rows, :] += total_of([x * y for x, y in zip(here, arriving)])
 
     count = cotangent.shape[1]
     inverse = lax.rsqrt(jnp.sum(square[...], axis=1, keepdims=True) / count + epsilon)
@@ -294,20 +364,39 @@
     square[...] = jnp.broadcast_to(inverse, square.shape)
     mixed[...] = jnp.broadcast_to(back, mixed.shape)
 
-    def finish(chunk, out_ref):
-        columns = columns_of(chunk)
-        here = latent[chunk]
-        arriving = cotangent[:, columns].astype(f32)
-        scaled = arriving * square[...]
-        gain = jnp.sum(scaled * here, axis=0, keepdims=True)
-        spot = pl.ds(pl.multiple_of(chip_block(place_ref, chunk) * 8, 8), 8)
-        gain_ref[spot, :] = jnp.broadcast_to(gain, (8, LANES))
-        d_latent = scaled * norm_ref[:, columns] - here * mixed[...]
-        place = pl.ds(pl.multiple_of(chunk % 16 * LANES, LANES), LANES)
-        out_ref[:, place] = d_latent.astype(bf16)
-
-    lax.fori_loop(0, 16, lambda chunk, carry: (finish(chunk, mine_ref), carry)[1], 0)
-    lax.fori_loop(16, 32, lambda chunk, carry: (finish(chunk, other_ref), carry)[1], 0)
+    def finish(slab, staged, out_ref):
+        chunks = [slab * 4 + part for part in range(4)]
+        columns = [columns_of(chunk) for chunk in chunks]
+        norm = [norm_ref[:, c] for c in columns]
+        gain = [jnp.zeros((8, LANES), f32)] * 4
+        first = slab % 4 * 512
+        for start in range(0, square.shape[0], 64):
+            rows = slice(start, start + 64)
+            scale, back = square[rows, :], mixed[rows, :]
+            for part in range(4):
+                here = latent[slab, rows, part * LANES : (part + 1) * LANES]
+                scaled = cotangent[rows, columns[part]].astype(f32) * scale
+                terms = scaled * here
+                terms = [terms[k : k + 8, :] for k in range(0, 64, 8)]
+                gain[part] += functools.reduce(jnp.add, terms)
+                staged[rows, first + part * LANES : first + (part + 1) * LANES] = (
+                    scaled * norm[part] - here * back
+                ).astype(bf16)
+        for part in range(4):
+            spot = pl.ds(pl.multiple_of(chip_block(place_ref, chunks[part]) * 8, 8), 8)
+            total = jnp.sum(gain[part], axis=0, keepdims=True)
+            gain_ref[spot, :] = jnp.broadcast_to(total, (8, LANES))
+        place = pl.ds(first, 512)
+        copy = pltpu.make_async_copy(
+            staged.at[:, place], out_ref.at[:, place], sems.at[40 + slab]
+        )
+        copy.start()
+        return copy
+
+    copies = [finish(slab, mine, mine_ref) for slab in range(4)]
+    copies += [finish(slab, other, other_ref) for slab in range(4, 8)]
+    for copy in copies:
+        copy.wait()
 
 
 def latent_call(place, attended, norm_gain, cotangent, weights):
@@ -322,14 +411,17 @@
         in_specs=[pl.BlockSpec(memory_space=pltpu.SMEM)]
         + [pl.BlockSpec(memory_space=pltpu.VMEM)] * 2
         + [pl.BlockSpec(memory_space=pl.ANY)] * 2,
-        out_specs=[pl.BlockSpec(memory_space=pltpu.VMEM)] * 3,
+        out_specs=[pl.BlockSpec(memory_space=pl.ANY)] * 2
+        + [pl.BlockSpec(memory_space=pltpu.VMEM)],
         scratch_shapes=[
             pltpu.VMEM(weights.shape, bf16),
             pltpu.VMEM((patches, count), bf16),
-            pltpu.VMEM((32, patches, LANES), f32),
+            pltpu.VMEM((8, patches, count // 8), f32),
             pltpu.VMEM((patches, LANES), f32),
             pltpu.VMEM((patches, LANES), f32),
-            pltpu.SemaphoreType.DMA((33,)),
+            pltpu.VMEM((patches, count // 2), bf16),
+            pltpu.VMEM((patches, count // 2), bf16),
+            pltpu.SemaphoreType.DMA((48,)),
         ],
         compiler_params=pltpu.CompilerParams(vmem_limit_bytes=VMEM_GRANT),
         cost_estimate=pl.CostEstimate(
@@ -339,23 +431,33 @@
     )(place, attended, norm_gain, cotangent, weights)
 
 
-def d_attended_kernel(place_ref, mine_ref, other_ref, weights_ref, out_ref, weight, total, sems):
+def d_attended_kernel(
+    place_ref, mine_ref, other_ref, weights_ref, out_ref, d_latent, weight, total, sems
+):
+    half = mine_ref.shape[1]
     pieces = fetch_weights(place_ref, weights_ref, weight, sems)
-    for copies in pieces:
-        for copy in copies:
+    copies = [
+        pltpu.make_async_copy(
+            (mine_ref, other_ref)[part // 2].at[:, pl.ds(part % 2 * half // 2, half // 2)],
+            d_latent.at[part],
+            sems.at[32 + part],
+        )
+        for part in range(4)
+    ]
+    for part in range(4):
+        copies[part].start()
+        for copy in pieces[2 * part] + pieces[2 * part + 1]:
             copy.start()
-    for slab in range(8):
-        source = mine_ref if slab < 4 else other_ref
-        d_latent = source[:, slab % 4 * 512 : slab % 4 * 512 + 512]
-        for copy in pieces[slab]:
+    for part in range(4):
+        for copy in [copies[part]] + pieces[2 * part] + pieces[2 * part + 1]:
             copy.wait()
-        part = dot(d_latent, weight[slab * 512 : slab * 512 + 512, :])
-        if slab == 0:
-            total[...] = part
-        elif slab < 7:
-            total[...] += part
+        terms = dot(d_latent[part], weight[part * 1024 : part * 1024 + 1024, :])
+        if part == 0:
+            total[...] = terms
+        elif part < 3:
+            total[...] += terms
         else:
-            out_ref[...] = (total[...] + part).astype(bf16)
+            out_ref[...] = (total[...] + terms).astype(bf16)
 
 
 def d_attended_call(place, mine, other, weights):
@@ -364,13 +466,13 @@
         d_attended_kernel,
         out_shape=jax.ShapeDtypeStruct((patches, width), bf16),
         in_specs=[pl.BlockSpec(memory_space=pltpu.SMEM)]
-        + [pl.BlockSpec(memory_space=pltpu.VMEM)] * 2
-        + [pl.BlockSpec(memory_space=pl.ANY)],
+        + [pl.BlockSpec(memory_space=pl.ANY)] * 3,
         out_specs=pl.BlockSpec(memory_space=pltpu.VMEM),
         scratch_shapes=[
+            pltpu.VMEM((4, patches, mine.shape[1] // 2), bf16),
             pltpu.VMEM(weights.shape, bf16),
             pltpu.VMEM((patches, width), f32),
-            pltpu.SemaphoreType.DMA((32,)),
+            pltpu.SemaphoreType.DMA((36,)),
         ],
         compiler_params=pltpu.CompilerParams(vmem_limit_bytes=VMEM_GRANT),
         cost_estimate=pl.CostEstimate(
@@ -383,28 +485,47 @@
 def d_proj_kernel(
     mine_ref, peer_ref, attended_ref, peer_attended_ref, gain_ref, after_ref, *refs
 ):
-    outs, (turned, peer_turned) = refs[:4], refs[4:]
-    turned[...] = attended_ref[...].T
-    peer_turned[...] = peer_attended_ref[...].T
-    width = turned.shape[0]
-    for k in range(RING):
-        distance = (RING - k) % RING
-        columns = slice(distance * 512, distance * 512 + 512)
-        part = dot(turned[...], mine_ref[:, columns])
-        part += dot(peer_turned[...], peer_ref[:, columns])
-        outs[k][:width, :] = part.astype(bf16)
-        outs[k][width:, :] = gain_ref[...]
+    outs, (d_latent, turned, staged, sems) = refs[:4], refs[4:]
+    patches, width = attended_ref.shape
+    arriving, leaving = [], []
+    for k in (1, 2, 3, 0):
+        columns = pl.ds((RING - k) % RING * 512, 512)
+        for side, source in enumerate((mine_ref, peer_ref)):
+            arriving.append(
+                pltpu.make_async_copy(
+                    source.at[:, columns],
+                    d_latent.at[k, pl.ds(side * patches, patches)],
+                    sems.at[2 * k + side],
+                )
+            )
+            arriving[-1].start()
+    turned[:, :patches] = attended_ref[...].T
+    turned[:, patches:] = peer_attended_ref[...].T
+    for step, k in enumerate((1, 2, 3, 0)):
+        arriving[2 * step].wait()
+        arriving[2 * step + 1].wait()
+        staged[k, :width, :] = dot(turned[...], d_latent[k]).astype(bf16)
+        staged[k, width:, :] = gain_ref[...]
+        leaving.append(pltpu.make_async_copy(staged.at[k], outs[k], sems.at[8 + k]))
+        leaving[-1].start()
+    for copy in leaving:
+        copy.wait()
 
 
 def d_proj_call(mine, peer, attended, peer_attended, gain, after):
     patches, width = attended.shape
+    vmem, anywhere = pl.BlockSpec(memory_space=pltpu.VMEM), pl.BlockSpec(memory_space=pl.ANY)
     return pl.pallas_call(
         d_proj_kernel,
         out_shape=[jax.ShapeDtypeStruct((width + 16, 512), bf16)] * 4,
-        in_specs=[pl.BlockSpec(memory_space=pltpu.VMEM)] * 5
-        + [pl.BlockSpec(memory_space=pl.ANY)],
-        out_specs=[pl.BlockSpec(memory_space=pltpu.VMEM)] * 4,
-        scratch_shapes=[pltpu.VMEM((width, patches), bf16)] * 2,
+        in_specs=[anywhere, anywhere, vmem, vmem, vmem, anywhere],
+        out_specs=[anywhere] * 4,
+        scratch_shapes=[
+            pltpu.VMEM((4, 2 * patches, 512), bf16),
+            pltpu.VMEM((width, 2 * patches), bf16),
+            pltpu.VMEM((4, width + 16, 512), bf16),
+            pltpu.SemaphoreType.DMA((12,)),
+        ],
         compiler_params=pltpu.CompilerParams(vmem_limit_bytes=VMEM_GRANT),
         cost_estimate=pl.CostEstimate(
             flops=4 * patches * mine.shape[1] * width, bytes_accessed=12 * MIB, transcendentals=0
@@ -635,10 +756,14 @@
     earlier = (ext_docs[None, :] < last_doc[:, None]) & (position[None, :] < ends[:, None])
     doc_start = jnp.sum(earlier.astype(jnp.int32), axis=1)
     first = jnp.maximum(jnp.maximum(ends - WIN, doc_start), jnp.where(seq_rank == 0, LOW, 0))
-    span = jnp.stack([first, ends], axis=1)
-    offsets = jnp.clip(ends[::PG] - WIN, 0, LOW + own + HIGH - SLAB) // 16 * 16
-
-    common = (offsets, span, low, high, keys, values, queries[0])
+    groups = patches // PG
+    marks = jnp.stack([first, ends]).reshape(2, groups, PG).transpose(1, 0, 2)
+    marks = jnp.pad(jnp.tile(marks, (1, 1, PAIR)), ((0, 0), (0, 6), (0, 0)))
+    marks = marks.reshape(groups * 8, PAIR * PG)
+    offsets = (ends[::PG] - WIN) // 16 * 16
+    short = (ends[PG - 1 :: PG] <= offsets + SHORT).astype(jnp.int32)
+
+    common = (offsets, short, marks, low, high, keys, values, queries[0])
     attended, level = forward_call(common)
     peer_attended = to_peer(attended)
 
@@ -652,10 +777,11 @@
 
     inputs = common + (attended, level, d_attended)
     d_query, d_keys, d_values, d_low, d_high = backward_call(inputs, to_send[0])
+    from_ring, d_query = lax.optimization_barrier((from_ring, d_query))
+    from_ring = ring(first_sum(from_ring), "second")
     from_ring, d_low, d_high = lax.optimization_barrier((from_ring, d_low, d_high))
     from_above = lax.ppermute(d_low, "seq", downward)
     from_below = lax.ppermute(d_high, "seq", upward)
-    from_ring = ring(first_sum(from_ring), "second")
     to_send = second_sum(place, from_ring)
     part, gain = stream_sum(stream_ring(to_send))
     d_proj = finish_call(place, stream_ring([part] * RING))

time: 220 us -> 202 us (0.918)
  Pallas kernels: 101 us -> 87 us
  waiting for transfers between devices: 50.6 us -> 47.1 us
    ppermute x6, waiting for transfers between devices: 15.7 us -> 7.64 us  [ring(): lax.ppermute(values[k], 'seq', along(which, k))]
    pallas_call x1, Pallas kernels: 32.2 us -> 24.6 us  [backward_call(): pl.pallas_call(backward_kernel, out_shape=[jax.ShapeDtypeStruct((count, w...]
    all_gather x1, waiting for transfers between devices: 25.4 us -> 29.5 us  [on_device(): weights = lax.all_gather(proj_weight, 'seq', axis=0, tiled=True)]
    pallas_call x1, Pallas kernels: 18 us -> 13.9 us  [forward_call(): pl.pallas_call(forward_kernel, out_shape=[jax.ShapeDtypeStruct((patches,...]
  transfers between devices with their start and end apart: 22 -> 22, of which waited for: 10 -> 9; matrix products, arithmetic and copies ran while one was open for 6% -> 6% of each run, Pallas kernels for 32% -> 26%
where the time goes in v2:
time: 202 us
  Pallas kernels  87 us (43%)
  waiting for transfers between devices  47.1 us (23%)
  starting transfers between devices  34 us (17%)
  between operations  14.4 us (7%)
  local copies, waits for them, and re-layouts  13.5 us (7%)
  other arithmetic  5.95 us (3%)
    all_gather x1, waiting for transfers between devices, on_device(): weights = lax.all_gather(proj_weight, 'seq', axis=0, tiled=True)  29.5 us
    pallas_call x1, Pallas kernels, backward_call(): pl.pallas_call(backward_kernel, out_shape=[jax.ShapeDtypeStruct((count, w...  24.6 us
    pallas_call x1, Pallas kernels, latent_call(): pl.pallas_call(latent_kernel, out_shape=[jax.ShapeDtypeStruct((patches, c...  17.4 us
    pallas_call x1, Pallas kernels, forward_call(): pl.pallas_call(forward_kernel, out_shape=[jax.ShapeDtypeStruct((patches,...  13.9 us
    ppermute x6, starting transfers between devices, ring(): lax.ppermute(values[k], 'seq', along(which, k))  9.66 us
    ppermute x6, starting transfers between devices, stream_ring(): lax.ppermute(values[k], 'dp', [(i, (i + k) % count) for i in range(count)])  9.34 us
    ppermute x6, waiting for transfers between devices, stream_ring(): lax.ppermute(values[k], 'dp', [(i, (i + k) % count) for i in range(count)])  9.25 us
    pallas_call x1, Pallas kernels, d_proj_call(): pl.pallas_call(d_proj_kernel, out_shape=[jax.ShapeDtypeStruct((width + 16...  8.83 us
  transfers between devices with their start and end apart: 22, of which 9 were waited for; matrix products, arithmetic and copies ran while one was open for 6% of the time, Pallas kernels for 26%

profile of v2, /device:TPU:0, one launch (start us, length us, event | category | flops | bytes accessed | tf_op | source)
XLA Modules:
  0.0 202.0 jit_solution(14615484926845288432)
XLA Ops:
  7.2 0.7 all-gather.2.cloned.1.call-update
  7.9 0.7 slice.49
  8.6 1.3 collective-permute-start.1
  9.9 0.7 slice_reduce_fusion
  10.6 3.0 %collective-permute-start = (s32[384]{0:T(512)S(1)}, s32[384]{0:T(512)S(1)}, u32[]{:S(2)}, u32[]{:S(2)}) collective-permute-start(s32[384]{0:T(512)S(1)} %slice_reduce_fusion), channel_id=1, source_target_pairs={{0,1},{1,2},{2,3},{3,4},{4,5},{5,6},{6,7},{7,8},{8,9},{9,10},{10,1... | collective-permute-start | bytes 4616 | tf_op jit(solution)/shard_map/ppermute | solution.py:743
  13.6 1.3 slice_bitcast_fusion.2
  14.9 1.0 pad_maximum_fusion.1
  15.9 1.4 collective-permute-start.3
  17.3 1.5 slice_bitcast_fusion
  19.0 3.8 %collective-permute-start.2 = (bf16[768,1024]{1,0:T(8,128)(2,1)S(1)}, bf16[768,1024]{1,0:T(8,128)(2,1)S(1)}, u32[]{:S(2)}, u32[]{:S(2)}) collective-permute-start(bf16[768,1024]{1,0:T(8,128)(2,1)S(1)} %pad_maximum_fusion), channel_id=1, source_target_pairs={{0,1},{1,2},{2,3},{3,4},{4,5},{5,6},{6,7},{7,8},{8,9},{9,10},{10,1... | collective-permute-start | bytes 4718600 | tf_op jit(solution)/shard_map/ppermute | solution.py:747
  24.4 0.9 select_reduce_fusion
  25.2 1.3 convert_reduce_fusion
  27.1 0.7 maximum_reduce_fusion
  28.7 1.2 copy-done
  29.8 13.9 %attention_forward.1 = (bf16[512,1024]{1,0:T(8,128)(2,1)}, f32[64,128]{1,0:T(8,128)}) custom-call(s32[8]{0:T(128)} %get-tuple-element.82.offset_ref, s32[8]{0:T(128)} %get-tuple-element.81.short_ref, s32[64,128]{1,0:T(8,128)} %pad_bitcast_fusion.span_ref, bf16[768,1024]{1,0:T(8,128)(2,1)} %copy-done, bf16[512,1024]{1,0:T(8,128)(2,1)} %collective-permute-done.3.high_ref, ...), custom_call_target="tpu_custom_call" | custom-call | flops 1241513984 | bytes 20971520 | tf_op jit(solution)/shard_map/attention_forward/pallas_call | solution.py:230
  43.8 29.5 %all-gather.2.cloned.1.call-done.weights_ref = bf16[4096,1024]{1,0:T(8,128)(2,1)} async-done(((bf16[128,1024]{1,0:T(8,128)(2,1)}), bf16[4096,1024]{1,0:T(8,128)(2,1)}) %all-gather.2.cloned.1.call-update) | async-done | bytes 8388624 | tf_op jit(solution)/shard_map/all_gather | solution.py:748
  73.3 17.4 %latent.1 = (bf16[512,2048]{1,0:T(8,128)(2,1)}, bf16[512,2048]{1,0:T(8,128)(2,1)}, f32[256,128]{1,0:T(8,128)}) custom-call(s32[4]{0:T(128)} %pad_add_fusion.1.place_ref, bf16[512,1024]{1,0:T(8,128)(2,1)} %get-tuple-element.42.attended_ref, f32[1,4096]{1,0:T(1,128)} %bitcast.56, bf16[512,4096]{1,0:T(8,128)(2,1)} %bitcast.55, ...), custom_call_target="tpu_custom_call" | custom-call | flops 4294967296 | bytes 18874368 | tf_op jit(solution)/shard_map/latent/pallas_call | solution.py:404
  91.3 0.9 slice.60
  92.6 8.5 %d_attended.1.after_ref.d_attended_ref = bf16[512,1024]{1,0:T(8,128)(2,1)} custom-call(s32[4]{0:T(128)} %pad_add_fusion.1.place_ref, bf16[512,2048]{1,0:T(8,128)(2,1)} %get-tuple-element.43.mine_ref, bf16[512,2048]{1,0:T(8,128)(2,1)} %get-tuple-element.44.other_ref, bf16[4096,1024]{1,0:T(8,128)(2,1)} %all-gather.2.cloned.1.call-done.weights_ref), custom_call_target="tpu_custom_call" | custom-call | flops 4294967296 | bytes 14680064 | tf_op jit(solution)/shard_map/d_attended/pallas_call | solution.py:465
  101.7 1.3 copy-done.17
  103.1 8.8 %d_proj.1 = (bf16[1040,512]{1,0:T(8,128)(2,1)}, bf16[1040,512]{1,0:T(8,128)(2,1)}, bf16[1040,512]{1,0:T(8,128)(2,1)}, bf16[1040,512]{1,0:T(8,128)(2,1)}) custom-call(bf16[512,2048]{1,0:T(8,128)(2,1)} %get-tuple-element.43.mine_ref, bf16[512,2048]{1,0:T(8,128)(2,1)} %copy-done.17, bf16[512,1024]{1,0:T(8,128)(2,1)} %get-tuple-element.42.attended_ref, ...), custom_call_target="tpu_custom_call" | custom-call | flops 4294967296 | bytes 12582912 | tf_op jit(solution)/shard_map/d_proj/pallas_call | solution.py:518
  111.9 1.2 collective-permute-start.7
  113.1 2.9 %collective-permute-start.8 = (bf16[1040,512]{1,0:T(8,128)(2,1)}, bf16[1040,512]{1,0:T(8,128)(2,1)S(1)}, u32[]{:S(2)}, u32[]{:S(2)}) collective-permute-start(bf16[1040,512]{1,0:T(8,128)(2,1)} %get-tuple-element.48), channel_id=1, source_target_pairs={{0,16},{1,5},{2,18},{3,7},{4,20},{5,1},{6,22},{7,3},{8,24},{9,13},... | collective-permute-start | bytes 3194888 | tf_op jit(solution)/shard_map/ppermute | solution.py:607
  116.0 1.4 collective-permute-start.9
  117.3 24.6 %attention_backward.1 = (bf16[512,1024]{1,0:T(8,128)(2,1)}, bf16[2048,1024]{1,0:T(8,128)(2,1)}, bf16[2048,1024]{1,0:T(8,128)(2,1)}, bf16[768,1024]{1,0:T(8,128)(2,1)}, bf16[512,1024]{1,0:T(8,128)(2,1)}) custom-call(s32[8]{0:T(128)} %get-tuple-element.82.offset_ref, s32[8]{0:T(128)} %get-tuple-element.81.short_ref, s32[64,128]{1,0:T(8,128)} %pad_bitcast_fusion.span_ref, ...), custom_call_target="tpu_custom_call" | custom-call | flops 4345298944 | bytes 41943040 | tf_op jit(solution)/shard_map/attention_backward/pallas_call | solution.py:264
  142.0 1.0 copy-done.2
  143.6 3.4 %first_sum.1 = (bf16[1088,128]{1,0:T(8,128)(2,1)}, bf16[1088,128]{1,0:T(8,128)(2,1)}, bf16[1088,128]{1,0:T(8,128)(2,1)}, bf16[1088,128]{1,0:T(8,128)(2,1)}) custom-call(bf16[1040,512]{1,0:T(8,128)(2,1)} %get-tuple-element.55.after_ref.refs_0_, bf16[1040,512]{1,0:T(8,128)(2,1)} %copy-done.2, bf16[1040,512]{1,0:T(8,128)(2,1)} %copy-done.3, ...), custom_call_target="tpu_custom_call" | custom-call | tf_op jit(solution)/shard_map/first_sum/pallas_call | solution.py:644
  147.2 2.7 %collective-permute-start.11 = (bf16[1088,128]{1,0:T(8,128)(2,1)}, bf16[1088,128]{1,0:T(8,128)(2,1)S(1)}, u32[]{:S(2)}, u32[]{:S(2)}) collective-permute-start(bf16[1088,128]{1,0:T(8,128)(2,1)} %get-tuple-element.61), channel_id=1, source_target_pairs={{0,4},{1,17},{2,6},{3,19},{4,0},{5,21},{6,2},{7,23},{8,12},{9,25},... | collective-permute-start | bytes 835592 | tf_op jit(solution)/shard_map/ppermute | solution.py:607
  149.9 1.4 collective-permute-start.12
  151.3 6.7 %collective-permute-done.10.refs_1_ = bf16[1088,128]{1,0:T(8,128)(2,1)S(1)} collective-permute-done((bf16[1088,128]{1,0:T(8,128)(2,1)}, bf16[1088,128]{1,0:T(8,128)(2,1)S(1)}, u32[]{:S(2)}, u32[]{:S(2)}) %collective-permute-start.10) | collective-permute-done | bytes 278560 | tf_op jit(solution)/shard_map/ppermute | solution.py:607
  158.0 0.9 collective-permute-done.12.refs_3_
  158.9 1.3 collective-permute-start.14
  160.2 3.1 %collective-permute-start.13 = (bf16[512,1024]{1,0:T(8,128)(2,1)}, bf16[512,1024]{1,0:T(8,128)(2,1)S(1)}, u32[]{:S(2)}, u32[]{:S(2)}) collective-permute-start(bf16[512,1024]{1,0:T(8,128)(2,1)} %get-tuple-element.65), channel_id=1, source_target_pairs={{0,1},{1,2},{2,3},{3,4},{4,5},{5,6},{6,7},{7,8},{8,9},{9,10},{10,1... | collective-permute-start | bytes 3145736 | tf_op jit(solution)/shard_map/ppermute | solution.py:784
  163.4 2.2 %second_sum.1 = (bf16[320,128]{1,0:T(8,128)(2,1)}, bf16[320,128]{1,0:T(8,128)(2,1)}, bf16[320,128]{1,0:T(8,128)(2,1)}, bf16[320,128]{1,0:T(8,128)(2,1)}) custom-call(s32[4]{0:T(128)} %pad_add_fusion.1.place_ref, bf16[1088,128]{1,0:T(8,128)(2,1)} %get-tuple-element.69.refs_0_, bf16[1088,128]{1,0:T(8,128)(2,1)} %copy-done.6, bf16[1088,128]{1,0:T(8,128)(2,1)} %copy-done.7, ...), custom_call_target="tpu_custom_call" | custom-call | tf_op jit(solution)/shard_map/second_sum/pallas_call | solution.py:669
  165.6 1.5 collective-permute-start.15
  167.1 2.7 %collective-permute-start.16 = (bf16[320,128]{1,0:T(8,128)(2,1)}, bf16[320,128]{1,0:T(8,128)(2,1)S(1)}, u32[]{:S(2)}, u32[]{:S(2)}) collective-permute-start(bf16[320,128]{1,0:T(8,128)(2,1)} %get-tuple-element.75), channel_id=1, source_target_pairs={{0,64},{32,96},{64,0},{96,32},{1,65},{33,97},{65,1},{97,33},{2,66}... | collective-permute-start | bytes 245768 | tf_op jit(solution)/shard_map/ppermute | solution.py:726
  169.8 1.4 collective-permute-start.17
  171.2 1.1 collective-permute-done.15.refs_1_
  172.3 2.5 %collective-permute-done.16.refs_2_ = bf16[320,128]{1,0:T(8,128)(2,1)S(1)} collective-permute-done((bf16[320,128]{1,0:T(8,128)(2,1)}, bf16[320,128]{1,0:T(8,128)(2,1)S(1)}, u32[]{:S(2)}, u32[]{:S(2)}) %collective-permute-start.16) | collective-permute-done | bytes 81952 | tf_op jit(solution)/shard_map/ppermute | solution.py:726
  175.6 1.7 stream_sum.1
  177.3 2.4 %collective-permute-start.20 = (bf16[256,128]{1,0:T(8,128)(2,1)}, bf16[256,128]{1,0:T(8,128)(2,1)S(1)}, u32[]{:S(2)}, u32[]{:S(2)}) collective-permute-start(bf16[256,128]{1,0:T(8,128)(2,1)} %get-tuple-element.77.refs_0_), channel_id=1, source_target_pairs={{0,96},{32,0},{64,32},{96,64},{1,97},{33,1},{65,33},{97,65},{2,98}... | collective-permute-start | bytes 196616 | tf_op jit(solution)/shard_map/ppermute | solution.py:726
  179.7 1.1 collective-permute-start.19
  181.0 1.5 collective-permute-done.20.refs_3_
  182.4 3.2 %collective-permute-done.19.refs_2_ = bf16[256,128]{1,0:T(8,128)(2,1)S(1)} collective-permute-done((bf16[256,128]{1,0:T(8,128)(2,1)}, bf16[256,128]{1,0:T(8,128)(2,1)S(1)}, u32[]{:S(2)}, u32[]{:S(2)}) %collective-permute-start.19) | collective-permute-done | bytes 65568 | tf_op jit(solution)/shard_map/ppermute | solution.py:726
  185.7 0.8 collective-permute-done.18.refs_1_
  187.1 1.9 d_proj_rows.1
  189.0 1.0 copy-done.5
  190.5 4.6 %rims.1 = (bf16[2048,1024]{1,0:T(8,128)(2,1)}, bf16[2048,1024]{1,0:T(8,128)(2,1)}) custom-call(bf16[2048,1024]{1,0:T(8,128)(2,1)} %get-tuple-element.53.key_in, bf16[2048,1024]{1,0:T(8,128)(2,1)} %get-tuple-element.54.value_in, bf16[512,1024]{1,0:T(8,128)(2,1)} %copy-done.5, bf16[768,1024]{1,0:T(8,128)(2,1)} %copy-done.1), custom_call_target="tpu_custom_call", output_to_operand_aliasing={{0}: (0, {}), {1}: (1, {})} | custom-call | tf_op jit(solution)/shard_map/rims/pallas_call | solution.py:576
  (72 shorter events, 7.6 us)
Async XLA Ops:
  7.2 66.1 %all-gather.2.cloned.1.call-start = ((), (), s32[]{:S(2)}) async-start(), calls=%async_computation | async-start | bytes 8650752 | tf_op jit(solution)/shard_map/all_gather | solution.py:748
  8.6 15.7 %collective-permute-start.1 = (s32[256]{0:T(256)S(1)}, s32[256]{0:T(256)S(1)}, u32[]{:S(2)}, u32[]{:S(2)}) collective-permute-start(s32[256]{0:T(256)S(1)} %bitcast.54), channel_id=1, source_target_pairs={{1,0},{2,1},{3,2},{4,3},{5,4},{6,5},{7,6},{8,7},{9,8},{10,9},{11,1... | collective-permute-start | bytes 3080 | tf_op jit(solution)/shard_map/ppermute | solution.py:744
  10.6 13.8 %collective-permute-start = (s32[384]{0:T(512)S(1)}, s32[384]{0:T(512)S(1)}, u32[]{:S(2)}, u32[]{:S(2)}) collective-permute-start(s32[384]{0:T(512)S(1)} %slice_reduce_fusion), channel_id=1, source_target_pairs={{0,1},{1,2},{2,3},{3,4},{4,5},{5,6},{6,7},{7,8},{8,9},{9,10},{10,1... | collective-permute-start | bytes 4616 | tf_op jit(solution)/shard_map/ppermute | solution.py:743
  15.9 6.9 %copy-start.16 = (s32[1,512]{1,0:T(1,128)S(1)}, s32[1,512]{1,0:T(1,128)}, u32[]{:S(2)}) copy-start(s32[1,512]{1,0:T(1,128)} %param.12) | copy-start | bytes 6148
  15.9 8.4 %copy-start.15 = (s32[1,2048]{1,0:T(1,128)S(1)}, s32[1,2048]{1,0:T(1,128)}, u32[]{:S(2)}) copy-start(s32[1,2048]{1,0:T(1,128)} %param.10) | copy-start | bytes 24580
  15.9 12.7 %collective-permute-start.3 = (bf16[512,1024]{1,0:T(8,128)(2,1)}, bf16[512,1024]{1,0:T(8,128)(2,1)}, u32[]{:S(2)}, u32[]{:S(2)}) collective-permute-start(bf16[512,1024]{1,0:T(8,128)(2,1)} %pad_maximum_fusion.1), channel_id=1, source_target_pairs={{1,0},{2,1},{3,2},{4,3},{5,4},{6,5},{7,6},{8,7},{9,8},{10,9},{11,1... | collective-permute-start | bytes 3145736 | tf_op jit(solution)/shard_map/ppermute | solution.py:747
  19.0 9.7 %collective-permute-start.2 = (bf16[768,1024]{1,0:T(8,128)(2,1)S(1)}, bf16[768,1024]{1,0:T(8,128)(2,1)S(1)}, u32[]{:S(2)}, u32[]{:S(2)}) collective-permute-start(bf16[768,1024]{1,0:T(8,128)(2,1)S(1)} %pad_maximum_fusion), channel_id=1, source_target_pairs={{0,1},{1,2},{2,3},{3,4},{4,5},{5,6},{6,7},{7,8},{8,9},{9,10},{10,1... | collective-permute-start | bytes 4718600 | tf_op jit(solution)/shard_map/ppermute | solution.py:747
  28.7 1.2 copy-start
  73.3 17.7 %copy-start.18 = (bf16[512,1024]{1,0:T(8,128)(2,1)S(1)}, bf16[512,1024]{1,0:T(8,128)(2,1)}, u32[]{:S(2)}) copy-start(bf16[512,1024]{1,0:T(8,128)(2,1)} %get-tuple-element.42.attended_ref) | copy-start | bytes 3145732
  90.6 11.1 %collective-permute-start.4 = (bf16[512,2048]{1,0:T(8,128)(2,1)}, bf16[512,2048]{1,0:T(8,128)(2,1)S(1)}, u32[]{:S(2)}, u32[]{:S(2)}) collective-permute-start(bf16[512,2048]{1,0:T(8,128)(2,1)} %get-tuple-element.44.other_ref), channel_id=1, source_target_pairs={{0,1},{1,0},{2,3},{3,2},{4,5},{5,4},{6,7},{7,6},{8,9},{9,8},{10,11... | collective-permute-start | bytes 6291464 | tf_op jit(solution)/shard_map/ppermute | solution.py:602
  91.0 10.7 %collective-permute-start.5 = (bf16[512,1024]{1,0:T(8,128)(2,1)S(1)}, bf16[512,1024]{1,0:T(8,128)(2,1)}, u32[]{:S(2)}, u32[]{:S(2)}) collective-permute-start(bf16[512,1024]{1,0:T(8,128)(2,1)S(1)} %copy-done.18), channel_id=1, source_target_pairs={{0,1},{1,0},{2,3},{3,2},{4,5},{5,4},{6,7},{7,6},{8,9},{9,8},{10,11... | collective-permute-start | bytes 3145736 | tf_op jit(solution)/shard_map/ppermute | solution.py:602
  92.2 8.9 %collective-permute-start.6 = (f32[8,512]{1,0:T(8,128)S(1)}, f32[8,512]{1,0:T(8,128)S(1)}, u32[]{:S(2)}, u32[]{:S(2)}) collective-permute-start(f32[8,512]{1,0:T(8,128)S(1)} %bitcast.45), channel_id=1, source_target_pairs={{0,1},{1,0},{2,3},{3,2},{4,5},{5,4},{6,7},{7,6},{8,9},{9,8},{10,11... | collective-permute-start | bytes 49160 | tf_op jit(solution)/shard_map/ppermute | solution.py:602
  101.7 1.3 copy-start.17
  111.9 30.0 %collective-permute-start.7 = (bf16[1040,512]{1,0:T(8,128)(2,1)}, bf16[1040,512]{1,0:T(8,128)(2,1)S(1)}, u32[]{:S(2)}, u32[]{:S(2)}) collective-permute-start(bf16[1040,512]{1,0:T(8,128)(2,1)} %get-tuple-element.47), channel_id=1, source_target_pairs={{0,8},{1,3},{2,10},{3,5},{4,12},{5,7},{6,14},{7,1},{8,16},{9,11},{... | collective-permute-start | bytes 3194888 | tf_op jit(solution)/shard_map/ppermute | solution.py:607
  113.1 28.8 %collective-permute-start.8 = (bf16[1040,512]{1,0:T(8,128)(2,1)}, bf16[1040,512]{1,0:T(8,128)(2,1)S(1)}, u32[]{:S(2)}, u32[]{:S(2)}) collective-permute-start(bf16[1040,512]{1,0:T(8,128)(2,1)} %get-tuple-element.48), channel_id=1, source_target_pairs={{0,16},{1,5},{2,18},{3,7},{4,20},{5,1},{6,22},{7,3},{8,24},{9,13},... | collective-permute-start | bytes 3194888 | tf_op jit(solution)/shard_map/ppermute | solution.py:607
  116.0 26.0 %collective-permute-start.9 = (bf16[1040,512]{1,0:T(8,128)(2,1)}, bf16[1040,512]{1,0:T(8,128)(2,1)S(1)}, u32[]{:S(2)}, u32[]{:S(2)}) collective-permute-start(bf16[1040,512]{1,0:T(8,128)(2,1)} %get-tuple-element.49), channel_id=1, source_target_pairs={{0,24},{1,7},{2,26},{3,1},{4,28},{5,3},{6,30},{7,5},{8,0},{9,15},{... | collective-permute-start | bytes 3194888 | tf_op jit(solution)/shard_map/ppermute | solution.py:607
  141.9 1.0 copy-start.2
  141.9 1.3 copy-start.3
  142.0 1.7 copy-start.4
  147.1 11.0 %collective-permute-start.10 = (bf16[1088,128]{1,0:T(8,128)(2,1)}, bf16[1088,128]{1,0:T(8,128)(2,1)S(1)}, u32[]{:S(2)}, u32[]{:S(2)}) collective-permute-start(bf16[1088,128]{1,0:T(8,128)(2,1)} %get-tuple-element.60), channel_id=1, source_target_pairs={{0,2},{1,9},{2,4},{3,11},{4,6},{5,13},{6,0},{7,15},{8,10},{9,17},{... | collective-permute-start | bytes 835592 | tf_op jit(solution)/shard_map/ppermute | solution.py:607
  147.2 10.8 %collective-permute-start.11 = (bf16[1088,128]{1,0:T(8,128)(2,1)}, bf16[1088,128]{1,0:T(8,128)(2,1)S(1)}, u32[]{:S(2)}, u32[]{:S(2)}) collective-permute-start(bf16[1088,128]{1,0:T(8,128)(2,1)} %get-tuple-element.61), channel_id=1, source_target_pairs={{0,4},{1,17},{2,6},{3,19},{4,0},{5,21},{6,2},{7,23},{8,12},{9,25},... | collective-permute-start | bytes 835592 | tf_op jit(solution)/shard_map/ppermute | solution.py:607
  149.9 9.0 %collective-permute-start.12 = (bf16[1088,128]{1,0:T(8,128)(2,1)}, bf16[1088,128]{1,0:T(8,128)(2,1)S(1)}, u32[]{:S(2)}, u32[]{:S(2)}) collective-permute-start(bf16[1088,128]{1,0:T(8,128)(2,1)} %get-tuple-element.62), channel_id=1, source_target_pairs={{0,6},{1,25},{2,0},{3,27},{4,2},{5,29},{6,4},{7,31},{8,14},{9,1},{... | collective-permute-start | bytes 835592 | tf_op jit(solution)/shard_map/ppermute | solution.py:607
  158.0 5.3 %copy-start.6 = (bf16[1088,128]{1,0:T(8,128)(2,1)}, bf16[1088,128]{1,0:T(8,128)(2,1)S(1)}, u32[]{:S(2)}) copy-start(bf16[1088,128]{1,0:T(8,128)(2,1)S(1)} %collective-permute-done.10.refs_1_) | copy-start | bytes 835588
  158.0 5.3 %copy-start.7 = (bf16[1088,128]{1,0:T(8,128)(2,1)}, bf16[1088,128]{1,0:T(8,128)(2,1)S(1)}, u32[]{:S(2)}) copy-start(bf16[1088,128]{1,0:T(8,128)(2,1)S(1)} %collective-permute-done.11.refs_2_) | copy-start | bytes 835588
  158.9 4.4 %copy-start.8 = (bf16[1088,128]{1,0:T(8,128)(2,1)}, bf16[1088,128]{1,0:T(8,128)(2,1)S(1)}, u32[]{:S(2)}) copy-start(bf16[1088,128]{1,0:T(8,128)(2,1)S(1)} %collective-permute-done.12.refs_3_) | copy-start | bytes 835588
  158.9 30.1 %collective-permute-start.14 = (bf16[768,1024]{1,0:T(8,128)(2,1)}, bf16[768,1024]{1,0:T(8,128)(2,1)S(1)}, u32[]{:S(2)}, u32[]{:S(2)}) collective-permute-start(bf16[768,1024]{1,0:T(8,128)(2,1)} %get-tuple-element.66), channel_id=1, source_target_pairs={{1,0},{2,1},{3,2},{4,3},{5,4},{6,5},{7,6},{8,7},{9,8},{10,9},{11,1... | collective-permute-start | bytes 4718600 | tf_op jit(solution)/shard_map/ppermute | solution.py:783
  160.2 28.8 %collective-permute-start.13 = (bf16[512,1024]{1,0:T(8,128)(2,1)}, bf16[512,1024]{1,0:T(8,128)(2,1)S(1)}, u32[]{:S(2)}, u32[]{:S(2)}) collective-permute-start(bf16[512,1024]{1,0:T(8,128)(2,1)} %get-tuple-element.65), channel_id=1, source_target_pairs={{0,1},{1,2},{2,3},{3,4},{4,5},{5,6},{6,7},{7,8},{8,9},{9,10},{10,1... | collective-permute-start | bytes 3145736 | tf_op jit(solution)/shard_map/ppermute | solution.py:784
  165.6 6.7 %collective-permute-start.15 = (bf16[320,128]{1,0:T(8,128)(2,1)}, bf16[320,128]{1,0:T(8,128)(2,1)S(1)}, u32[]{:S(2)}, u32[]{:S(2)}) collective-permute-start(bf16[320,128]{1,0:T(8,128)(2,1)} %get-tuple-element.74), channel_id=1, source_target_pairs={{0,32},{32,64},{64,96},{96,0},{1,33},{33,65},{65,97},{97,1},{2,34}... | collective-permute-start | bytes 245768 | tf_op jit(solution)/shard_map/ppermute | solution.py:726
  167.1 7.8 %collective-permute-start.16 = (bf16[320,128]{1,0:T(8,128)(2,1)}, bf16[320,128]{1,0:T(8,128)(2,1)S(1)}, u32[]{:S(2)}, u32[]{:S(2)}) collective-permute-start(bf16[320,128]{1,0:T(8,128)(2,1)} %get-tuple-element.75), channel_id=1, source_target_pairs={{0,64},{32,96},{64,0},{96,32},{1,65},{33,97},{65,1},{97,33},{2,66}... | collective-permute-start | bytes 245768 | tf_op jit(solution)/shard_map/ppermute | solution.py:726
  169.8 5.2 %collective-permute-start.17 = (bf16[320,128]{1,0:T(8,128)(2,1)}, bf16[320,128]{1,0:T(8,128)(2,1)S(1)}, u32[]{:S(2)}, u32[]{:S(2)}) collective-permute-start(bf16[320,128]{1,0:T(8,128)(2,1)} %get-tuple-element.76), channel_id=1, source_target_pairs={{0,96},{32,0},{64,32},{96,64},{1,97},{33,1},{65,33},{97,65},{2,98}... | collective-permute-start | bytes 245768 | tf_op jit(solution)/shard_map/ppermute | solution.py:726
  172.3 2.7 %copy-start.9 = (bf16[320,128]{1,0:T(8,128)(2,1)}, bf16[320,128]{1,0:T(8,128)(2,1)S(1)}, u32[]{:S(2)}) copy-start(bf16[320,128]{1,0:T(8,128)(2,1)S(1)} %collective-permute-done.15.refs_1_) | copy-start | bytes 245764
  174.8 0.6 copy-start.10
  175.0 0.6 copy-start.11
  177.3 5.2 %collective-permute-start.20 = (bf16[256,128]{1,0:T(8,128)(2,1)}, bf16[256,128]{1,0:T(8,128)(2,1)S(1)}, u32[]{:S(2)}, u32[]{:S(2)}) collective-permute-start(bf16[256,128]{1,0:T(8,128)(2,1)} %get-tuple-element.77.refs_0_), channel_id=1, source_target_pairs={{0,96},{32,0},{64,32},{96,64},{1,97},{33,1},{65,33},{97,65},{2,98}... | collective-permute-start | bytes 196616 | tf_op jit(solution)/shard_map/ppermute | solution.py:726
  179.7 6.0 %collective-permute-start.19 = (bf16[256,128]{1,0:T(8,128)(2,1)}, bf16[256,128]{1,0:T(8,128)(2,1)S(1)}, u32[]{:S(2)}, u32[]{:S(2)}) collective-permute-start(bf16[256,128]{1,0:T(8,128)(2,1)} %get-tuple-element.77.refs_0_), channel_id=1, source_target_pairs={{0,64},{32,96},{64,0},{96,32},{1,65},{33,97},{65,1},{97,33},{2,66}... | collective-permute-start | bytes 196616 | tf_op jit(solution)/shard_map/ppermute | solution.py:726
  180.8 5.7 %collective-permute-start.18 = (bf16[256,128]{1,0:T(8,128)(2,1)}, bf16[256,128]{1,0:T(8,128)(2,1)S(1)}, u32[]{:S(2)}, u32[]{:S(2)}) collective-permute-start(bf16[256,128]{1,0:T(8,128)(2,1)} %get-tuple-element.77.refs_0_), channel_id=1, source_target_pairs={{0,32},{32,64},{64,96},{96,0},{1,33},{33,65},{65,97},{97,1},{2,34}... | collective-permute-start | bytes 196616 | tf_op jit(solution)/shard_map/ppermute | solution.py:726
  182.4 4.1 %copy-start.12 = (bf16[256,128]{1,0:T(8,128)(2,1)}, bf16[256,128]{1,0:T(8,128)(2,1)S(1)}, u32[]{:S(2)}) copy-start(bf16[256,128]{1,0:T(8,128)(2,1)S(1)} %collective-permute-done.20.refs_3_) | copy-start | bytes 196612
  185.7 0.9 copy-start.13
  186.5 0.6 copy-start.14
  189.0 1.0 copy-start.5
  189.0 1.5 copy-start.1
Sparse Core Ops, SparseCore 0:
  10.3 62.9 all-gather.1

commit v3 on v2

--- a/solution.py
+++ b/solution.py
@@ -485,9 +485,12 @@
 def d_proj_kernel(
     mine_ref, peer_ref, attended_ref, peer_attended_ref, gain_ref, after_ref, *refs
 ):
-    outs, (d_latent, turned, staged, sems) = refs[:4], refs[4:]
+    outs, (d_latent, rows, turned, staged, sems) = refs[:4], refs[4:]
     patches, width = attended_ref.shape
-    arriving, leaving = [], []
+    arriving, leaving, sides = [], [], []
+    for side, source in enumerate((attended_ref, peer_attended_ref)):
+        sides.append(pltpu.make_async_copy(source, rows.at[side], sems.at[12 + side]))
+        sides[-1].start()
     for k in (1, 2, 3, 0):
         columns = pl.ds((RING - k) % RING * 512, 512)
         for side, source in enumerate((mine_ref, peer_ref)):
@@ -499,8 +502,9 @@
                 )
             )
             arriving[-1].start()
-    turned[:, :patches] = attended_ref[...].T
-    turned[:, patches:] = peer_attended_ref[...].T
+    for side in range(2):
+        sides[side].wait()
+        turned[:, side * patches : (side + 1) * patches] = rows[side].T
     for step, k in enumerate((1, 2, 3, 0)):
         arriving[2 * step].wait()
         arriving[2 * step + 1].wait()
@@ -518,13 +522,14 @@
     return pl.pallas_call(
         d_proj_kernel,
         out_shape=[jax.ShapeDtypeStruct((width + 16, 512), bf16)] * 4,
-        in_specs=[anywhere, anywhere, vmem, vmem, vmem, anywhere],
+        in_specs=[anywhere] * 4 + [vmem, anywhere],
         out_specs=[anywhere] * 4,
         scratch_shapes=[
             pltpu.VMEM((4, 2 * patches, 512), bf16),
+            pltpu.VMEM((2, patches, width), bf16),
             pltpu.VMEM((width, 2 * patches), bf16),
             pltpu.VMEM((4, width + 16, 512), bf16),
-            pltpu.SemaphoreType.DMA((12,)),
+            pltpu.SemaphoreType.DMA((14,)),
         ],
         compiler_params=pltpu.CompilerParams(vmem_limit_bytes=VMEM_GRANT),
         cost_estimate=pl.CostEstimate(
@@ -701,23 +706,25 @@
 
 
 def finish_kernel(place_ref, *refs):
-    parts, out_ref = refs[:4], refs[4]
+    parts, out_ref = refs[:4], refs[5]
     quarter = parts[0].shape[0]
     for k in range(RING):
         start = pl.multiple_of((place_ref[3] - k + RING) % RING * quarter, quarter)
         out_ref[:, pl.ds(start, quarter)] = parts[k][...].astype(f32).T
 
 
-def finish_call(place, parts):
+def finish_call(place, parts, after):
     quarter = parts[0].shape[0]
     vmem = pl.BlockSpec(memory_space=pltpu.VMEM)
     return pl.pallas_call(
         finish_kernel,
         out_shape=jax.ShapeDtypeStruct((LANES, RING * quarter), f32),
-        in_specs=[pl.BlockSpec(memory_space=pltpu.SMEM)] + [vmem] * 4,
+        in_specs=[pl.BlockSpec(memory_space=pltpu.SMEM)]
+        + [vmem] * 4
+        + [pl.BlockSpec(memory_space=pl.ANY)],
         out_specs=vmem,
         name="d_proj_rows",
-    )(place, *parts)
+    )(place, *parts, after)
 
 
 def stream_ring(values):
@@ -779,15 +786,14 @@
     d_query, d_keys, d_values, d_low, d_high = backward_call(inputs, to_send[0])
     from_ring, d_query = lax.optimization_barrier((from_ring, d_query))
     from_ring = ring(first_sum(from_ring), "second")
-    from_ring, d_low, d_high = lax.optimization_barrier((from_ring, d_low, d_high))
+    from_ring[1], d_low, d_high = lax.optimization_barrier((from_ring[1], d_low, d_high))
     from_above = lax.ppermute(d_low, "seq", downward)
     from_below = lax.ppermute(d_high, "seq", upward)
     to_send = second_sum(place, from_ring)
     part, gain = stream_sum(stream_ring(to_send))
-    d_proj = finish_call(place, stream_ring([part] * RING))
+    d_keys, d_values = rim_call(d_keys, d_values, from_below, from_above)
+    d_proj = finish_call(place, stream_ring([part] * RING), d_keys)
     d_gain = gain.reshape(-1)
-
-    d_keys, d_values = rim_call(d_keys, d_values, from_below, from_above)
     return (d_query[None], d_keys[None], d_values[None], d_proj, d_gain)
 
 

time: 202 us -> 217 us (1.074)
  waiting for transfers between devices: 47.1 us -> 60.8 us
    ppermute x6, waiting for transfers between devices: 7.64 us -> 27.7 us  [ring(): lax.ppermute(values[k], 'seq', along(which, k))]
    ppermute x6, waiting for transfers between devices: 9.25 us -> 2.88 us  [stream_ring(): lax.ppermute(values[k], 'dp', [(i, (i + k) % count) for i in range(count)])]
  transfers between devices with their start and end apart: 22 -> 22, of which waited for: 9 -> 7; matrix products, arithmetic and copies ran while one was open for 6% -> 6% of each run, Pallas kernels for 26% -> 26%
where the time goes in v3:
time: 217 us; the launch traced here: 215 us
  Pallas kernels  86.9 us (40%)
  waiting for transfers between devices  60.8 us (28%)
  starting transfers between devices  33 us (15%)
  between operations  14.4 us (7%)
  local copies, waits for them, and re-layouts  14.3 us (7%)
  other arithmetic  5.95 us (3%)
    all_gather x1, waiting for transfers between devices, on_device(): weights = lax.all_gather(proj_weight, 'seq', axis=0, tiled=True)  29.5 us
    ppermute x6, waiting for transfers between devices, ring(): lax.ppermute(values[k], 'seq', along(which, k))  27.7 us
    pallas_call x1, Pallas kernels, backward_call(): pl.pallas_call(backward_kernel, out_shape=[jax.ShapeDtypeStruct((count, w...  24.6 us
    pallas_call x1, Pallas kernels, latent_call(): pl.pallas_call(latent_kernel, out_shape=[jax.ShapeDtypeStruct((patches, c...  17.4 us
    pallas_call x1, Pallas kernels, forward_call(): pl.pallas_call(forward_kernel, out_shape=[jax.ShapeDtypeStruct((patches,...  13.9 us
    ppermute x6, starting transfers between devices, stream_ring(): lax.ppermute(values[k], 'dp', [(i, (i + k) % count) for i in range(count)])  9.82 us
    pallas_call x1, Pallas kernels, d_proj_call(): pl.pallas_call(d_proj_kernel, out_shape=[jax.ShapeDtypeStruct((width + 16...  8.7 us
    pallas_call x1, Pallas kernels, d_attended_call(): pl.pallas_call(d_attended_kernel, out_shape=jax.ShapeDtypeStruct((patches...  8.54 us
  transfers between devices with their start and end apart: 22, of which 7 were waited for; matrix products, arithmetic and copies ran while one was open for 6% of the time, Pallas kernels for 26%

profile of v3, /device:TPU:0, one launch (start us, length us, event | category | flops | bytes accessed | tf_op | source)
XLA Modules:
  0.0 215.3 jit_solution(6583388907618696366)
XLA Ops:
  7.2 0.7 all-gather.2.cloned.1.call-update
  7.9 0.7 slice.49
  8.6 1.3 collective-permute-start.1
  9.9 0.7 slice_reduce_fusion
  10.6 3.0 %collective-permute-start = (s32[384]{0:T(512)S(1)}, s32[384]{0:T(512)S(1)}, u32[]{:S(2)}, u32[]{:S(2)}) collective-permute-start(s32[384]{0:T(512)S(1)} %slice_reduce_fusion), channel_id=1, source_target_pairs={{0,1},{1,2},{2,3},{3,4},{4,5},{5,6},{6,7},{7,8},{8,9},{9,10},{10,1... | collective-permute-start | bytes 4616 | tf_op jit(solution)/shard_map/ppermute | solution.py:750
  13.6 1.3 slice_bitcast_fusion.2
  14.9 1.0 pad_maximum_fusion.1
  15.9 1.4 collective-permute-start.3
  17.3 1.5 slice_bitcast_fusion
  19.0 3.8 %collective-permute-start.2 = (bf16[768,1024]{1,0:T(8,128)(2,1)S(1)}, bf16[768,1024]{1,0:T(8,128)(2,1)S(1)}, u32[]{:S(2)}, u32[]{:S(2)}) collective-permute-start(bf16[768,1024]{1,0:T(8,128)(2,1)S(1)} %pad_maximum_fusion), channel_id=1, source_target_pairs={{0,1},{1,2},{2,3},{3,4},{4,5},{5,6},{6,7},{7,8},{8,9},{9,10},{10,1... | collective-permute-start | bytes 4718600 | tf_op jit(solution)/shard_map/ppermute | solution.py:754
  23.7 0.7 pad_add_fusion.1.place_ref
  24.4 0.9 select_reduce_fusion
  25.2 1.3 convert_reduce_fusion
  27.1 0.7 maximum_reduce_fusion
  28.0 0.6 pad_bitcast_fusion.span_ref
  28.7 1.2 copy-done
  29.8 13.9 %attention_forward.1 = (bf16[512,1024]{1,0:T(8,128)(2,1)}, f32[64,128]{1,0:T(8,128)}) custom-call(s32[8]{0:T(128)} %get-tuple-element.76.offset_ref, s32[8]{0:T(128)} %get-tuple-element.75.short_ref, s32[64,128]{1,0:T(8,128)} %pad_bitcast_fusion.span_ref, bf16[768,1024]{1,0:T(8,128)(2,1)} %copy-done, bf16[512,1024]{1,0:T(8,128)(2,1)} %collective-permute-done.3.high_ref, ...), custom_call_target="tpu_custom_call" | custom-call | flops 1241513984 | bytes 20971520 | tf_op jit(solution)/shard_map/attention_forward/pallas_call | solution.py:230
  43.8 29.5 %all-gather.2.cloned.1.call-done.weights_ref = bf16[4096,1024]{1,0:T(8,128)(2,1)} async-done(((bf16[128,1024]{1,0:T(8,128)(2,1)}), bf16[4096,1024]{1,0:T(8,128)(2,1)}) %all-gather.2.cloned.1.call-update) | async-done | bytes 8388624 | tf_op jit(solution)/shard_map/all_gather | solution.py:755
  73.3 17.4 %latent.1 = (bf16[512,2048]{1,0:T(8,128)(2,1)}, bf16[512,2048]{1,0:T(8,128)(2,1)}, f32[256,128]{1,0:T(8,128)}) custom-call(s32[4]{0:T(128)} %pad_add_fusion.1.place_ref, bf16[512,1024]{1,0:T(8,128)(2,1)} %get-tuple-element.39.attended_ref, f32[1,4096]{1,0:T(1,128)} %bitcast.56, bf16[512,4096]{1,0:T(8,128)(2,1)} %bitcast.55, ...), custom_call_target="tpu_custom_call" | custom-call | flops 4294967296 | bytes 18874368 | tf_op jit(solution)/shard_map/latent/pallas_call | solution.py:404
  91.3 0.9 slice.60
  92.6 8.5 %d_attended.1.after_ref.d_attended_ref = bf16[512,1024]{1,0:T(8,128)(2,1)} custom-call(s32[4]{0:T(128)} %pad_add_fusion.1.place_ref, bf16[512,2048]{1,0:T(8,128)(2,1)} %get-tuple-element.40.mine_ref, bf16[512,2048]{1,0:T(8,128)(2,1)} %get-tuple-element.41.other_ref, bf16[4096,1024]{1,0:T(8,128)(2,1)} %all-gather.2.cloned.1.call-done.weights_ref), custom_call_target="tpu_custom_call" | custom-call | flops 4294967296 | bytes 14680064 | tf_op jit(solution)/shard_map/d_attended/pallas_call | solution.py:465
  101.7 1.3 copy-done.17
  103.1 8.7 %d_proj.1 = (bf16[1040,512]{1,0:T(8,128)(2,1)}, bf16[1040,512]{1,0:T(8,128)(2,1)}, bf16[1040,512]{1,0:T(8,128)(2,1)}, bf16[1040,512]{1,0:T(8,128)(2,1)}) custom-call(bf16[512,2048]{1,0:T(8,128)(2,1)} %get-tuple-element.40.mine_ref, bf16[512,2048]{1,0:T(8,128)(2,1)} %copy-done.17, bf16[512,1024]{1,0:T(8,128)(2,1)} %get-tuple-element.39.attended_ref, ...), custom_call_target="tpu_custom_call" | custom-call | flops 4294967296 | bytes 12582912 | tf_op jit(solution)/shard_map/d_proj/pallas_call | solution.py:522
  111.8 1.2 collective-permute-start.7
  113.0 2.9 %collective-permute-start.8 = (bf16[1040,512]{1,0:T(8,128)(2,1)}, bf16[1040,512]{1,0:T(8,128)(2,1)S(1)}, u32[]{:S(2)}, u32[]{:S(2)}) collective-permute-start(bf16[1040,512]{1,0:T(8,128)(2,1)} %get-tuple-element.45), channel_id=1, source_target_pairs={{0,16},{1,5},{2,18},{3,7},{4,20},{5,1},{6,22},{7,3},{8,24},{9,13},... | collective-permute-start | bytes 3194888 | tf_op jit(solution)/shard_map/ppermute | solution.py:612
  115.8 1.4 collective-permute-start.9
  117.2 24.6 %attention_backward.1 = (bf16[512,1024]{1,0:T(8,128)(2,1)}, bf16[2048,1024]{1,0:T(8,128)(2,1)}, bf16[2048,1024]{1,0:T(8,128)(2,1)}, bf16[768,1024]{1,0:T(8,128)(2,1)}, bf16[512,1024]{1,0:T(8,128)(2,1)}) custom-call(s32[8]{0:T(128)} %get-tuple-element.76.offset_ref, s32[8]{0:T(128)} %get-tuple-element.75.short_ref, s32[64,128]{1,0:T(8,128)} %pad_bitcast_fusion.span_ref, ...), custom_call_target="tpu_custom_call" | custom-call | flops 4345298944 | bytes 41943040 | tf_op jit(solution)/shard_map/attention_backward/pallas_call | solution.py:264
  141.8 1.0 copy-done.2
  143.5 3.4 %first_sum.1 = (bf16[1088,128]{1,0:T(8,128)(2,1)}, bf16[1088,128]{1,0:T(8,128)(2,1)}, bf16[1088,128]{1,0:T(8,128)(2,1)}, bf16[1088,128]{1,0:T(8,128)(2,1)}) custom-call(bf16[1040,512]{1,0:T(8,128)(2,1)} %get-tuple-element.52.after_ref.refs_0_, bf16[1040,512]{1,0:T(8,128)(2,1)} %copy-done.2, bf16[1040,512]{1,0:T(8,128)(2,1)} %copy-done.3, ...), custom_call_target="tpu_custom_call" | custom-call | tf_op jit(solution)/shard_map/first_sum/pallas_call | solution.py:649
  147.1 7.8 %collective-permute-done.10.refs_1_ = bf16[1088,128]{1,0:T(8,128)(2,1)S(1)} collective-permute-done((bf16[1088,128]{1,0:T(8,128)(2,1)}, bf16[1088,128]{1,0:T(8,128)(2,1)S(1)}, u32[]{:S(2)}, u32[]{:S(2)}) %collective-permute-start.10) | collective-permute-done | bytes 278560 | tf_op jit(solution)/shard_map/ppermute | solution.py:612
  154.9 1.3 collective-permute-start.12
  156.2 3.1 %collective-permute-start.11 = (bf16[512,1024]{1,0:T(8,128)(2,1)}, bf16[512,1024]{1,0:T(8,128)(2,1)S(1)}, u32[]{:S(2)}, u32[]{:S(2)}) collective-permute-start(bf16[512,1024]{1,0:T(8,128)(2,1)} %get-tuple-element.59), channel_id=1, source_target_pairs={{0,1},{1,2},{2,3},{3,4},{4,5},{5,6},{6,7},{7,8},{8,9},{9,10},{10,1... | collective-permute-start | bytes 3145736 | tf_op jit(solution)/shard_map/ppermute | solution.py:791
  159.7 2.2 %collective-permute-start.14 = (bf16[1088,128]{1,0:T(8,128)(2,1)}, bf16[1088,128]{1,0:T(8,128)(2,1)S(1)}, u32[]{:S(2)}, u32[]{:S(2)}) collective-permute-start(bf16[1088,128]{1,0:T(8,128)(2,1)} %get-tuple-element.66), channel_id=1, source_target_pairs={{0,6},{1,25},{2,0},{3,27},{4,2},{5,29},{6,4},{7,31},{8,14},{9,1},{... | collective-permute-start | bytes 835592 | tf_op jit(solution)/shard_map/ppermute | solution.py:612
  161.9 8.8 %collective-permute-done.13.refs_2_ = bf16[1088,128]{1,0:T(8,128)(2,1)S(1)} collective-permute-done((bf16[1088,128]{1,0:T(8,128)(2,1)}, bf16[1088,128]{1,0:T(8,128)(2,1)S(1)}, u32[]{:S(2)}, u32[]{:S(2)}) %collective-permute-start.13) | collective-permute-done | bytes 278560 | tf_op jit(solution)/shard_map/ppermute | solution.py:612
  170.7 11.1 %collective-permute-done.14.refs_3_ = bf16[1088,128]{1,0:T(8,128)(2,1)S(1)} collective-permute-done((bf16[1088,128]{1,0:T(8,128)(2,1)}, bf16[1088,128]{1,0:T(8,128)(2,1)S(1)}, u32[]{:S(2)}, u32[]{:S(2)}) %collective-permute-start.14) | collective-permute-done | bytes 278560 | tf_op jit(solution)/shard_map/ppermute | solution.py:612
  181.8 0.7 copy-done.8
  182.5 2.2 %second_sum.1 = (bf16[320,128]{1,0:T(8,128)(2,1)}, bf16[320,128]{1,0:T(8,128)(2,1)}, bf16[320,128]{1,0:T(8,128)(2,1)}, bf16[320,128]{1,0:T(8,128)(2,1)}) custom-call(s32[4]{0:T(128)} %pad_add_fusion.1.place_ref, bf16[1088,128]{1,0:T(8,128)(2,1)} %get-tuple-element.63.refs_0_, bf16[1088,128]{1,0:T(8,128)(2,1)} %copy-done.6, bf16[1088,128]{1,0:T(8,128)(2,1)} %copy-done.7, ...), custom_call_target="tpu_custom_call" | custom-call | tf_op jit(solution)/shard_map/second_sum/pallas_call | solution.py:674
  184.8 1.5 collective-permute-start.15
  186.3 2.7 %collective-permute-start.16 = (bf16[320,128]{1,0:T(8,128)(2,1)}, bf16[320,128]{1,0:T(8,128)(2,1)S(1)}, u32[]{:S(2)}, u32[]{:S(2)}) collective-permute-start(bf16[320,128]{1,0:T(8,128)(2,1)} %get-tuple-element.69), channel_id=1, source_target_pairs={{0,64},{32,96},{64,0},{96,32},{1,65},{33,97},{65,1},{97,33},{2,66}... | collective-permute-start | bytes 245768 | tf_op jit(solution)/shard_map/ppermute | solution.py:733
  189.0 1.8 collective-permute-start.17
  190.7 1.1 collective-permute-done.15.refs_1_
  191.9 1.2 collective-permute-done.16.refs_2_
  194.2 1.7 stream_sum.1
  195.9 3.0 %collective-permute-start.20 = (bf16[256,128]{1,0:T(8,128)(2,1)}, bf16[256,128]{1,0:T(8,128)(2,1)S(1)}, u32[]{:S(2)}, u32[]{:S(2)}) collective-permute-start(bf16[256,128]{1,0:T(8,128)(2,1)} %get-tuple-element.71.refs_0_), channel_id=1, source_target_pairs={{0,96},{32,0},{64,32},{96,64},{1,97},{33,1},{65,33},{97,65},{2,98}... | collective-permute-start | bytes 196616 | tf_op jit(solution)/shard_map/ppermute | solution.py:733
  198.9 0.9 collective-permute-start.18
  199.8 1.0 copy-done.5
  201.3 4.6 %rims.1 = (bf16[2048,1024]{1,0:T(8,128)(2,1)}, bf16[2048,1024]{1,0:T(8,128)(2,1)}) custom-call(bf16[2048,1024]{1,0:T(8,128)(2,1)} %get-tuple-element.50.key_in, bf16[2048,1024]{1,0:T(8,128)(2,1)} %get-tuple-element.51.value_in, bf16[512,1024]{1,0:T(8,128)(2,1)} %copy-done.5, bf16[768,1024]{1,0:T(8,128)(2,1)} %copy-done.1), custom_call_target="tpu_custom_call", output_to_operand_aliasing={{0}: (0, {}), {1}: (1, {})} | custom-call | tf_op jit(solution)/shard_map/rims/pallas_call | solution.py:581
  206.5 1.9 d_proj_rows.1
  (72 shorter events, 7.0 us)
Async XLA Ops:
  7.2 66.1 %all-gather.2.cloned.1.call-start = ((), (), s32[]{:S(2)}) async-start(), calls=%async_computation | async-start | bytes 8650752 | tf_op jit(solution)/shard_map/all_gather | solution.py:755
  8.6 15.7 %collective-permute-start.1 = (s32[256]{0:T(256)S(1)}, s32[256]{0:T(256)S(1)}, u32[]{:S(2)}, u32[]{:S(2)}) collective-permute-start(s32[256]{0:T(256)S(1)} %bitcast.54), channel_id=1, source_target_pairs={{1,0},{2,1},{3,2},{4,3},{5,4},{6,5},{7,6},{8,7},{9,8},{10,9},{11,1... | collective-permute-start | bytes 3080 | tf_op jit(solution)/shard_map/ppermute | solution.py:751
  10.6 13.8 %collective-permute-start = (s32[384]{0:T(512)S(1)}, s32[384]{0:T(512)S(1)}, u32[]{:S(2)}, u32[]{:S(2)}) collective-permute-start(s32[384]{0:T(512)S(1)} %slice_reduce_fusion), channel_id=1, source_target_pairs={{0,1},{1,2},{2,3},{3,4},{4,5},{5,6},{6,7},{7,8},{8,9},{9,10},{10,1... | collective-permute-start | bytes 4616 | tf_op jit(solution)/shard_map/ppermute | solution.py:750
  15.9 6.9 %copy-start.16 = (s32[1,512]{1,0:T(1,128)S(1)}, s32[1,512]{1,0:T(1,128)}, u32[]{:S(2)}) copy-start(s32[1,512]{1,0:T(1,128)} %param.12) | copy-start | bytes 6148
  15.9 8.4 %copy-start.15 = (s32[1,2048]{1,0:T(1,128)S(1)}, s32[1,2048]{1,0:T(1,128)}, u32[]{:S(2)}) copy-start(s32[1,2048]{1,0:T(1,128)} %param.10) | copy-start | bytes 24580
  15.9 12.7 %collective-permute-start.3 = (bf16[512,1024]{1,0:T(8,128)(2,1)}, bf16[512,1024]{1,0:T(8,128)(2,1)}, u32[]{:S(2)}, u32[]{:S(2)}) collective-permute-start(bf16[512,1024]{1,0:T(8,128)(2,1)} %pad_maximum_fusion.1), channel_id=1, source_target_pairs={{1,0},{2,1},{3,2},{4,3},{5,4},{6,5},{7,6},{8,7},{9,8},{10,9},{11,1... | collective-permute-start | bytes 3145736 | tf_op jit(solution)/shard_map/ppermute | solution.py:754
  19.0 9.7 %collective-permute-start.2 = (bf16[768,1024]{1,0:T(8,128)(2,1)S(1)}, bf16[768,1024]{1,0:T(8,128)(2,1)S(1)}, u32[]{:S(2)}, u32[]{:S(2)}) collective-permute-start(bf16[768,1024]{1,0:T(8,128)(2,1)S(1)} %pad_maximum_fusion), channel_id=1, source_target_pairs={{0,1},{1,2},{2,3},{3,4},{4,5},{5,6},{6,7},{7,8},{8,9},{9,10},{10,1... | collective-permute-start | bytes 4718600 | tf_op jit(solution)/shard_map/ppermute | solution.py:754
  28.7 1.2 copy-start
  73.3 17.7 %copy-start.18 = (bf16[512,1024]{1,0:T(8,128)(2,1)S(1)}, bf16[512,1024]{1,0:T(8,128)(2,1)}, u32[]{:S(2)}) copy-start(bf16[512,1024]{1,0:T(8,128)(2,1)} %get-tuple-element.39.attended_ref) | copy-start | bytes 3145732
  90.6 11.1 %collective-permute-start.4 = (bf16[512,2048]{1,0:T(8,128)(2,1)}, bf16[512,2048]{1,0:T(8,128)(2,1)S(1)}, u32[]{:S(2)}, u32[]{:S(2)}) collective-permute-start(bf16[512,2048]{1,0:T(8,128)(2,1)} %get-tuple-element.41.other_ref), channel_id=1, source_target_pairs={{0,1},{1,0},{2,3},{3,2},{4,5},{5,4},{6,7},{7,6},{8,9},{9,8},{10,11... | collective-permute-start | bytes 6291464 | tf_op jit(solution)/shard_map/ppermute | solution.py:607
  91.0 10.7 %collective-permute-start.5 = (bf16[512,1024]{1,0:T(8,128)(2,1)S(1)}, bf16[512,1024]{1,0:T(8,128)(2,1)}, u32[]{:S(2)}, u32[]{:S(2)}) collective-permute-start(bf16[512,1024]{1,0:T(8,128)(2,1)S(1)} %copy-done.18), channel_id=1, source_target_pairs={{0,1},{1,0},{2,3},{3,2},{4,5},{5,4},{6,7},{7,6},{8,9},{9,8},{10,11... | collective-permute-start | bytes 3145736 | tf_op jit(solution)/shard_map/ppermute | solution.py:607
  92.2 8.9 %collective-permute-start.6 = (f32[8,512]{1,0:T(8,128)S(1)}, f32[8,512]{1,0:T(8,128)S(1)}, u32[]{:S(2)}, u32[]{:S(2)}) collective-permute-start(f32[8,512]{1,0:T(8,128)S(1)} %bitcast.45), channel_id=1, source_target_pairs={{0,1},{1,0},{2,3},{3,2},{4,5},{5,4},{6,7},{7,6},{8,9},{9,8},{10,11... | collective-permute-start | bytes 49160 | tf_op jit(solution)/shard_map/ppermute | solution.py:607
  101.7 1.3 copy-start.17
  111.8 30.0 %collective-permute-start.7 = (bf16[1040,512]{1,0:T(8,128)(2,1)}, bf16[1040,512]{1,0:T(8,128)(2,1)S(1)}, u32[]{:S(2)}, u32[]{:S(2)}) collective-permute-start(bf16[1040,512]{1,0:T(8,128)(2,1)} %get-tuple-element.44), channel_id=1, source_target_pairs={{0,8},{1,3},{2,10},{3,5},{4,12},{5,7},{6,14},{7,1},{8,16},{9,11},{... | collective-permute-start | bytes 3194888 | tf_op jit(solution)/shard_map/ppermute | solution.py:612
  113.0 28.8 %collective-permute-start.8 = (bf16[1040,512]{1,0:T(8,128)(2,1)}, bf16[1040,512]{1,0:T(8,128)(2,1)S(1)}, u32[]{:S(2)}, u32[]{:S(2)}) collective-permute-start(bf16[1040,512]{1,0:T(8,128)(2,1)} %get-tuple-element.45), channel_id=1, source_target_pairs={{0,16},{1,5},{2,18},{3,7},{4,20},{5,1},{6,22},{7,3},{8,24},{9,13},... | collective-permute-start | bytes 3194888 | tf_op jit(solution)/shard_map/ppermute | solution.py:612
  115.8 26.0 %collective-permute-start.9 = (bf16[1040,512]{1,0:T(8,128)(2,1)}, bf16[1040,512]{1,0:T(8,128)(2,1)S(1)}, u32[]{:S(2)}, u32[]{:S(2)}) collective-permute-start(bf16[1040,512]{1,0:T(8,128)(2,1)} %get-tuple-element.46), channel_id=1, source_target_pairs={{0,24},{1,7},{2,26},{3,1},{4,28},{5,3},{6,30},{7,5},{8,0},{9,15},{... | collective-permute-start | bytes 3194888 | tf_op jit(solution)/shard_map/ppermute | solution.py:612
  141.8 1.0 copy-start.2
  141.8 1.3 copy-start.3
  141.8 1.7 copy-start.4
  146.9 8.0 %collective-permute-start.10 = (bf16[1088,128]{1,0:T(8,128)(2,1)}, bf16[1088,128]{1,0:T(8,128)(2,1)S(1)}, u32[]{:S(2)}, u32[]{:S(2)}) collective-permute-start(bf16[1088,128]{1,0:T(8,128)(2,1)} %get-tuple-element.56), channel_id=1, source_target_pairs={{0,2},{1,9},{2,4},{3,11},{4,6},{5,13},{6,0},{7,15},{8,10},{9,17},{... | collective-permute-start | bytes 835592 | tf_op jit(solution)/shard_map/ppermute | solution.py:612
  154.9 26.9 %copy-start.6 = (bf16[1088,128]{1,0:T(8,128)(2,1)}, bf16[1088,128]{1,0:T(8,128)(2,1)S(1)}, u32[]{:S(2)}) copy-start(bf16[1088,128]{1,0:T(8,128)(2,1)S(1)} %collective-permute-done.10.refs_1_) | copy-start | bytes 835588
  154.9 44.9 %collective-permute-start.12 = (bf16[768,1024]{1,0:T(8,128)(2,1)}, bf16[768,1024]{1,0:T(8,128)(2,1)S(1)}, u32[]{:S(2)}, u32[]{:S(2)}) collective-permute-start(bf16[768,1024]{1,0:T(8,128)(2,1)} %get-tuple-element.60), channel_id=1, source_target_pairs={{1,0},{2,1},{3,2},{4,3},{5,4},{6,5},{7,6},{8,7},{9,8},{10,9},{11,1... | collective-permute-start | bytes 4718600 | tf_op jit(solution)/shard_map/ppermute | solution.py:790
  156.2 43.6 %collective-permute-start.11 = (bf16[512,1024]{1,0:T(8,128)(2,1)}, bf16[512,1024]{1,0:T(8,128)(2,1)S(1)}, u32[]{:S(2)}, u32[]{:S(2)}) collective-permute-start(bf16[512,1024]{1,0:T(8,128)(2,1)} %get-tuple-element.59), channel_id=1, source_target_pairs={{0,1},{1,2},{2,3},{3,4},{4,5},{5,6},{6,7},{7,8},{8,9},{9,10},{10,1... | collective-permute-start | bytes 3145736 | tf_op jit(solution)/shard_map/ppermute | solution.py:791
  159.3 11.4 %collective-permute-start.13 = (bf16[1088,128]{1,0:T(8,128)(2,1)}, bf16[1088,128]{1,0:T(8,128)(2,1)S(1)}, u32[]{:S(2)}, u32[]{:S(2)}) collective-permute-start(bf16[1088,128]{1,0:T(8,128)(2,1)} %get-tuple-element.65), channel_id=1, source_target_pairs={{0,4},{1,17},{2,6},{3,19},{4,0},{5,21},{6,2},{7,23},{8,12},{9,25},... | collective-permute-start | bytes 835592 | tf_op jit(solution)/shard_map/ppermute | solution.py:612
  159.7 22.1 %collective-permute-start.14 = (bf16[1088,128]{1,0:T(8,128)(2,1)}, bf16[1088,128]{1,0:T(8,128)(2,1)S(1)}, u32[]{:S(2)}, u32[]{:S(2)}) collective-permute-start(bf16[1088,128]{1,0:T(8,128)(2,1)} %get-tuple-element.66), channel_id=1, source_target_pairs={{0,6},{1,25},{2,0},{3,27},{4,2},{5,29},{6,4},{7,31},{8,14},{9,1},{... | collective-permute-start | bytes 835592 | tf_op jit(solution)/shard_map/ppermute | solution.py:612
  170.7 11.1 %copy-start.7 = (bf16[1088,128]{1,0:T(8,128)(2,1)}, bf16[1088,128]{1,0:T(8,128)(2,1)S(1)}, u32[]{:S(2)}) copy-start(bf16[1088,128]{1,0:T(8,128)(2,1)S(1)} %collective-permute-done.13.refs_2_) | copy-start | bytes 835588
  181.8 0.7 copy-start.8
  184.8 7.1 %collective-permute-start.15 = (bf16[320,128]{1,0:T(8,128)(2,1)}, bf16[320,128]{1,0:T(8,128)(2,1)S(1)}, u32[]{:S(2)}, u32[]{:S(2)}) collective-permute-start(bf16[320,128]{1,0:T(8,128)(2,1)} %get-tuple-element.68), channel_id=1, source_target_pairs={{0,32},{32,64},{64,96},{96,0},{1,33},{33,65},{65,97},{97,1},{2,34}... | collective-permute-start | bytes 245768 | tf_op jit(solution)/shard_map/ppermute | solution.py:733
  186.3 6.8 %collective-permute-start.16 = (bf16[320,128]{1,0:T(8,128)(2,1)}, bf16[320,128]{1,0:T(8,128)(2,1)S(1)}, u32[]{:S(2)}, u32[]{:S(2)}) collective-permute-start(bf16[320,128]{1,0:T(8,128)(2,1)} %get-tuple-element.69), channel_id=1, source_target_pairs={{0,64},{32,96},{64,0},{96,32},{1,65},{33,97},{65,1},{97,33},{2,66}... | collective-permute-start | bytes 245768 | tf_op jit(solution)/shard_map/ppermute | solution.py:733
  189.0 4.7 %collective-permute-start.17 = (bf16[320,128]{1,0:T(8,128)(2,1)}, bf16[320,128]{1,0:T(8,128)(2,1)S(1)}, u32[]{:S(2)}, u32[]{:S(2)}) collective-permute-start(bf16[320,128]{1,0:T(8,128)(2,1)} %get-tuple-element.70), channel_id=1, source_target_pairs={{0,96},{32,0},{64,32},{96,64},{1,97},{33,1},{65,33},{97,65},{2,98}... | collective-permute-start | bytes 245768 | tf_op jit(solution)/shard_map/ppermute | solution.py:733
  191.8 1.8 copy-start.9
  193.0 0.6 copy-start.10
  193.6 0.6 copy-start.11
  195.9 9.9 %collective-permute-start.20 = (bf16[256,128]{1,0:T(8,128)(2,1)}, bf16[256,128]{1,0:T(8,128)(2,1)S(1)}, u32[]{:S(2)}, u32[]{:S(2)}) collective-permute-start(bf16[256,128]{1,0:T(8,128)(2,1)} %get-tuple-element.71.refs_0_), channel_id=1, source_target_pairs={{0,96},{32,0},{64,32},{96,64},{1,97},{33,1},{65,33},{97,65},{2,98}... | collective-permute-start | bytes 196616 | tf_op jit(solution)/shard_map/ppermute | solution.py:733
  198.9 7.0 %collective-permute-start.19 = (bf16[256,128]{1,0:T(8,128)(2,1)}, bf16[256,128]{1,0:T(8,128)(2,1)S(1)}, u32[]{:S(2)}, u32[]{:S(2)}) collective-permute-start(bf16[256,128]{1,0:T(8,128)(2,1)} %get-tuple-element.71.refs_0_), channel_id=1, source_target_pairs={{0,64},{32,96},{64,0},{96,32},{1,65},{33,97},{65,1},{97,33},{2,66}... | collective-permute-start | bytes 196616 | tf_op jit(solution)/shard_map/ppermute | solution.py:733
  198.9 7.0 %collective-permute-start.18 = (bf16[256,128]{1,0:T(8,128)(2,1)}, bf16[256,128]{1,0:T(8,128)(2,1)S(1)}, u32[]{:S(2)}, u32[]{:S(2)}) collective-permute-start(bf16[256,128]{1,0:T(8,128)(2,1)} %get-tuple-element.71.refs_0_), channel_id=1, source_target_pairs={{0,32},{32,64},{64,96},{96,0},{1,33},{33,65},{65,97},{97,1},{2,34}... | collective-permute-start | bytes 196616 | tf_op jit(solution)/shard_map/ppermute | solution.py:733
  199.8 1.0 copy-start.5
  199.8 1.5 copy-start.1
  205.9 0.6 copy-start.12
  205.9 0.6 copy-start.13
  205.9 0.6 copy-start.14
Sparse Core Ops, SparseCore 0:
  10.3 62.9 all-gather.1

commit v4 on v3

--- a/solution.py
+++ b/solution.py
@@ -629,60 +629,58 @@
     return value[:rows] + value[rows:]
 
 
-def first_sum_kernel(*refs):
+def first_sum_kernel(place_ref, *refs):
     parts, outs = refs[:4], refs[4:]
     width = parts[0].shape[0] - 16
-    gain = joined(total_of([ref[width:, :] for ref in parts]))
+    quarter = width // RING
+    gain = halves(joined(total_of([ref[width:, :] for ref in parts])))
+    for k in (1, 2, 3, 0):
+        rows = pl.ds(pl.multiple_of((place_ref[3] + k) % RING * quarter, quarter), quarter)
+        outs[k][:quarter, :] = total_of([ref[rows, :] for ref in parts]).astype(bf16)
+        outs[k][quarter:, :] = gain
+
+
+def first_sum(place, parts):
+    width = parts[0].shape[0] - 16
+    vmem = pl.BlockSpec(memory_space=pltpu.VMEM)
+    return pl.pallas_call(
+        first_sum_kernel,
+        out_shape=[jax.ShapeDtypeStruct((width // RING + 16, 512), bf16)] * RING,
+        in_specs=[pl.BlockSpec(memory_space=pltpu.SMEM)] + [vmem] * 4,
+        out_specs=[vmem] * RING,
+        compiler_params=pltpu.CompilerParams(vmem_limit_bytes=VMEM_GRANT),
+        name="first_sum",
+    )(place, *parts)
+
+
+def second_sum_kernel(*refs):
+    parts, outs = refs[:4], refs[4:]
+    quarter = parts[0].shape[0] - 16
+    gain = joined(total_of([ref[quarter:, :] for ref in parts]))
     gain = halves(
         jnp.concatenate([gain[:, k * LANES : (k + 1) * LANES] for k in range(RING)])
     )
     for k in range(RING):
         start = (RING - k) % RING * LANES
         columns = slice(start, start + LANES)
-        outs[k][:width, :] = total_of([ref[:width, columns] for ref in parts]).astype(bf16)
-        outs[k][width:, :] = gain
-
-
-def first_sum(parts):
-    width = parts[0].shape[0] - 16
+        outs[k][:quarter, :] = total_of([ref[:quarter, columns] for ref in parts]).astype(bf16)
+        outs[k][quarter:, :] = gain
+
+
+def second_sum(parts):
+    quarter = parts[0].shape[0] - 16
     vmem = pl.BlockSpec(memory_space=pltpu.VMEM)
     return pl.pallas_call(
-        first_sum_kernel,
-        out_shape=[jax.ShapeDtypeStruct((width + 64, LANES), bf16)] * RING,
+        second_sum_kernel,
+        out_shape=[jax.ShapeDtypeStruct((quarter + 64, LANES), bf16)] * RING,
         in_specs=[vmem] * 4,
-        out_specs=[vmem] * 4,
+        out_specs=[vmem] * RING,
         compiler_params=pltpu.CompilerParams(vmem_limit_bytes=VMEM_GRANT),
-        name="first_sum",
+        name="second_sum",
     )(*parts)
 
 
-def second_sum_kernel(place_ref, *refs):
-    parts, outs, total = refs[:4], refs[4:8], refs[8]
-    width = total.shape[0]
-    quarter = width // RING
-    total[...] = total_of([ref[:width, :] for ref in parts])
-    gain = halves(joined(total_of([ref[width:, :] for ref in parts])))
-    for k in range(RING):
-        start = pl.multiple_of((place_ref[3] + k) % RING * quarter, quarter)
-        outs[k][:quarter, :] = total[pl.ds(start, quarter), :].astype(bf16)
-        outs[k][quarter:, :] = gain
-
-
-def second_sum(place, parts):
-    width = parts[0].shape[0] - 64
-    vmem = pl.BlockSpec(memory_space=pltpu.VMEM)
-    return pl.pallas_call(
-        second_sum_kernel,
-        out_shape=[jax.ShapeDtypeStruct((width // RING + 64, LANES), bf16)] * RING,
-        in_specs=[pl.BlockSpec(memory_space=pltpu.SMEM)]
-        + [vmem] * 4,
-        out_specs=[vmem] * RING,
-        scratch_shapes=[pltpu.VMEM((width, LANES), f32)],
-        name="second_sum",
-    )(place, *parts)
-
-
-def stream_sum_kernel(*refs):
+def last_sum_kernel(*refs):
     parts, part_ref, gain_ref = refs[:4], refs[4], refs[5]
     quarter = part_ref.shape[0]
     total = total_of([ref[...] for ref in parts])
@@ -690,18 +688,18 @@
     gain_ref[...] = joined(total[quarter:, :])
 
 
-def stream_sum(parts):
+def last_sum(parts):
     quarter = parts[0].shape[0] - 64
     vmem = pl.BlockSpec(memory_space=pltpu.VMEM)
     return pl.pallas_call(
-        stream_sum_kernel,
+        last_sum_kernel,
         out_shape=[
             jax.ShapeDtypeStruct((quarter, LANES), bf16),
             jax.ShapeDtypeStruct((32, LANES), f32),
         ],
         in_specs=[vmem] * 4,
         out_specs=[vmem] * 2,
-        name="stream_sum",
+        name="last_sum",
     )(*parts)
 
 
@@ -785,12 +783,11 @@
     inputs = common + (attended, level, d_attended)
     d_query, d_keys, d_values, d_low, d_high = backward_call(inputs, to_send[0])
     from_ring, d_query = lax.optimization_barrier((from_ring, d_query))
-    from_ring = ring(first_sum(from_ring), "second")
-    from_ring[1], d_low, d_high = lax.optimization_barrier((from_ring[1], d_low, d_high))
+    to_send, d_low, d_high = lax.optimization_barrier((first_sum(place, from_ring), d_low, d_high))
+    from_streams = stream_ring(to_send)
     from_above = lax.ppermute(d_low, "seq", downward)
     from_below = lax.ppermute(d_high, "seq", upward)
-    to_send = second_sum(place, from_ring)
-    part, gain = stream_sum(stream_ring(to_send))
+    part, gain = last_sum(ring(second_sum(from_streams), "second"))
     d_keys, d_values = rim_call(d_keys, d_values, from_below, from_above)
     d_proj = finish_call(place, stream_ring([part] * RING), d_keys)
     d_gain = gain.reshape(-1)

time: 217 us -> 202 us (0.931)
  waiting for transfers between devices: 60.8 us -> 45.7 us
    ppermute x6, waiting for transfers between devices: 27.7 us -> 3.39 us  [ring(): lax.ppermute(values[k], 'seq', along(which, k))]
    ppermute x6, waiting for transfers between devices: 2.88 us -> 12.1 us  [stream_ring(): lax.ppermute(values[k], 'dp', [(i, (i + k) % count) for i in range(count)])]
  transfers between devices with their start and end apart: 22 -> 22, of which waited for: 7 -> 6; matrix products, arithmetic and copies ran while one was open for 6% -> 6% of each run, Pallas kernels for 26% -> 27%
where the time goes in v4:
time: 202 us; the launch traced here: 201 us
  Pallas kernels  86.7 us (43%)
  waiting for transfers between devices  45.7 us (23%)
  starting transfers between devices  33.7 us (17%)
  local copies, waits for them, and re-layouts  15 us (7%)
  between operations  14.4 us (7%)
  other arithmetic  5.95 us (3%)
    all_gather x1, waiting for transfers between devices, on_device(): weights = lax.all_gather(proj_weight, 'seq', axis=0, tiled=True)  29.5 us
    pallas_call x1, Pallas kernels, backward_call(): pl.pallas_call(backward_kernel, out_shape=[jax.ShapeDtypeStruct((count, w...  24.6 us
    pallas_call x1, Pallas kernels, latent_call(): pl.pallas_call(latent_kernel, out_shape=[jax.ShapeDtypeStruct((patches, c...  17.4 us
    pallas_call x1, Pallas kernels, forward_call(): pl.pallas_call(forward_kernel, out_shape=[jax.ShapeDtypeStruct((patches,...  13.9 us
    ppermute x6, waiting for transfers between devices, stream_ring(): lax.ppermute(values[k], 'dp', [(i, (i + k) % count) for i in range(count)])  12.1 us
    ppermute x6, starting transfers between devices, ring(): lax.ppermute(values[k], 'seq', along(which, k))  9.65 us
    ppermute x6, starting transfers between devices, stream_ring(): lax.ppermute(values[k], 'dp', [(i, (i + k) % count) for i in range(count)])  9.11 us
    pallas_call x1, Pallas kernels, d_proj_call(): pl.pallas_call(d_proj_kernel, out_shape=[jax.ShapeDtypeStruct((width + 16...  8.7 us
  transfers between devices with their start and end apart: 22, of which 6 were waited for; matrix products, arithmetic and copies ran while one was open for 6% of the time, Pallas kernels for 27%

profile of v4, /device:TPU:0, one launch (start us, length us, event | category | flops | bytes accessed | tf_op | source)
XLA Modules:
  0.0 201.4 jit_solution(1708983270773447623)
XLA Ops:
  7.2 0.7 all-gather.2.cloned.1.call-update
  7.9 0.7 slice.49
  8.6 1.3 collective-permute-start.1
  9.9 0.7 slice_reduce_fusion
  10.6 3.0 %collective-permute-start = (s32[384]{0:T(512)S(1)}, s32[384]{0:T(512)S(1)}, u32[]{:S(2)}, u32[]{:S(2)}) collective-permute-start(s32[384]{0:T(512)S(1)} %slice_reduce_fusion), channel_id=1, source_target_pairs={{0,1},{1,2},{2,3},{3,4},{4,5},{5,6},{6,7},{7,8},{8,9},{9,10},{10,1... | collective-permute-start | bytes 4616 | tf_op jit(solution)/shard_map/ppermute | solution.py:748
  13.6 1.3 slice_bitcast_fusion.2
  14.9 1.0 pad_maximum_fusion.1
  15.9 1.4 collective-permute-start.3
  17.3 1.5 slice_bitcast_fusion
  19.0 3.8 %collective-permute-start.2 = (bf16[768,1024]{1,0:T(8,128)(2,1)S(1)}, bf16[768,1024]{1,0:T(8,128)(2,1)S(1)}, u32[]{:S(2)}, u32[]{:S(2)}) collective-permute-start(bf16[768,1024]{1,0:T(8,128)(2,1)S(1)} %pad_maximum_fusion), channel_id=1, source_target_pairs={{0,1},{1,2},{2,3},{3,4},{4,5},{5,6},{6,7},{7,8},{8,9},{9,10},{10,1... | collective-permute-start | bytes 4718600 | tf_op jit(solution)/shard_map/ppermute | solution.py:752
  24.4 0.9 select_reduce_fusion
  25.2 1.3 convert_reduce_fusion
  27.1 0.7 maximum_reduce_fusion
  28.7 1.2 copy-done
  29.8 13.9 %attention_forward.1 = (bf16[512,1024]{1,0:T(8,128)(2,1)}, f32[64,128]{1,0:T(8,128)}) custom-call(s32[8]{0:T(128)} %get-tuple-element.82.offset_ref, s32[8]{0:T(128)} %get-tuple-element.81.short_ref, s32[64,128]{1,0:T(8,128)} %pad_bitcast_fusion.span_ref, bf16[768,1024]{1,0:T(8,128)(2,1)} %copy-done, bf16[512,1024]{1,0:T(8,128)(2,1)} %collective-permute-done.3.high_ref, ...), custom_call_target="tpu_custom_call" | custom-call | flops 1241513984 | bytes 20971520 | tf_op jit(solution)/shard_map/attention_forward/pallas_call | solution.py:230
  43.8 29.5 %all-gather.2.cloned.1.call-done.weights_ref = bf16[4096,1024]{1,0:T(8,128)(2,1)} async-done(((bf16[128,1024]{1,0:T(8,128)(2,1)}), bf16[4096,1024]{1,0:T(8,128)(2,1)}) %all-gather.2.cloned.1.call-update) | async-done | bytes 8388624 | tf_op jit(solution)/shard_map/all_gather | solution.py:753
  73.3 17.4 %latent.1 = (bf16[512,2048]{1,0:T(8,128)(2,1)}, bf16[512,2048]{1,0:T(8,128)(2,1)}, f32[256,128]{1,0:T(8,128)}) custom-call(s32[4]{0:T(128)} %pad_add_fusion.1.place_ref, bf16[512,1024]{1,0:T(8,128)(2,1)} %get-tuple-element.42.attended_ref, f32[1,4096]{1,0:T(1,128)} %bitcast.56, bf16[512,4096]{1,0:T(8,128)(2,1)} %bitcast.55, ...), custom_call_target="tpu_custom_call" | custom-call | flops 4294967296 | bytes 18874368 | tf_op jit(solution)/shard_map/latent/pallas_call | solution.py:404
  91.3 0.9 slice.60
  92.6 8.5 %d_attended.1.after_ref.d_attended_ref = bf16[512,1024]{1,0:T(8,128)(2,1)} custom-call(s32[4]{0:T(128)} %pad_add_fusion.1.place_ref, bf16[512,2048]{1,0:T(8,128)(2,1)} %get-tuple-element.43.mine_ref, bf16[512,2048]{1,0:T(8,128)(2,1)} %get-tuple-element.44.other_ref, bf16[4096,1024]{1,0:T(8,128)(2,1)} %all-gather.2.cloned.1.call-done.weights_ref), custom_call_target="tpu_custom_call" | custom-call | flops 4294967296 | bytes 14680064 | tf_op jit(solution)/shard_map/d_attended/pallas_call | solution.py:465
  101.7 1.3 copy-done.17
  103.1 8.7 %d_proj.1 = (bf16[1040,512]{1,0:T(8,128)(2,1)}, bf16[1040,512]{1,0:T(8,128)(2,1)}, bf16[1040,512]{1,0:T(8,128)(2,1)}, bf16[1040,512]{1,0:T(8,128)(2,1)}) custom-call(bf16[512,2048]{1,0:T(8,128)(2,1)} %get-tuple-element.43.mine_ref, bf16[512,2048]{1,0:T(8,128)(2,1)} %copy-done.17, bf16[512,1024]{1,0:T(8,128)(2,1)} %get-tuple-element.42.attended_ref, ...), custom_call_target="tpu_custom_call" | custom-call | flops 4294967296 | bytes 12582912 | tf_op jit(solution)/shard_map/d_proj/pallas_call | solution.py:522
  111.8 1.2 collective-permute-start.7
  113.0 2.9 %collective-permute-start.8 = (bf16[1040,512]{1,0:T(8,128)(2,1)}, bf16[1040,512]{1,0:T(8,128)(2,1)S(1)}, u32[]{:S(2)}, u32[]{:S(2)}) collective-permute-start(bf16[1040,512]{1,0:T(8,128)(2,1)} %get-tuple-element.48), channel_id=1, source_target_pairs={{0,16},{1,5},{2,18},{3,7},{4,20},{5,1},{6,22},{7,3},{8,24},{9,13},... | collective-permute-start | bytes 3194888 | tf_op jit(solution)/shard_map/ppermute | solution.py:612
  115.8 1.4 collective-permute-start.9
  117.2 24.6 %attention_backward.1 = (bf16[512,1024]{1,0:T(8,128)(2,1)}, bf16[2048,1024]{1,0:T(8,128)(2,1)}, bf16[2048,1024]{1,0:T(8,128)(2,1)}, bf16[768,1024]{1,0:T(8,128)(2,1)}, bf16[512,1024]{1,0:T(8,128)(2,1)}) custom-call(s32[8]{0:T(128)} %get-tuple-element.82.offset_ref, s32[8]{0:T(128)} %get-tuple-element.81.short_ref, s32[64,128]{1,0:T(8,128)} %pad_bitcast_fusion.span_ref, ...), custom_call_target="tpu_custom_call" | custom-call | flops 4345298944 | bytes 41943040 | tf_op jit(solution)/shard_map/attention_backward/pallas_call | solution.py:264
  141.8 1.0 copy-done.2
  143.5 3.4 %first_sum.1 = (bf16[272,512]{1,0:T(8,128)(2,1)}, bf16[272,512]{1,0:T(8,128)(2,1)}, bf16[272,512]{1,0:T(8,128)(2,1)}, bf16[272,512]{1,0:T(8,128)(2,1)}) custom-call(s32[4]{0:T(128)} %pad_add_fusion.1.place_ref, bf16[1040,512]{1,0:T(8,128)(2,1)} %get-tuple-element.55.after_ref.refs_0_, bf16[1040,512]{1,0:T(8,128)(2,1)} %copy-done.2, ...), custom_call_target="tpu_custom_call" | custom-call | tf_op jit(solution)/shard_map/first_sum/pallas_call | solution.py:646
  146.9 1.3 collective-permute-start.11
  148.2 3.1 %collective-permute-start.10 = (bf16[512,1024]{1,0:T(8,128)(2,1)}, bf16[512,1024]{1,0:T(8,128)(2,1)S(1)}, u32[]{:S(2)}, u32[]{:S(2)}) collective-permute-start(bf16[512,1024]{1,0:T(8,128)(2,1)} %get-tuple-element.65), channel_id=1, source_target_pairs={{0,1},{1,2},{2,3},{3,4},{4,5},{5,6},{6,7},{7,8},{8,9},{9,10},{10,1... | collective-permute-start | bytes 3145736 | tf_op jit(solution)/shard_map/ppermute | solution.py:789
  151.3 1.6 collective-permute-start.12
  152.9 2.7 %collective-permute-start.13 = (bf16[272,512]{1,0:T(8,128)(2,1)}, bf16[272,512]{1,0:T(8,128)(2,1)S(1)}, u32[]{:S(2)}, u32[]{:S(2)}) collective-permute-start(bf16[272,512]{1,0:T(8,128)(2,1)} %get-tuple-element.71), channel_id=1, source_target_pairs={{0,64},{32,96},{64,0},{96,32},{1,65},{33,97},{65,1},{97,33},{2,66}... | collective-permute-start | bytes 835592 | tf_op jit(solution)/shard_map/ppermute | solution.py:731
  155.6 1.4 collective-permute-start.14
  157.0 5.2 %collective-permute-done.12.refs_1_ = bf16[272,512]{1,0:T(8,128)(2,1)S(1)} collective-permute-done((bf16[272,512]{1,0:T(8,128)(2,1)}, bf16[272,512]{1,0:T(8,128)(2,1)S(1)}, u32[]{:S(2)}, u32[]{:S(2)}) %collective-permute-start.12) | collective-permute-done | bytes 278560 | tf_op jit(solution)/shard_map/ppermute | solution.py:731
  162.2 6.9 %collective-permute-done.13.refs_2_ = bf16[272,512]{1,0:T(8,128)(2,1)S(1)} collective-permute-done((bf16[272,512]{1,0:T(8,128)(2,1)}, bf16[272,512]{1,0:T(8,128)(2,1)S(1)}, u32[]{:S(2)}, u32[]{:S(2)}) %collective-permute-start.13) | collective-permute-done | bytes 278560 | tf_op jit(solution)/shard_map/ppermute | solution.py:731
  169.2 0.7 copy-done.7
  169.9 0.7 copy-done.8
  170.6 2.0 %second_sum.1 = (bf16[320,128]{1,0:T(8,128)(2,1)}, bf16[320,128]{1,0:T(8,128)(2,1)}, bf16[320,128]{1,0:T(8,128)(2,1)}, bf16[320,128]{1,0:T(8,128)(2,1)}) custom-call(bf16[272,512]{1,0:T(8,128)(2,1)} %get-tuple-element.69.refs_0_, bf16[272,512]{1,0:T(8,128)(2,1)} %copy-done.6, bf16[272,512]{1,0:T(8,128)(2,1)} %copy-done.7, bf16[272,512]{1,0:T(8,128)(2,1)} %copy-done.8), custom_call_target="tpu_custom_call" | custom-call | tf_op jit(solution)/shard_map/second_sum/pallas_call | solution.py:673
  173.2 1.5 collective-permute-start.16
  174.7 2.1 %collective-permute-start.17 = (bf16[320,128]{1,0:T(8,128)(2,1)}, bf16[320,128]{1,0:T(8,128)(2,1)S(1)}, u32[]{:S(2)}, u32[]{:S(2)}) collective-permute-start(bf16[320,128]{1,0:T(8,128)(2,1)} %get-tuple-element.76), channel_id=1, source_target_pairs={{0,6},{1,25},{2,0},{3,27},{4,2},{5,29},{6,4},{7,31},{8,14},{9,1},{... | collective-permute-start | bytes 245768 | tf_op jit(solution)/shard_map/ppermute | solution.py:612
  176.8 1.6 collective-permute-done.15.refs_1_
  178.5 0.9 collective-permute-done.16.refs_2_
  179.4 0.8 collective-permute-done.17.refs_3_
  180.8 1.7 last_sum.1
  182.5 1.8 collective-permute-start.20
  184.3 1.2 collective-permute-start.19
  185.9 1.0 copy-done.5
  187.4 4.6 %rims.1 = (bf16[2048,1024]{1,0:T(8,128)(2,1)}, bf16[2048,1024]{1,0:T(8,128)(2,1)}) custom-call(bf16[2048,1024]{1,0:T(8,128)(2,1)} %get-tuple-element.53.key_in, bf16[2048,1024]{1,0:T(8,128)(2,1)} %get-tuple-element.54.value_in, bf16[512,1024]{1,0:T(8,128)(2,1)} %copy-done.5, bf16[768,1024]{1,0:T(8,128)(2,1)} %copy-done.1), custom_call_target="tpu_custom_call", output_to_operand_aliasing={{0}: (0, {}), {1}: (1, {})} | custom-call | tf_op jit(solution)/shard_map/rims/pallas_call | solution.py:581
  192.7 1.9 d_proj_rows.1
  (72 shorter events, 8.2 us)
Async XLA Ops:
  7.2 66.1 %all-gather.2.cloned.1.call-start = ((), (), s32[]{:S(2)}) async-start(), calls=%async_computation | async-start | bytes 8650752 | tf_op jit(solution)/shard_map/all_gather | solution.py:753
  8.6 15.7 %collective-permute-start.1 = (s32[256]{0:T(256)S(1)}, s32[256]{0:T(256)S(1)}, u32[]{:S(2)}, u32[]{:S(2)}) collective-permute-start(s32[256]{0:T(256)S(1)} %bitcast.54), channel_id=1, source_target_pairs={{1,0},{2,1},{3,2},{4,3},{5,4},{6,5},{7,6},{8,7},{9,8},{10,9},{11,1... | collective-permute-start | bytes 3080 | tf_op jit(solution)/shard_map/ppermute | solution.py:749
  10.6 13.8 %collective-permute-start = (s32[384]{0:T(512)S(1)}, s32[384]{0:T(512)S(1)}, u32[]{:S(2)}, u32[]{:S(2)}) collective-permute-start(s32[384]{0:T(512)S(1)} %slice_reduce_fusion), channel_id=1, source_target_pairs={{0,1},{1,2},{2,3},{3,4},{4,5},{5,6},{6,7},{7,8},{8,9},{9,10},{10,1... | collective-permute-start | bytes 4616 | tf_op jit(solution)/shard_map/ppermute | solution.py:748
  15.9 6.9 %copy-start.16 = (s32[1,512]{1,0:T(1,128)S(1)}, s32[1,512]{1,0:T(1,128)}, u32[]{:S(2)}) copy-start(s32[1,512]{1,0:T(1,128)} %param.12) | copy-start | bytes 6148
  15.9 8.4 %copy-start.15 = (s32[1,2048]{1,0:T(1,128)S(1)}, s32[1,2048]{1,0:T(1,128)}, u32[]{:S(2)}) copy-start(s32[1,2048]{1,0:T(1,128)} %param.10) | copy-start | bytes 24580
  15.9 12.7 %collective-permute-start.3 = (bf16[512,1024]{1,0:T(8,128)(2,1)}, bf16[512,1024]{1,0:T(8,128)(2,1)}, u32[]{:S(2)}, u32[]{:S(2)}) collective-permute-start(bf16[512,1024]{1,0:T(8,128)(2,1)} %pad_maximum_fusion.1), channel_id=1, source_target_pairs={{1,0},{2,1},{3,2},{4,3},{5,4},{6,5},{7,6},{8,7},{9,8},{10,9},{11,1... | collective-permute-start | bytes 3145736 | tf_op jit(solution)/shard_map/ppermute | solution.py:752
  19.0 9.7 %collective-permute-start.2 = (bf16[768,1024]{1,0:T(8,128)(2,1)S(1)}, bf16[768,1024]{1,0:T(8,128)(2,1)S(1)}, u32[]{:S(2)}, u32[]{:S(2)}) collective-permute-start(bf16[768,1024]{1,0:T(8,128)(2,1)S(1)} %pad_maximum_fusion), channel_id=1, source_target_pairs={{0,1},{1,2},{2,3},{3,4},{4,5},{5,6},{6,7},{7,8},{8,9},{9,10},{10,1... | collective-permute-start | bytes 4718600 | tf_op jit(solution)/shard_map/ppermute | solution.py:752
  28.7 1.2 copy-start
  73.3 17.7 %copy-start.18 = (bf16[512,1024]{1,0:T(8,128)(2,1)S(1)}, bf16[512,1024]{1,0:T(8,128)(2,1)}, u32[]{:S(2)}) copy-start(bf16[512,1024]{1,0:T(8,128)(2,1)} %get-tuple-element.42.attended_ref) | copy-start | bytes 3145732
  90.6 11.1 %collective-permute-start.4 = (bf16[512,2048]{1,0:T(8,128)(2,1)}, bf16[512,2048]{1,0:T(8,128)(2,1)S(1)}, u32[]{:S(2)}, u32[]{:S(2)}) collective-permute-start(bf16[512,2048]{1,0:T(8,128)(2,1)} %get-tuple-element.44.other_ref), channel_id=1, source_target_pairs={{0,1},{1,0},{2,3},{3,2},{4,5},{5,4},{6,7},{7,6},{8,9},{9,8},{10,11... | collective-permute-start | bytes 6291464 | tf_op jit(solution)/shard_map/ppermute | solution.py:607
  91.0 10.7 %collective-permute-start.5 = (bf16[512,1024]{1,0:T(8,128)(2,1)S(1)}, bf16[512,1024]{1,0:T(8,128)(2,1)}, u32[]{:S(2)}, u32[]{:S(2)}) collective-permute-start(bf16[512,1024]{1,0:T(8,128)(2,1)S(1)} %copy-done.18), channel_id=1, source_target_pairs={{0,1},{1,0},{2,3},{3,2},{4,5},{5,4},{6,7},{7,6},{8,9},{9,8},{10,11... | collective-permute-start | bytes 3145736 | tf_op jit(solution)/shard_map/ppermute | solution.py:607
  92.2 8.9 %collective-permute-start.6 = (f32[8,512]{1,0:T(8,128)S(1)}, f32[8,512]{1,0:T(8,128)S(1)}, u32[]{:S(2)}, u32[]{:S(2)}) collective-permute-start(f32[8,512]{1,0:T(8,128)S(1)} %bitcast.45), channel_id=1, source_target_pairs={{0,1},{1,0},{2,3},{3,2},{4,5},{5,4},{6,7},{7,6},{8,9},{9,8},{10,11... | collective-permute-start | bytes 49160 | tf_op jit(solution)/shard_map/ppermute | solution.py:607
  101.7 1.3 copy-start.17
  111.8 30.0 %collective-permute-start.7 = (bf16[1040,512]{1,0:T(8,128)(2,1)}, bf16[1040,512]{1,0:T(8,128)(2,1)S(1)}, u32[]{:S(2)}, u32[]{:S(2)}) collective-permute-start(bf16[1040,512]{1,0:T(8,128)(2,1)} %get-tuple-element.47), channel_id=1, source_target_pairs={{0,8},{1,3},{2,10},{3,5},{4,12},{5,7},{6,14},{7,1},{8,16},{9,11},{... | collective-permute-start | bytes 3194888 | tf_op jit(solution)/shard_map/ppermute | solution.py:612
  113.0 28.8 %collective-permute-start.8 = (bf16[1040,512]{1,0:T(8,128)(2,1)}, bf16[1040,512]{1,0:T(8,128)(2,1)S(1)}, u32[]{:S(2)}, u32[]{:S(2)}) collective-permute-start(bf16[1040,512]{1,0:T(8,128)(2,1)} %get-tuple-element.48), channel_id=1, source_target_pairs={{0,16},{1,5},{2,18},{3,7},{4,20},{5,1},{6,22},{7,3},{8,24},{9,13},... | collective-permute-start | bytes 3194888 | tf_op jit(solution)/shard_map/ppermute | solution.py:612
  115.8 26.0 %collective-permute-start.9 = (bf16[1040,512]{1,0:T(8,128)(2,1)}, bf16[1040,512]{1,0:T(8,128)(2,1)S(1)}, u32[]{:S(2)}, u32[]{:S(2)}) collective-permute-start(bf16[1040,512]{1,0:T(8,128)(2,1)} %get-tuple-element.49), channel_id=1, source_target_pairs={{0,24},{1,7},{2,26},{3,1},{4,28},{5,3},{6,30},{7,5},{8,0},{9,15},{... | collective-permute-start | bytes 3194888 | tf_op jit(solution)/shard_map/ppermute | solution.py:612
  141.8 1.0 copy-start.2
  141.8 1.3 copy-start.3
  141.8 1.7 copy-start.4
  146.9 39.0 %collective-permute-start.11 = (bf16[768,1024]{1,0:T(8,128)(2,1)}, bf16[768,1024]{1,0:T(8,128)(2,1)S(1)}, u32[]{:S(2)}, u32[]{:S(2)}) collective-permute-start(bf16[768,1024]{1,0:T(8,128)(2,1)} %get-tuple-element.66), channel_id=1, source_target_pairs={{1,0},{2,1},{3,2},{4,3},{5,4},{6,5},{7,6},{8,7},{9,8},{10,9},{11,1... | collective-permute-start | bytes 4718600 | tf_op jit(solution)/shard_map/ppermute | solution.py:788
  148.2 37.7 %collective-permute-start.10 = (bf16[512,1024]{1,0:T(8,128)(2,1)}, bf16[512,1024]{1,0:T(8,128)(2,1)S(1)}, u32[]{:S(2)}, u32[]{:S(2)}) collective-permute-start(bf16[512,1024]{1,0:T(8,128)(2,1)} %get-tuple-element.65), channel_id=1, source_target_pairs={{0,1},{1,2},{2,3},{3,4},{4,5},{5,6},{6,7},{7,8},{8,9},{9,10},{10,1... | collective-permute-start | bytes 3145736 | tf_op jit(solution)/shard_map/ppermute | solution.py:789
  151.3 10.9 %collective-permute-start.12 = (bf16[272,512]{1,0:T(8,128)(2,1)}, bf16[272,512]{1,0:T(8,128)(2,1)S(1)}, u32[]{:S(2)}, u32[]{:S(2)}) collective-permute-start(bf16[272,512]{1,0:T(8,128)(2,1)} %get-tuple-element.70), channel_id=1, source_target_pairs={{0,32},{32,64},{64,96},{96,0},{1,33},{33,65},{65,97},{97,1},{2,34}... | collective-permute-start | bytes 835592 | tf_op jit(solution)/shard_map/ppermute | solution.py:731
  152.9 16.3 %collective-permute-start.13 = (bf16[272,512]{1,0:T(8,128)(2,1)}, bf16[272,512]{1,0:T(8,128)(2,1)S(1)}, u32[]{:S(2)}, u32[]{:S(2)}) collective-permute-start(bf16[272,512]{1,0:T(8,128)(2,1)} %get-tuple-element.71), channel_id=1, source_target_pairs={{0,64},{32,96},{64,0},{96,32},{1,65},{33,97},{65,1},{97,33},{2,66}... | collective-permute-start | bytes 835592 | tf_op jit(solution)/shard_map/ppermute | solution.py:731
  155.6 13.5 %collective-permute-start.14 = (bf16[272,512]{1,0:T(8,128)(2,1)}, bf16[272,512]{1,0:T(8,128)(2,1)S(1)}, u32[]{:S(2)}, u32[]{:S(2)}) collective-permute-start(bf16[272,512]{1,0:T(8,128)(2,1)} %get-tuple-element.72), channel_id=1, source_target_pairs={{0,96},{32,0},{64,32},{96,64},{1,97},{33,1},{65,33},{97,65},{2,98}... | collective-permute-start | bytes 835592 | tf_op jit(solution)/shard_map/ppermute | solution.py:731
  162.2 6.9 %copy-start.6 = (bf16[272,512]{1,0:T(8,128)(2,1)}, bf16[272,512]{1,0:T(8,128)(2,1)S(1)}, u32[]{:S(2)}) copy-start(bf16[272,512]{1,0:T(8,128)(2,1)S(1)} %collective-permute-done.12.refs_1_) | copy-start | bytes 835588
  169.1 0.7 copy-start.7
  169.8 0.7 copy-start.8
  172.6 5.9 %collective-permute-start.15 = (bf16[320,128]{1,0:T(8,128)(2,1)}, bf16[320,128]{1,0:T(8,128)(2,1)S(1)}, u32[]{:S(2)}, u32[]{:S(2)}) collective-permute-start(bf16[320,128]{1,0:T(8,128)(2,1)} %get-tuple-element.74), channel_id=1, source_target_pairs={{0,2},{1,9},{2,4},{3,11},{4,6},{5,13},{6,0},{7,15},{8,10},{9,17},{... | collective-permute-start | bytes 245768 | tf_op jit(solution)/shard_map/ppermute | solution.py:612
  173.2 6.2 %collective-permute-start.16 = (bf16[320,128]{1,0:T(8,128)(2,1)}, bf16[320,128]{1,0:T(8,128)(2,1)S(1)}, u32[]{:S(2)}, u32[]{:S(2)}) collective-permute-start(bf16[320,128]{1,0:T(8,128)(2,1)} %get-tuple-element.75), channel_id=1, source_target_pairs={{0,4},{1,17},{2,6},{3,19},{4,0},{5,21},{6,2},{7,23},{8,12},{9,25},... | collective-permute-start | bytes 245768 | tf_op jit(solution)/shard_map/ppermute | solution.py:612
  174.7 5.5 %collective-permute-start.17 = (bf16[320,128]{1,0:T(8,128)(2,1)}, bf16[320,128]{1,0:T(8,128)(2,1)S(1)}, u32[]{:S(2)}, u32[]{:S(2)}) collective-permute-start(bf16[320,128]{1,0:T(8,128)(2,1)} %get-tuple-element.76), channel_id=1, source_target_pairs={{0,6},{1,25},{2,0},{3,27},{4,2},{5,29},{6,4},{7,31},{8,14},{9,1},{... | collective-permute-start | bytes 245768 | tf_op jit(solution)/shard_map/ppermute | solution.py:612
  178.5 1.7 copy-start.9
  179.4 0.8 copy-start.10
  180.2 0.6 copy-start.11
  182.5 9.5 %collective-permute-start.20 = (bf16[256,128]{1,0:T(8,128)(2,1)}, bf16[256,128]{1,0:T(8,128)(2,1)S(1)}, u32[]{:S(2)}, u32[]{:S(2)}) collective-permute-start(bf16[256,128]{1,0:T(8,128)(2,1)} %get-tuple-element.77.refs_0_), channel_id=1, source_target_pairs={{0,96},{32,0},{64,32},{96,64},{1,97},{33,1},{65,33},{97,65},{2,98}... | collective-permute-start | bytes 196616 | tf_op jit(solution)/shard_map/ppermute | solution.py:731
  184.3 7.7 %collective-permute-start.19 = (bf16[256,128]{1,0:T(8,128)(2,1)}, bf16[256,128]{1,0:T(8,128)(2,1)S(1)}, u32[]{:S(2)}, u32[]{:S(2)}) collective-permute-start(bf16[256,128]{1,0:T(8,128)(2,1)} %get-tuple-element.77.refs_0_), channel_id=1, source_target_pairs={{0,64},{32,96},{64,0},{96,32},{1,65},{33,97},{65,1},{97,33},{2,66}... | collective-permute-start | bytes 196616 | tf_op jit(solution)/shard_map/ppermute | solution.py:731
  185.5 6.5 %collective-permute-start.18 = (bf16[256,128]{1,0:T(8,128)(2,1)}, bf16[256,128]{1,0:T(8,128)(2,1)S(1)}, u32[]{:S(2)}, u32[]{:S(2)}) collective-permute-start(bf16[256,128]{1,0:T(8,128)(2,1)} %get-tuple-element.77.refs_0_), channel_id=1, source_target_pairs={{0,32},{32,64},{64,96},{96,0},{1,33},{33,65},{65,97},{97,1},{2,34}... | collective-permute-start | bytes 196616 | tf_op jit(solution)/shard_map/ppermute | solution.py:731
  185.9 1.0 copy-start.5
  185.9 1.5 copy-start.1
  192.0 0.6 copy-start.12
  192.0 0.6 copy-start.13
  192.0 0.6 copy-start.14
Sparse Core Ops, SparseCore 0:
  10.3 62.9 all-gather.1

commit v5 on v4

--- a/solution.py
+++ b/solution.py
@@ -312,8 +312,8 @@
 
 def latent_kernel(
     place_ref, attended_ref, norm_ref, cotangent_ref, weights_ref,
-    mine_ref, other_ref, gain_ref,
-    weight, cotangent, latent, square, mixed, mine, other, sems,
+    mine_ref, other_ref, gain_ref, d_attended_ref,
+    weight, cotangent, latent, square, mixed, mine, other, total, sems,
 ):
     pieces = fetch_weights(place_ref, weights_ref, weight, sems)
     rows_each = cotangent.shape[0] // 8
@@ -393,8 +393,18 @@
         copy.start()
         return copy
 
-    copies = [finish(slab, mine, mine_ref) for slab in range(4)]
-    copies += [finish(slab, other, other_ref) for slab in range(4, 8)]
+    copies = []
+    for part in range(4):
+        staged, out_ref = (mine, mine_ref) if part < 2 else (other, other_ref)
+        copies += [finish(slab, staged, out_ref) for slab in (2 * part, 2 * part + 1)]
+        columns = slice(part % 2 * 1024, part % 2 * 1024 + 1024)
+        terms = dot(staged[:, columns], weight[part * 1024 : part * 1024 + 1024, :])
+        if part == 0:
+            total[...] = terms
+        elif part < 3:
+            total[...] += terms
+        else:
+            d_attended_ref[...] = (total[...] + terms).astype(bf16)
     for copy in copies:
         copy.wait()
 
@@ -407,12 +417,13 @@
             jax.ShapeDtypeStruct((patches, count // 2), bf16),
             jax.ShapeDtypeStruct((patches, count // 2), bf16),
             jax.ShapeDtypeStruct((count // LANES * 8, LANES), f32),
+            jax.ShapeDtypeStruct(attended.shape, bf16),
         ],
         in_specs=[pl.BlockSpec(memory_space=pltpu.SMEM)]
         + [pl.BlockSpec(memory_space=pltpu.VMEM)] * 2
         + [pl.BlockSpec(memory_space=pl.ANY)] * 2,
         out_specs=[pl.BlockSpec(memory_space=pl.ANY)] * 2
-        + [pl.BlockSpec(memory_space=pltpu.VMEM)],
+        + [pl.BlockSpec(memory_space=pltpu.VMEM)] * 2,
         scratch_shapes=[
             pltpu.VMEM(weights.shape, bf16),
             pltpu.VMEM((patches, count), bf16),
@@ -421,69 +432,19 @@
             pltpu.VMEM((patches, LANES), f32),
             pltpu.VMEM((patches, count // 2), bf16),
             pltpu.VMEM((patches, count // 2), bf16),
+            pltpu.VMEM(attended.shape, f32),
             pltpu.SemaphoreType.DMA((48,)),
         ],
         compiler_params=pltpu.CompilerParams(vmem_limit_bytes=VMEM_GRANT),
         cost_estimate=pl.CostEstimate(
-            flops=2 * patches * count * 1024, bytes_accessed=18 * MIB, transcendentals=patches
+            flops=4 * patches * count * 1024, bytes_accessed=18 * MIB, transcendentals=patches
         ),
         name="latent",
     )(place, attended, norm_gain, cotangent, weights)
 
 
-def d_attended_kernel(
-    place_ref, mine_ref, other_ref, weights_ref, out_ref, d_latent, weight, total, sems
-):
-    half = mine_ref.shape[1]
-    pieces = fetch_weights(place_ref, weights_ref, weight, sems)
-    copies = [
-        pltpu.make_async_copy(
-            (mine_ref, other_ref)[part // 2].at[:, pl.ds(part % 2 * half // 2, half // 2)],
-            d_latent.at[part],
-            sems.at[32 + part],
-        )
-        for part in range(4)
-    ]
-    for part in range(4):
-        copies[part].start()
-        for copy in pieces[2 * part] + pieces[2 * part + 1]:
-            copy.start()
-    for part in range(4):
-        for copy in [copies[part]] + pieces[2 * part] + pieces[2 * part + 1]:
-            copy.wait()
-        terms = dot(d_latent[part], weight[part * 1024 : part * 1024 + 1024, :])
-        if part == 0:
-            total[...] = terms
-        elif part < 3:
-            total[...] += terms
-        else:
-            out_ref[...] = (total[...] + terms).astype(bf16)
-
-
-def d_attended_call(place, mine, other, weights):
-    patches, width = mine.shape[0], weights.shape[1]
-    return pl.pallas_call(
-        d_attended_kernel,
-        out_shape=jax.ShapeDtypeStruct((patches, width), bf16),
-        in_specs=[pl.BlockSpec(memory_space=pltpu.SMEM)]
-        + [pl.BlockSpec(memory_space=pl.ANY)] * 3,
-        out_specs=pl.BlockSpec(memory_space=pltpu.VMEM),
-        scratch_shapes=[
-            pltpu.VMEM((4, patches, mine.shape[1] // 2), bf16),
-            pltpu.VMEM(weights.shape, bf16),
-            pltpu.VMEM((patches, width), f32),
-            pltpu.SemaphoreType.DMA((36,)),
-        ],
-        compiler_params=pltpu.CompilerParams(vmem_limit_bytes=VMEM_GRANT),
-        cost_estimate=pl.CostEstimate(
-            flops=4 * patches * mine.shape[1] * width, bytes_accessed=14 * MIB, transcendentals=0
-        ),
-        name="d_attended",
-    )(place, mine, other, weights)
-
-
 def d_proj_kernel(
-    mine_ref, peer_ref, attended_ref, peer_attended_ref, gain_ref, after_ref, *refs
+    mine_ref, peer_ref, attended_ref, peer_attended_ref, gain_ref, *refs
 ):
     outs, (d_latent, rows, turned, staged, sems) = refs[:4], refs[4:]
     patches, width = attended_ref.shape
@@ -516,13 +477,13 @@
         copy.wait()
 
 
-def d_proj_call(mine, peer, attended, peer_attended, gain, after):
+def d_proj_call(mine, peer, attended, peer_attended, gain):
     patches, width = attended.shape
     vmem, anywhere = pl.BlockSpec(memory_space=pltpu.VMEM), pl.BlockSpec(memory_space=pl.ANY)
     return pl.pallas_call(
         d_proj_kernel,
         out_shape=[jax.ShapeDtypeStruct((width + 16, 512), bf16)] * 4,
-        in_specs=[anywhere] * 4 + [vmem, anywhere],
+        in_specs=[anywhere] * 4 + [vmem],
         out_specs=[anywhere] * 4,
         scratch_shapes=[
             pltpu.VMEM((4, 2 * patches, 512), bf16),
@@ -536,55 +497,48 @@
             flops=4 * patches * mine.shape[1] * width, bytes_accessed=12 * MIB, transcendentals=0
         ),
         name="d_proj",
-    )(mine, peer, attended, peer_attended, gain, after)
+    )(mine, peer, attended, peer_attended, gain)
 
 
 def rim_kernel(
-    key_in, value_in, below_ref, above_ref, key_out, value_out, key_rim, value_rim, sems
+    key_in, value_in, below_ref, above_ref, key_out, value_out, rims, arriving, sems
 ):
     own = key_in.shape[0]
     places = ((pl.ds(0, HIGH), pl.ds(0, HIGH)), (pl.ds(own - LOW, LOW), pl.ds(HIGH, LOW)))
-
-    def copies(outward):
-        found = []
-        for which, (source, out, rim) in enumerate(
-            ((key_in, key_out, key_rim), (value_in, value_out, value_rim))
-        ):
-            for side, (far, near) in enumerate(places):
-                sem = sems.at[4 * outward + 2 * which + side]
-                if outward:
-                    found.append(pltpu.make_async_copy(rim.at[near], out.at[far], sem))
-                else:
-                    found.append(pltpu.make_async_copy(source.at[far], rim.at[near], sem))
-        return found
-
-    inward, outward = copies(0), copies(1)
-    for copy in inward:
-        copy.start()
-    for which, rim in enumerate((key_rim, value_rim)):
-        inward[2 * which].wait()
-        below = below_ref[which * HIGH : (which + 1) * HIGH, :].astype(f32)
-        rim[:HIGH, :] = (rim[:HIGH, :].astype(f32) + below).astype(bf16)
-        outward[2 * which].start()
-        inward[2 * which + 1].wait()
-        above = above_ref[which * LOW : (which + 1) * LOW, :].astype(f32)
-        rim[HIGH:, :] = (rim[HIGH:, :].astype(f32) + above).astype(bf16)
-        outward[2 * which + 1].start()
-    for copy in outward:
-        copy.wait()
+    steps = []
+    for which, (source, out) in enumerate(((key_in, key_out), (value_in, value_out))):
+        for side, (far, near) in enumerate(places):
+            count = (HIGH, LOW)[side]
+            from_ref = (below_ref, above_ref)[side].at[pl.ds(which * count, count)]
+            rim, other = rims.at[which, near], arriving.at[which, near]
+            sem = 3 * (2 * which + side)
+            inward = [
+                pltpu.make_async_copy(source.at[far], rim, sems.at[sem]),
+                pltpu.make_async_copy(from_ref, other, sems.at[sem + 1]),
+            ]
+            outward = pltpu.make_async_copy(rim, out.at[far], sems.at[sem + 2])
+            for copy in inward:
+                copy.start()
+            steps.append((rim, other, inward, outward))
+    for rim, other, inward, outward in steps:
+        for copy in inward:
+            copy.wait()
+        rim[...] = (rim[...].astype(f32) + other[...].astype(f32)).astype(bf16)
+        outward.start()
+    for *_, outward in steps:
+        outward.wait()
 
 
 def rim_call(d_key, d_value, from_below, from_above):
     width = from_below.shape[1]
     anywhere = pl.BlockSpec(memory_space=pl.ANY)
-    vmem = pl.BlockSpec(memory_space=pltpu.VMEM)
     return pl.pallas_call(
         rim_kernel,
         out_shape=[jax.ShapeDtypeStruct(d_key.shape, bf16)] * 2,
-        in_specs=[anywhere, anywhere, vmem, vmem],
-        out_specs=[anywhere, anywhere],
-        scratch_shapes=[pltpu.VMEM((HIGH + LOW, width), bf16)] * 2
-        + [pltpu.SemaphoreType.DMA((8,))],
+        in_specs=[anywhere] * 4,
+        out_specs=[anywhere] * 2,
+        scratch_shapes=[pltpu.VMEM((2, HIGH + LOW, width), bf16)] * 2
+        + [pltpu.SemaphoreType.DMA((12,))],
         input_output_aliases={0: 0, 1: 1},
         compiler_params=pltpu.CompilerParams(vmem_limit_bytes=VMEM_GRANT),
         name="rims",
@@ -681,14 +635,14 @@
 
 
 def last_sum_kernel(*refs):
-    parts, part_ref, gain_ref = refs[:4], refs[4], refs[5]
+    parts, part_ref, gain_ref = refs[:4], refs[5], refs[6]
     quarter = part_ref.shape[0]
     total = total_of([ref[...] for ref in parts])
     part_ref[...] = total[:quarter, :].astype(bf16)
     gain_ref[...] = joined(total[quarter:, :])
 
 
-def last_sum(parts):
+def last_sum(parts, after):
     quarter = parts[0].shape[0] - 64
     vmem = pl.BlockSpec(memory_space=pltpu.VMEM)
     return pl.pallas_call(
@@ -697,32 +651,31 @@
             jax.ShapeDtypeStruct((quarter, LANES), bf16),
             jax.ShapeDtypeStruct((32, LANES), f32),
         ],
-        in_specs=[vmem] * 4,
+        in_specs=[vmem] * 4 + [pl.BlockSpec(memory_space=pl.ANY)],
         out_specs=[vmem] * 2,
         name="last_sum",
-    )(*parts)
+    )(*parts, after)
 
 
 def finish_kernel(place_ref, *refs):
-    parts, out_ref = refs[:4], refs[5]
+    parts, out_ref = refs[:4], refs[4]
     quarter = parts[0].shape[0]
     for k in range(RING):
         start = pl.multiple_of((place_ref[3] - k + RING) % RING * quarter, quarter)
         out_ref[:, pl.ds(start, quarter)] = parts[k][...].astype(f32).T
 
 
-def finish_call(place, parts, after):
+def finish_call(place, parts):
     quarter = parts[0].shape[0]
     vmem = pl.BlockSpec(memory_space=pltpu.VMEM)
     return pl.pallas_call(
         finish_kernel,
         out_shape=jax.ShapeDtypeStruct((LANES, RING * quarter), f32),
         in_specs=[pl.BlockSpec(memory_space=pltpu.SMEM)]
-        + [vmem] * 4
-        + [pl.BlockSpec(memory_space=pl.ANY)],
+        + [vmem] * 4,
         out_specs=vmem,
         name="d_proj_rows",
-    )(place, *parts, after)
+    )(place, *parts)
 
 
 def stream_ring(values):
@@ -772,12 +725,11 @@
     attended, level = forward_call(common)
     peer_attended = to_peer(attended)
 
-    mine, other, gain = latent_call(place, attended, norm_gain[None], cotangent[0], weights)
+    mine, other, gain, d_attended = latent_call(place, attended, norm_gain[None], cotangent[0], weights)
     peer_mine = to_peer(other)
     gain = gain.reshape(RING, 8, 8, LANES)[:, :, 0].transpose(1, 0, 2).reshape(8, 512)
     gain = gain + to_peer(gain)
-    d_attended = d_attended_call(place, mine, other, weights)
-    to_send = d_proj_call(mine, peer_mine, attended, peer_attended, halves(gain), d_attended)
+    to_send = d_proj_call(mine, peer_mine, attended, peer_attended, halves(gain))
     from_ring = ring(to_send, "first")
 
     inputs = common + (attended, level, d_attended)
@@ -787,9 +739,10 @@
     from_streams = stream_ring(to_send)
     from_above = lax.ppermute(d_low, "seq", downward)
     from_below = lax.ppermute(d_high, "seq", upward)
-    part, gain = last_sum(ring(second_sum(from_streams), "second"))
+    from_ring = ring(second_sum(from_streams), "second")
     d_keys, d_values = rim_call(d_keys, d_values, from_below, from_above)
-    d_proj = finish_call(place, stream_ring([part] * RING), d_keys)
+    part, gain = last_sum(from_ring, d_keys)
+    d_proj = finish_call(place, stream_ring([part] * RING))
     d_gain = gain.reshape(-1)
     return (d_query[None], d_keys[None], d_values[None], d_proj, d_gain)
 

time: 202 us -> 201 us (level)
  Pallas kernels: 86.7 us -> 79 us
  waiting for transfers between devices: 45.7 us -> 51.7 us
    pallas_call x1 -> x0, Pallas kernels: 8.54 us -> none  [d_attended_call(): pl.pallas_call(d_attended_kernel, out_shape=jax.ShapeDtypeStruct((patches...]
    ppermute x6, waiting for transfers between devices: 12.1 us -> 17.3 us  [stream_ring(): lax.ppermute(values[k], 'dp', [(i, (i + k) % count) for i in range(count)])]
    ppermute x3, waiting for transfers between devices: 0.01 us -> 3.8 us  [to_peer(): lax.ppermute(value, 'seq', [(i, i ^ 1) for i in range(lax.axis_size('seq'...]
    ppermute x6, waiting for transfers between devices: 3.39 us -> 0.02 us  [ring(): lax.ppermute(values[k], 'seq', along(which, k))]
    unnamed x38 -> x40, local copies, waits for them, and re-layouts: 8.31 us -> 9.26 us
  transfers between devices with their start and end apart: 22 -> 22, of which waited for: 6 -> 7; matrix products, arithmetic and copies ran while one was open for 6% -> 6% of each run, Pallas kernels for 27% -> 22%
where the time goes in v5:
time: 201 us
  Pallas kernels  79 us (39%)
  waiting for transfers between devices  51.7 us (26%)
  starting transfers between devices  33.8 us (17%)
  local copies, waits for them, and re-layouts  15.9 us (8%)
  between operations  14.4 us (7%)
  other arithmetic  5.89 us (3%)
    all_gather x1, waiting for transfers between devices, on_device(): weights = lax.all_gather(proj_weight, 'seq', axis=0, tiled=True)  29.9 us
    pallas_call x1, Pallas kernels, backward_call(): pl.pallas_call(backward_kernel, out_shape=[jax.ShapeDtypeStruct((count, w...  24.5 us
    pallas_call x1, Pallas kernels, latent_call(): pl.pallas_call(latent_kernel, out_shape=[jax.ShapeDtypeStruct((patches, c...  19.2 us
    ppermute x6, waiting for transfers between devices, stream_ring(): lax.ppermute(values[k], 'dp', [(i, (i + k) % count) for i in range(count)])  17.3 us
    pallas_call x1, Pallas kernels, forward_call(): pl.pallas_call(forward_kernel, out_shape=[jax.ShapeDtypeStruct((patches,...  13.8 us
    ppermute x6, starting transfers between devices, ring(): lax.ppermute(values[k], 'seq', along(which, k))  9.69 us
    unnamed x40, local copies, waits for them, and re-layouts  9.26 us
    ppermute x6, starting transfers between devices, stream_ring(): lax.ppermute(values[k], 'dp', [(i, (i + k) % count) for i in range(count)])  9.15 us
  transfers between devices with their start and end apart: 22, of which 7 were waited for; matrix products, arithmetic and copies ran while one was open for 6% of the time, Pallas kernels for 22%

profile of v5, /device:TPU:0, one launch (start us, length us, event | category | flops | bytes accessed | tf_op | source)
XLA Modules:
  0.0 200.7 jit_solution(8376345853685439457)
XLA Ops:
  7.2 0.7 all-gather.2.cloned.1.call-update
  7.9 0.7 slice.49
  8.6 1.3 collective-permute-start.1
  9.9 0.7 slice_reduce_fusion
  10.6 3.0 %collective-permute-start = (s32[384]{0:T(512)S(1)}, s32[384]{0:T(512)S(1)}, u32[]{:S(2)}, u32[]{:S(2)}) collective-permute-start(s32[384]{0:T(512)S(1)} %slice_reduce_fusion), channel_id=1, source_target_pairs={{0,1},{1,2},{2,3},{3,4},{4,5},{5,6},{6,7},{7,8},{8,9},{9,10},{10,1... | collective-permute-start | bytes 4616 | tf_op jit(solution)/shard_map/ppermute | solution.py:701
  13.6 1.3 slice_bitcast_fusion.2
  14.9 1.0 pad_maximum_fusion.1
  15.9 1.4 collective-permute-start.3
  17.3 1.5 slice_bitcast_fusion
  19.0 3.8 %collective-permute-start.2 = (bf16[768,1024]{1,0:T(8,128)(2,1)S(1)}, bf16[768,1024]{1,0:T(8,128)(2,1)S(1)}, u32[]{:S(2)}, u32[]{:S(2)}) collective-permute-start(bf16[768,1024]{1,0:T(8,128)(2,1)S(1)} %pad_maximum_fusion), channel_id=1, source_target_pairs={{0,1},{1,2},{2,3},{3,4},{4,5},{5,6},{6,7},{7,8},{8,9},{9,10},{10,1... | collective-permute-start | bytes 4718600 | tf_op jit(solution)/shard_map/ppermute | solution.py:705
  24.3 0.9 select_reduce_fusion
  25.2 1.3 convert_reduce_fusion
  28.6 1.1 copy-done
  29.7 13.8 %attention_forward.1 = (bf16[512,1024]{1,0:T(8,128)(2,1)}, f32[64,128]{1,0:T(8,128)}) custom-call(s32[8]{0:T(128)} %get-tuple-element.84.offset_ref, s32[8]{0:T(128)} %get-tuple-element.83.short_ref, s32[64,128]{1,0:T(8,128)} %pad_bitcast_fusion.span_ref, bf16[768,1024]{1,0:T(8,128)(2,1)} %copy-done, bf16[512,1024]{1,0:T(8,128)(2,1)} %collective-permute-done.3.high_ref, ...), custom_call_target="tpu_custom_call" | custom-call | flops 1241513984 | bytes 20971520 | tf_op jit(solution)/shard_map/attention_forward/pallas_call | solution.py:230
  43.5 29.9 %all-gather.2.cloned.1.call-done.weights_ref = bf16[4096,1024]{1,0:T(8,128)(2,1)} async-done(((bf16[128,1024]{1,0:T(8,128)(2,1)}), bf16[4096,1024]{1,0:T(8,128)(2,1)}) %all-gather.2.cloned.1.call-update) | async-done | bytes 8388624 | tf_op jit(solution)/shard_map/all_gather | solution.py:706
  73.4 19.2 %latent.1 = (bf16[512,2048]{1,0:T(8,128)(2,1)}, bf16[512,2048]{1,0:T(8,128)(2,1)}, f32[256,128]{1,0:T(8,128)}, bf16[512,1024]{1,0:T(8,128)(2,1)}) custom-call(s32[4]{0:T(128)} %pad_add_fusion.1.place_ref, bf16[512,1024]{1,0:T(8,128)(2,1)} %get-tuple-element.43.attended_ref, f32[1,4096]{1,0:T(1,128)} %bitcast.56, bf16[512,4096]{1,0:T(8,128)(2,1)} %bitcast.55, ...), custom_call_target="tpu_custom_call" | custom-call | flops 8589934592 | bytes 18874368 | tf_op jit(solution)/shard_map/latent/pallas_call | solution.py:414
  93.4 0.9 slice.60
  94.6 3.8 %collective-permute-done.6 = f32[8,512]{1,0:T(8,128)S(1)} collective-permute-done((f32[8,512]{1,0:T(8,128)S(1)}, f32[8,512]{1,0:T(8,128)S(1)}, u32[]{:S(2)}, u32[]{:S(2)}) %collective-permute-start.6) | collective-permute-done | bytes 16416 | tf_op jit(solution)/shard_map/ppermute | solution.py:561
  99.0 1.0 copy-done.19
  100.0 1.3 copy-done.17
  101.3 8.7 %d_proj.1 = (bf16[1040,512]{1,0:T(8,128)(2,1)}, bf16[1040,512]{1,0:T(8,128)(2,1)}, bf16[1040,512]{1,0:T(8,128)(2,1)}, bf16[1040,512]{1,0:T(8,128)(2,1)}) custom-call(bf16[512,2048]{1,0:T(8,128)(2,1)} %get-tuple-element.44.mine_ref, bf16[512,2048]{1,0:T(8,128)(2,1)} %copy-done.17, bf16[512,1024]{1,0:T(8,128)(2,1)} %get-tuple-element.43.attended_ref, ...), custom_call_target="tpu_custom_call" | custom-call | flops 4294967296 | bytes 12582912 | tf_op jit(solution)/shard_map/d_proj/pallas_call | solution.py:483
  110.0 1.2 collective-permute-start.7
  111.2 2.9 %collective-permute-start.8 = (bf16[1040,512]{1,0:T(8,128)(2,1)}, bf16[1040,512]{1,0:T(8,128)(2,1)S(1)}, u32[]{:S(2)}, u32[]{:S(2)}) collective-permute-start(bf16[1040,512]{1,0:T(8,128)(2,1)} %get-tuple-element.49), channel_id=1, source_target_pairs={{0,16},{1,5},{2,18},{3,7},{4,20},{5,1},{6,22},{7,3},{8,24},{9,13},... | collective-permute-start | bytes 3194888 | tf_op jit(solution)/shard_map/ppermute | solution.py:566
  114.1 1.4 collective-permute-start.9
  115.4 24.5 %attention_backward.1 = (bf16[512,1024]{1,0:T(8,128)(2,1)}, bf16[2048,1024]{1,0:T(8,128)(2,1)}, bf16[2048,1024]{1,0:T(8,128)(2,1)}, bf16[768,1024]{1,0:T(8,128)(2,1)}, bf16[512,1024]{1,0:T(8,128)(2,1)}) custom-call(s32[8]{0:T(128)} %get-tuple-element.84.offset_ref, s32[8]{0:T(128)} %get-tuple-element.83.short_ref, s32[64,128]{1,0:T(8,128)} %pad_bitcast_fusion.span_ref, ...), custom_call_target="tpu_custom_call" | custom-call | flops 4345298944 | bytes 41943040 | tf_op jit(solution)/shard_map/attention_backward/pallas_call | solution.py:264
  140.0 1.0 copy-done.2
  141.7 3.4 %first_sum.1 = (bf16[272,512]{1,0:T(8,128)(2,1)}, bf16[272,512]{1,0:T(8,128)(2,1)}, bf16[272,512]{1,0:T(8,128)(2,1)}, bf16[272,512]{1,0:T(8,128)(2,1)}) custom-call(s32[4]{0:T(128)} %pad_add_fusion.1.place_ref, bf16[1040,512]{1,0:T(8,128)(2,1)} %get-tuple-element.57.after_ref.refs_0_, bf16[1040,512]{1,0:T(8,128)(2,1)} %copy-done.2, ...), custom_call_target="tpu_custom_call" | custom-call | tf_op jit(solution)/shard_map/first_sum/pallas_call | solution.py:600
  145.1 1.3 collective-permute-start.11
  146.4 3.1 %collective-permute-start.10 = (bf16[512,1024]{1,0:T(8,128)(2,1)}, bf16[512,1024]{1,0:T(8,128)(2,1)S(1)}, u32[]{:S(2)}, u32[]{:S(2)}) collective-permute-start(bf16[512,1024]{1,0:T(8,128)(2,1)} %get-tuple-element.67), channel_id=1, source_target_pairs={{0,1},{1,2},{2,3},{3,4},{4,5},{5,6},{6,7},{7,8},{8,9},{9,10},{10,1... | collective-permute-start | bytes 3145736 | tf_op jit(solution)/shard_map/ppermute | solution.py:741
  149.5 1.6 collective-permute-start.12
  151.0 2.8 %collective-permute-start.13 = (bf16[272,512]{1,0:T(8,128)(2,1)}, bf16[272,512]{1,0:T(8,128)(2,1)S(1)}, u32[]{:S(2)}, u32[]{:S(2)}) collective-permute-start(bf16[272,512]{1,0:T(8,128)(2,1)} %get-tuple-element.73), channel_id=1, source_target_pairs={{0,64},{32,96},{64,0},{96,32},{1,65},{33,97},{65,1},{97,33},{2,66}... | collective-permute-start | bytes 835592 | tf_op jit(solution)/shard_map/ppermute | solution.py:684
  153.8 1.4 collective-permute-start.14
  155.3 5.2 %collective-permute-done.12.refs_1_ = bf16[272,512]{1,0:T(8,128)(2,1)S(1)} collective-permute-done((bf16[272,512]{1,0:T(8,128)(2,1)}, bf16[272,512]{1,0:T(8,128)(2,1)S(1)}, u32[]{:S(2)}, u32[]{:S(2)}) %collective-permute-start.12) | collective-permute-done | bytes 278560 | tf_op jit(solution)/shard_map/ppermute | solution.py:684
  160.5 6.9 %collective-permute-done.13.refs_2_ = bf16[272,512]{1,0:T(8,128)(2,1)S(1)} collective-permute-done((bf16[272,512]{1,0:T(8,128)(2,1)}, bf16[272,512]{1,0:T(8,128)(2,1)S(1)}, u32[]{:S(2)}, u32[]{:S(2)}) %collective-permute-start.13) | collective-permute-done | bytes 278560 | tf_op jit(solution)/shard_map/ppermute | solution.py:684
  167.4 0.7 copy-done.7
  168.1 0.7 copy-done.8
  168.9 2.0 second_sum.1
  171.5 1.5 collective-permute-start.16
  173.0 2.1 %collective-permute-start.17 = (bf16[320,128]{1,0:T(8,128)(2,1)}, bf16[320,128]{1,0:T(8,128)(2,1)S(1)}, u32[]{:S(2)}, u32[]{:S(2)}) collective-permute-start(bf16[320,128]{1,0:T(8,128)(2,1)} %get-tuple-element.78), channel_id=1, source_target_pairs={{0,6},{1,25},{2,0},{3,27},{4,2},{5,29},{6,4},{7,31},{8,14},{9,1},{... | collective-permute-start | bytes 245768 | tf_op jit(solution)/shard_map/ppermute | solution.py:566
  175.1 1.0 copy-done.5
  176.6 3.8 %rims.1 = (bf16[2048,1024]{1,0:T(8,128)(2,1)}, bf16[2048,1024]{1,0:T(8,128)(2,1)}) custom-call(bf16[2048,1024]{1,0:T(8,128)(2,1)} %get-tuple-element.55.key_in, bf16[2048,1024]{1,0:T(8,128)(2,1)} %get-tuple-element.56.value_in, bf16[512,1024]{1,0:T(8,128)(2,1)} %copy-done.5, bf16[768,1024]{1,0:T(8,128)(2,1)} %copy-done.1), custom_call_target="tpu_custom_call", output_to_operand_aliasing={{0}: (0, {}), {1}: (1, {})} | custom-call | tf_op jit(solution)/shard_map/rims/pallas_call | solution.py:535
  181.1 1.7 last_sum.1
  182.8 1.7 collective-permute-start.20
  184.5 1.1 collective-permute-start.19
  186.2 1.1 collective-permute-done.20.refs_3_
  187.3 3.2 %collective-permute-done.19.refs_2_ = bf16[256,128]{1,0:T(8,128)(2,1)S(1)} collective-permute-done((bf16[256,128]{1,0:T(8,128)(2,1)}, bf16[256,128]{1,0:T(8,128)(2,1)S(1)}, u32[]{:S(2)}, u32[]{:S(2)}) %collective-permute-start.19) | collective-permute-done | bytes 65568 | tf_op jit(solution)/shard_map/ppermute | solution.py:684
  190.5 0.8 collective-permute-done.18.refs_1_
  192.0 1.9 d_proj_rows.1
  (73 shorter events, 9.0 us)
Async XLA Ops:
  7.2 66.2 %all-gather.2.cloned.1.call-start = ((), (), s32[]{:S(2)}) async-start(), calls=%async_computation | async-start | bytes 8650752 | tf_op jit(solution)/shard_map/all_gather | solution.py:706
  8.6 15.7 %collective-permute-start.1 = (s32[256]{0:T(256)S(1)}, s32[256]{0:T(256)S(1)}, u32[]{:S(2)}, u32[]{:S(2)}) collective-permute-start(s32[256]{0:T(256)S(1)} %bitcast.54), channel_id=1, source_target_pairs={{1,0},{2,1},{3,2},{4,3},{5,4},{6,5},{7,6},{8,7},{9,8},{10,9},{11,1... | collective-permute-start | bytes 3080 | tf_op jit(solution)/shard_map/ppermute | solution.py:702
  10.6 13.7 %collective-permute-start = (s32[384]{0:T(512)S(1)}, s32[384]{0:T(512)S(1)}, u32[]{:S(2)}, u32[]{:S(2)}) collective-permute-start(s32[384]{0:T(512)S(1)} %slice_reduce_fusion), channel_id=1, source_target_pairs={{0,1},{1,2},{2,3},{3,4},{4,5},{5,6},{6,7},{7,8},{8,9},{9,10},{10,1... | collective-permute-start | bytes 4616 | tf_op jit(solution)/shard_map/ppermute | solution.py:701
  15.9 6.9 %copy-start.16 = (s32[1,512]{1,0:T(1,128)S(1)}, s32[1,512]{1,0:T(1,128)}, u32[]{:S(2)}) copy-start(s32[1,512]{1,0:T(1,128)} %param.12) | copy-start | bytes 6148
  15.9 8.4 %copy-start.15 = (s32[1,2048]{1,0:T(1,128)S(1)}, s32[1,2048]{1,0:T(1,128)}, u32[]{:S(2)}) copy-start(s32[1,2048]{1,0:T(1,128)} %param.10) | copy-start | bytes 24580
  15.9 12.7 %collective-permute-start.3 = (bf16[512,1024]{1,0:T(8,128)(2,1)}, bf16[512,1024]{1,0:T(8,128)(2,1)}, u32[]{:S(2)}, u32[]{:S(2)}) collective-permute-start(bf16[512,1024]{1,0:T(8,128)(2,1)} %pad_maximum_fusion.1), channel_id=1, source_target_pairs={{1,0},{2,1},{3,2},{4,3},{5,4},{6,5},{7,6},{8,7},{9,8},{10,9},{11,1... | collective-permute-start | bytes 3145736 | tf_op jit(solution)/shard_map/ppermute | solution.py:705
  19.0 9.6 %collective-permute-start.2 = (bf16[768,1024]{1,0:T(8,128)(2,1)S(1)}, bf16[768,1024]{1,0:T(8,128)(2,1)S(1)}, u32[]{:S(2)}, u32[]{:S(2)}) collective-permute-start(bf16[768,1024]{1,0:T(8,128)(2,1)S(1)} %pad_maximum_fusion), channel_id=1, source_target_pairs={{0,1},{1,2},{2,3},{3,4},{4,5},{5,6},{6,7},{7,8},{8,9},{9,10},{10,1... | collective-permute-start | bytes 4718600 | tf_op jit(solution)/shard_map/ppermute | solution.py:705
  28.6 1.1 copy-start
  73.4 19.7 %copy-start.18 = (bf16[512,1024]{1,0:T(8,128)(2,1)S(1)}, bf16[512,1024]{1,0:T(8,128)(2,1)}, u32[]{:S(2)}) copy-start(bf16[512,1024]{1,0:T(8,128)(2,1)} %get-tuple-element.43.attended_ref) | copy-start | bytes 3145732
  92.6 6.4 %collective-permute-start.4 = (bf16[512,2048]{1,0:T(8,128)(2,1)}, bf16[512,2048]{1,0:T(8,128)(2,1)S(1)}, u32[]{:S(2)}, u32[]{:S(2)}) collective-permute-start(bf16[512,2048]{1,0:T(8,128)(2,1)} %get-tuple-element.45), channel_id=1, source_target_pairs={{0,1},{1,0},{2,3},{3,2},{4,5},{5,4},{6,7},{7,6},{8,9},{9,8},{10,11... | collective-permute-start | bytes 6291464 | tf_op jit(solution)/shard_map/ppermute | solution.py:561
  93.1 5.9 %collective-permute-start.5 = (bf16[512,1024]{1,0:T(8,128)(2,1)S(1)}, bf16[512,1024]{1,0:T(8,128)(2,1)S(1)}, u32[]{:S(2)}, u32[]{:S(2)}) collective-permute-start(bf16[512,1024]{1,0:T(8,128)(2,1)S(1)} %copy-done.18), channel_id=1, source_target_pairs={{0,1},{1,0},{2,3},{3,2},{4,5},{5,4},{6,7},{7,6},{8,9},{9,8},{10,11... | collective-permute-start | bytes 3145736 | tf_op jit(solution)/shard_map/ppermute | solution.py:561
  94.3 4.1 %collective-permute-start.6 = (f32[8,512]{1,0:T(8,128)S(1)}, f32[8,512]{1,0:T(8,128)S(1)}, u32[]{:S(2)}, u32[]{:S(2)}) collective-permute-start(f32[8,512]{1,0:T(8,128)S(1)} %bitcast.45), channel_id=1, source_target_pairs={{0,1},{1,0},{2,3},{3,2},{4,5},{5,4},{6,7},{7,6},{8,9},{9,8},{10,11... | collective-permute-start | bytes 49160 | tf_op jit(solution)/shard_map/ppermute | solution.py:561
  99.0 1.0 copy-start.19
  100.0 1.3 copy-start.17
  110.0 30.0 %collective-permute-start.7 = (bf16[1040,512]{1,0:T(8,128)(2,1)}, bf16[1040,512]{1,0:T(8,128)(2,1)S(1)}, u32[]{:S(2)}, u32[]{:S(2)}) collective-permute-start(bf16[1040,512]{1,0:T(8,128)(2,1)} %get-tuple-element.48), channel_id=1, source_target_pairs={{0,8},{1,3},{2,10},{3,5},{4,12},{5,7},{6,14},{7,1},{8,16},{9,11},{... | collective-permute-start | bytes 3194888 | tf_op jit(solution)/shard_map/ppermute | solution.py:566
  111.2 28.8 %collective-permute-start.8 = (bf16[1040,512]{1,0:T(8,128)(2,1)}, bf16[1040,512]{1,0:T(8,128)(2,1)S(1)}, u32[]{:S(2)}, u32[]{:S(2)}) collective-permute-start(bf16[1040,512]{1,0:T(8,128)(2,1)} %get-tuple-element.49), channel_id=1, source_target_pairs={{0,16},{1,5},{2,18},{3,7},{4,20},{5,1},{6,22},{7,3},{8,24},{9,13},... | collective-permute-start | bytes 3194888 | tf_op jit(solution)/shard_map/ppermute | solution.py:566
  114.1 25.9 %collective-permute-start.9 = (bf16[1040,512]{1,0:T(8,128)(2,1)}, bf16[1040,512]{1,0:T(8,128)(2,1)S(1)}, u32[]{:S(2)}, u32[]{:S(2)}) collective-permute-start(bf16[1040,512]{1,0:T(8,128)(2,1)} %get-tuple-element.50), channel_id=1, source_target_pairs={{0,24},{1,7},{2,26},{3,1},{4,28},{5,3},{6,30},{7,5},{8,0},{9,15},{... | collective-permute-start | bytes 3194888 | tf_op jit(solution)/shard_map/ppermute | solution.py:566
  140.0 1.0 copy-start.2
  140.0 1.3 copy-start.3
  140.0 1.7 copy-start.4
  145.1 30.0 %collective-permute-start.11 = (bf16[768,1024]{1,0:T(8,128)(2,1)}, bf16[768,1024]{1,0:T(8,128)(2,1)S(1)}, u32[]{:S(2)}, u32[]{:S(2)}) collective-permute-start(bf16[768,1024]{1,0:T(8,128)(2,1)} %get-tuple-element.68), channel_id=1, source_target_pairs={{1,0},{2,1},{3,2},{4,3},{5,4},{6,5},{7,6},{8,7},{9,8},{10,9},{11,1... | collective-permute-start | bytes 4718600 | tf_op jit(solution)/shard_map/ppermute | solution.py:740
  146.4 28.7 %collective-permute-start.10 = (bf16[512,1024]{1,0:T(8,128)(2,1)}, bf16[512,1024]{1,0:T(8,128)(2,1)S(1)}, u32[]{:S(2)}, u32[]{:S(2)}) collective-permute-start(bf16[512,1024]{1,0:T(8,128)(2,1)} %get-tuple-element.67), channel_id=1, source_target_pairs={{0,1},{1,2},{2,3},{3,4},{4,5},{5,6},{6,7},{7,8},{8,9},{9,10},{10,1... | collective-permute-start | bytes 3145736 | tf_op jit(solution)/shard_map/ppermute | solution.py:741
  149.5 11.0 %collective-permute-start.12 = (bf16[272,512]{1,0:T(8,128)(2,1)}, bf16[272,512]{1,0:T(8,128)(2,1)S(1)}, u32[]{:S(2)}, u32[]{:S(2)}) collective-permute-start(bf16[272,512]{1,0:T(8,128)(2,1)} %get-tuple-element.72), channel_id=1, source_target_pairs={{0,32},{32,64},{64,96},{96,0},{1,33},{33,65},{65,97},{97,1},{2,34}... | collective-permute-start | bytes 835592 | tf_op jit(solution)/shard_map/ppermute | solution.py:684
  151.0 16.4 %collective-permute-start.13 = (bf16[272,512]{1,0:T(8,128)(2,1)}, bf16[272,512]{1,0:T(8,128)(2,1)S(1)}, u32[]{:S(2)}, u32[]{:S(2)}) collective-permute-start(bf16[272,512]{1,0:T(8,128)(2,1)} %get-tuple-element.73), channel_id=1, source_target_pairs={{0,64},{32,96},{64,0},{96,32},{1,65},{33,97},{65,1},{97,33},{2,66}... | collective-permute-start | bytes 835592 | tf_op jit(solution)/shard_map/ppermute | solution.py:684
  153.8 13.6 %collective-permute-start.14 = (bf16[272,512]{1,0:T(8,128)(2,1)}, bf16[272,512]{1,0:T(8,128)(2,1)S(1)}, u32[]{:S(2)}, u32[]{:S(2)}) collective-permute-start(bf16[272,512]{1,0:T(8,128)(2,1)} %get-tuple-element.74), channel_id=1, source_target_pairs={{0,96},{32,0},{64,32},{96,64},{1,97},{33,1},{65,33},{97,65},{2,98}... | collective-permute-start | bytes 835592 | tf_op jit(solution)/shard_map/ppermute | solution.py:684
  160.5 6.9 %copy-start.6 = (bf16[272,512]{1,0:T(8,128)(2,1)}, bf16[272,512]{1,0:T(8,128)(2,1)S(1)}, u32[]{:S(2)}) copy-start(bf16[272,512]{1,0:T(8,128)(2,1)S(1)} %collective-permute-done.12.refs_1_) | copy-start | bytes 835588
  167.4 0.7 copy-start.7
  168.1 0.7 copy-start.8
  170.9 9.6 %collective-permute-start.15 = (bf16[320,128]{1,0:T(8,128)(2,1)}, bf16[320,128]{1,0:T(8,128)(2,1)S(1)}, u32[]{:S(2)}, u32[]{:S(2)}) collective-permute-start(bf16[320,128]{1,0:T(8,128)(2,1)} %get-tuple-element.76), channel_id=1, source_target_pairs={{0,2},{1,9},{2,4},{3,11},{4,6},{5,13},{6,0},{7,15},{8,10},{9,17},{... | collective-permute-start | bytes 245768 | tf_op jit(solution)/shard_map/ppermute | solution.py:566
  171.5 9.0 %collective-permute-start.16 = (bf16[320,128]{1,0:T(8,128)(2,1)}, bf16[320,128]{1,0:T(8,128)(2,1)S(1)}, u32[]{:S(2)}, u32[]{:S(2)}) collective-permute-start(bf16[320,128]{1,0:T(8,128)(2,1)} %get-tuple-element.77), channel_id=1, source_target_pairs={{0,4},{1,17},{2,6},{3,19},{4,0},{5,21},{6,2},{7,23},{8,12},{9,25},... | collective-permute-start | bytes 245768 | tf_op jit(solution)/shard_map/ppermute | solution.py:566
  173.0 7.5 %collective-permute-start.17 = (bf16[320,128]{1,0:T(8,128)(2,1)}, bf16[320,128]{1,0:T(8,128)(2,1)S(1)}, u32[]{:S(2)}, u32[]{:S(2)}) collective-permute-start(bf16[320,128]{1,0:T(8,128)(2,1)} %get-tuple-element.78), channel_id=1, source_target_pairs={{0,6},{1,25},{2,0},{3,27},{4,2},{5,29},{6,4},{7,31},{8,14},{9,1},{... | collective-permute-start | bytes 245768 | tf_op jit(solution)/shard_map/ppermute | solution.py:566
  175.1 1.0 copy-start.5
  175.1 1.5 copy-start.1
  180.5 0.6 copy-start.9
  180.5 0.6 copy-start.10
  180.5 0.6 copy-start.11
  182.8 4.5 %collective-permute-start.20 = (bf16[256,128]{1,0:T(8,128)(2,1)}, bf16[256,128]{1,0:T(8,128)(2,1)S(1)}, u32[]{:S(2)}, u32[]{:S(2)}) collective-permute-start(bf16[256,128]{1,0:T(8,128)(2,1)} %get-tuple-element.79.refs_0_), channel_id=1, source_target_pairs={{0,96},{32,0},{64,32},{96,64},{1,97},{33,1},{65,33},{97,65},{2,98}... | collective-permute-start | bytes 196616 | tf_op jit(solution)/shard_map/ppermute | solution.py:684
  184.5 6.0 %collective-permute-start.19 = (bf16[256,128]{1,0:T(8,128)(2,1)}, bf16[256,128]{1,0:T(8,128)(2,1)S(1)}, u32[]{:S(2)}, u32[]{:S(2)}) collective-permute-start(bf16[256,128]{1,0:T(8,128)(2,1)} %get-tuple-element.79.refs_0_), channel_id=1, source_target_pairs={{0,64},{32,96},{64,0},{96,32},{1,65},{33,97},{65,1},{97,33},{2,66}... | collective-permute-start | bytes 196616 | tf_op jit(solution)/shard_map/ppermute | solution.py:684
  185.7 5.7 %collective-permute-start.18 = (bf16[256,128]{1,0:T(8,128)(2,1)}, bf16[256,128]{1,0:T(8,128)(2,1)S(1)}, u32[]{:S(2)}, u32[]{:S(2)}) collective-permute-start(bf16[256,128]{1,0:T(8,128)(2,1)} %get-tuple-element.79.refs_0_), channel_id=1, source_target_pairs={{0,32},{32,64},{64,96},{96,0},{1,33},{33,65},{65,97},{97,1},{2,34}... | collective-permute-start | bytes 196616 | tf_op jit(solution)/shard_map/ppermute | solution.py:684
  187.3 4.1 %copy-start.12 = (bf16[256,128]{1,0:T(8,128)(2,1)}, bf16[256,128]{1,0:T(8,128)(2,1)S(1)}, u32[]{:S(2)}) copy-start(bf16[256,128]{1,0:T(8,128)(2,1)S(1)} %collective-permute-done.20.refs_3_) | copy-start | bytes 196612
  190.5 0.9 copy-start.13
  191.4 0.6 copy-start.14
Sparse Core Ops, SparseCore 0:
  10.3 63.0 all-gather.1

commit v6 on v5

--- a/solution.py
+++ b/solution.py
@@ -583,66 +583,68 @@
     return value[:rows] + value[rows:]
 
 
-def first_sum_kernel(place_ref, *refs):
+def first_sum_kernel(*refs):
     parts, outs = refs[:4], refs[4:]
     width = parts[0].shape[0] - 16
-    quarter = width // RING
-    gain = halves(joined(total_of([ref[width:, :] for ref in parts])))
-    for k in (1, 2, 3, 0):
-        rows = pl.ds(pl.multiple_of((place_ref[3] + k) % RING * quarter, quarter), quarter)
-        outs[k][:quarter, :] = total_of([ref[rows, :] for ref in parts]).astype(bf16)
-        outs[k][quarter:, :] = gain
-
-
-def first_sum(place, parts):
-    width = parts[0].shape[0] - 16
-    vmem = pl.BlockSpec(memory_space=pltpu.VMEM)
-    return pl.pallas_call(
-        first_sum_kernel,
-        out_shape=[jax.ShapeDtypeStruct((width // RING + 16, 512), bf16)] * RING,
-        in_specs=[pl.BlockSpec(memory_space=pltpu.SMEM)] + [vmem] * 4,
-        out_specs=[vmem] * RING,
-        compiler_params=pltpu.CompilerParams(vmem_limit_bytes=VMEM_GRANT),
-        name="first_sum",
-    )(place, *parts)
-
-
-def second_sum_kernel(*refs):
-    parts, outs = refs[:4], refs[4:]
-    quarter = parts[0].shape[0] - 16
-    gain = joined(total_of([ref[quarter:, :] for ref in parts]))
+    gain = joined(total_of([ref[width:, :] for ref in parts]))
     gain = halves(
         jnp.concatenate([gain[:, k * LANES : (k + 1) * LANES] for k in range(RING)])
     )
     for k in range(RING):
         start = (RING - k) % RING * LANES
         columns = slice(start, start + LANES)
-        outs[k][:quarter, :] = total_of([ref[:quarter, columns] for ref in parts]).astype(bf16)
+        outs[k][:width, :] = total_of([ref[:width, columns] for ref in parts]).astype(bf16)
+        outs[k][width:, :] = gain
+
+
+def first_sum(parts):
+    width = parts[0].shape[0] - 16
+    vmem = pl.BlockSpec(memory_space=pltpu.VMEM)
+    return pl.pallas_call(
+        first_sum_kernel,
+        out_shape=[jax.ShapeDtypeStruct((width + 64, LANES), bf16)] * RING,
+        in_specs=[vmem] * 4,
+        out_specs=[vmem] * 4,
+        compiler_params=pltpu.CompilerParams(vmem_limit_bytes=VMEM_GRANT),
+        name="first_sum",
+    )(*parts)
+
+
+def second_sum_kernel(place_ref, *refs):
+    parts, outs, total = refs[:4], refs[4:8], refs[8]
+    width = total.shape[0]
+    quarter = width // RING
+    total[...] = total_of([ref[:width, :] for ref in parts])
+    gain = halves(joined(total_of([ref[width:, :] for ref in parts])))
+    for k in range(RING):
+        start = pl.multiple_of((place_ref[3] + k) % RING * quarter, quarter)
+        outs[k][:quarter, :] = total[pl.ds(start, quarter), :].astype(bf16)
         outs[k][quarter:, :] = gain
 
 
-def second_sum(parts):
-    quarter = parts[0].shape[0] - 16
+def second_sum(place, parts):
+    width = parts[0].shape[0] - 64
     vmem = pl.BlockSpec(memory_space=pltpu.VMEM)
     return pl.pallas_call(
         second_sum_kernel,
-        out_shape=[jax.ShapeDtypeStruct((quarter + 64, LANES), bf16)] * RING,
-        in_specs=[vmem] * 4,
+        out_shape=[jax.ShapeDtypeStruct((width // RING + 64, LANES), bf16)] * RING,
+        in_specs=[pl.BlockSpec(memory_space=pltpu.SMEM)]
+        + [vmem] * 4,
         out_specs=[vmem] * RING,
-        compiler_params=pltpu.CompilerParams(vmem_limit_bytes=VMEM_GRANT),
+        scratch_shapes=[pltpu.VMEM((width, LANES), f32)],
         name="second_sum",
-    )(*parts)
+    )(place, *parts)
 
 
 def last_sum_kernel(*refs):
-    parts, part_ref, gain_ref = refs[:4], refs[5], refs[6]
+    parts, part_ref, gain_ref = refs[:4], refs[4], refs[5]
     quarter = part_ref.shape[0]
     total = total_of([ref[...] for ref in parts])
     part_ref[...] = total[:quarter, :].astype(bf16)
     gain_ref[...] = joined(total[quarter:, :])
 
 
-def last_sum(parts, after):
+def last_sum(parts):
     quarter = parts[0].shape[0] - 64
     vmem = pl.BlockSpec(memory_space=pltpu.VMEM)
     return pl.pallas_call(
@@ -651,10 +653,10 @@
             jax.ShapeDtypeStruct((quarter, LANES), bf16),
             jax.ShapeDtypeStruct((32, LANES), f32),
         ],
-        in_specs=[vmem] * 4 + [pl.BlockSpec(memory_space=pl.ANY)],
+        in_specs=[vmem] * 4,
         out_specs=[vmem] * 2,
         name="last_sum",
-    )(*parts, after)
+    )(*parts)
 
 
 def finish_kernel(place_ref, *refs):
@@ -735,14 +737,13 @@
     inputs = common + (attended, level, d_attended)
     d_query, d_keys, d_values, d_low, d_high = backward_call(inputs, to_send[0])
     from_ring, d_query = lax.optimization_barrier((from_ring, d_query))
-    to_send, d_low, d_high = lax.optimization_barrier((first_sum(place, from_ring), d_low, d_high))
-    from_streams = stream_ring(to_send)
+    from_ring = ring(first_sum(from_ring), "second")
+    from_ring, d_low, d_high = lax.optimization_barrier((from_ring, d_low, d_high))
     from_above = lax.ppermute(d_low, "seq", downward)
     from_below = lax.ppermute(d_high, "seq", upward)
-    from_ring = ring(second_sum(from_streams), "second")
+    part, gain = last_sum(stream_ring(second_sum(place, from_ring)))
+    d_proj = finish_call(place, stream_ring([part] * RING))
     d_keys, d_values = rim_call(d_keys, d_values, from_below, from_above)
-    part, gain = last_sum(from_ring, d_keys)
-    d_proj = finish_call(place, stream_ring([part] * RING))
     d_gain = gain.reshape(-1)
     return (d_query[None], d_keys[None], d_values[None], d_proj, d_gain)
 

time: 201 us -> 200 us (level)
    ppermute x6, waiting for transfers between devices: 17.3 us -> 8.45 us  [stream_ring(): lax.ppermute(values[k], 'dp', [(i, (i + k) % count) for i in range(count)])]
    ppermute x6, waiting for transfers between devices: 0.02 us -> 7.49 us  [ring(): lax.ppermute(values[k], 'seq', along(which, k))]
  transfers between devices with their start and end apart: 22 -> 22, of which waited for: 7 -> 9; matrix products, arithmetic and copies ran while one was open for 6% -> 6% of each run, Pallas kernels for 22% -> 22%
where the time goes in v6:
time: 200 us; the launch traced here: 199 us
  Pallas kernels  79.3 us (40%)
  waiting for transfers between devices  50.3 us (25%)
  starting transfers between devices  34.5 us (17%)
  local copies, waits for them, and re-layouts  14.5 us (7%)
  between operations  14.3 us (7%)
  other arithmetic  5.89 us (3%)
    all_gather x1, waiting for transfers between devices, on_device(): weights = lax.all_gather(proj_weight, 'seq', axis=0, tiled=True)  29.9 us
    pallas_call x1, Pallas kernels, backward_call(): pl.pallas_call(backward_kernel, out_shape=[jax.ShapeDtypeStruct((count, w...  24.5 us
    pallas_call x1, Pallas kernels, latent_call(): pl.pallas_call(latent_kernel, out_shape=[jax.ShapeDtypeStruct((patches, c...  19.2 us
    pallas_call x1, Pallas kernels, forward_call(): pl.pallas_call(forward_kernel, out_shape=[jax.ShapeDtypeStruct((patches,...  13.8 us
    ppermute x6, starting transfers between devices, ring(): lax.ppermute(values[k], 'seq', along(which, k))  9.8 us
    ppermute x6, starting transfers between devices, stream_ring(): lax.ppermute(values[k], 'dp', [(i, (i + k) % count) for i in range(count)])  9.75 us
    pallas_call x1, Pallas kernels, d_proj_call(): pl.pallas_call(d_proj_kernel, out_shape=[jax.ShapeDtypeStruct((width + 16...  8.69 us
    ppermute x6, waiting for transfers between devices, stream_ring(): lax.ppermute(values[k], 'dp', [(i, (i + k) % count) for i in range(count)])  8.45 us
  transfers between devices with their start and end apart: 22, of which 9 were waited for; matrix products, arithmetic and copies ran while one was open for 6% of the time, Pallas kernels for 22%

profile of v6, /device:TPU:0, one launch (start us, length us, event | category | flops | bytes accessed | tf_op | source)
XLA Modules:
  0.0 198.9 jit_solution(17712816787781426542)
XLA Ops:
  7.9 0.7 slice.49
  8.6 1.3 collective-permute-start.1
  9.9 0.7 slice_reduce_fusion
  10.6 3.0 %collective-permute-start = (s32[384]{0:T(512)S(1)}, s32[384]{0:T(512)S(1)}, u32[]{:S(2)}, u32[]{:S(2)}) collective-permute-start(s32[384]{0:T(512)S(1)} %slice_reduce_fusion), channel_id=1, source_target_pairs={{0,1},{1,2},{2,3},{3,4},{4,5},{5,6},{6,7},{7,8},{8,9},{9,10},{10,1... | collective-permute-start | bytes 4616 | tf_op jit(solution)/shard_map/ppermute | solution.py:703
  13.6 1.3 slice_bitcast_fusion.2
  14.9 1.0 pad_maximum_fusion.1
  15.9 1.4 collective-permute-start.3
  17.3 1.5 slice_bitcast_fusion
  19.0 3.8 %collective-permute-start.2 = (bf16[768,1024]{1,0:T(8,128)(2,1)S(1)}, bf16[768,1024]{1,0:T(8,128)(2,1)S(1)}, u32[]{:S(2)}, u32[]{:S(2)}) collective-permute-start(bf16[768,1024]{1,0:T(8,128)(2,1)S(1)} %pad_maximum_fusion), channel_id=1, source_target_pairs={{0,1},{1,2},{2,3},{3,4},{4,5},{5,6},{6,7},{7,8},{8,9},{9,10},{10,1... | collective-permute-start | bytes 4718600 | tf_op jit(solution)/shard_map/ppermute | solution.py:707
  24.3 0.9 select_reduce_fusion
  25.2 1.3 convert_reduce_fusion
  28.6 1.1 copy-done
  29.7 13.8 %attention_forward.1 = (bf16[512,1024]{1,0:T(8,128)(2,1)}, f32[64,128]{1,0:T(8,128)}) custom-call(s32[8]{0:T(128)} %get-tuple-element.84.offset_ref, s32[8]{0:T(128)} %get-tuple-element.83.short_ref, s32[64,128]{1,0:T(8,128)} %pad_bitcast_fusion.span_ref, bf16[768,1024]{1,0:T(8,128)(2,1)} %copy-done, bf16[512,1024]{1,0:T(8,128)(2,1)} %collective-permute-done.3.high_ref, ...), custom_call_target="tpu_custom_call" | custom-call | flops 1241513984 | bytes 20971520 | tf_op jit(solution)/shard_map/attention_forward/pallas_call | solution.py:230
  43.5 29.9 %all-gather.2.cloned.1.call-done.weights_ref = bf16[4096,1024]{1,0:T(8,128)(2,1)} async-done(((bf16[128,1024]{1,0:T(8,128)(2,1)}), bf16[4096,1024]{1,0:T(8,128)(2,1)}) %all-gather.2.cloned.1.call-update) | async-done | bytes 8388624 | tf_op jit(solution)/shard_map/all_gather | solution.py:708
  73.4 19.2 %latent.1 = (bf16[512,2048]{1,0:T(8,128)(2,1)}, bf16[512,2048]{1,0:T(8,128)(2,1)}, f32[256,128]{1,0:T(8,128)}, bf16[512,1024]{1,0:T(8,128)(2,1)}) custom-call(s32[4]{0:T(128)} %pad_add_fusion.1.place_ref, bf16[512,1024]{1,0:T(8,128)(2,1)} %get-tuple-element.43.attended_ref, f32[1,4096]{1,0:T(1,128)} %bitcast.56, bf16[512,4096]{1,0:T(8,128)(2,1)} %bitcast.55, ...), custom_call_target="tpu_custom_call" | custom-call | flops 8589934592 | bytes 18874368 | tf_op jit(solution)/shard_map/latent/pallas_call | solution.py:414
  93.4 0.9 slice.60
  94.6 3.8 %collective-permute-done.6 = f32[8,512]{1,0:T(8,128)S(1)} collective-permute-done((f32[8,512]{1,0:T(8,128)S(1)}, f32[8,512]{1,0:T(8,128)S(1)}, u32[]{:S(2)}, u32[]{:S(2)}) %collective-permute-start.6) | collective-permute-done | bytes 16416 | tf_op jit(solution)/shard_map/ppermute | solution.py:561
  99.0 1.0 copy-done.19
  100.0 1.3 copy-done.17
  101.3 8.7 %d_proj.1 = (bf16[1040,512]{1,0:T(8,128)(2,1)}, bf16[1040,512]{1,0:T(8,128)(2,1)}, bf16[1040,512]{1,0:T(8,128)(2,1)}, bf16[1040,512]{1,0:T(8,128)(2,1)}) custom-call(bf16[512,2048]{1,0:T(8,128)(2,1)} %get-tuple-element.44.mine_ref, bf16[512,2048]{1,0:T(8,128)(2,1)} %copy-done.17, bf16[512,1024]{1,0:T(8,128)(2,1)} %get-tuple-element.43.attended_ref, ...), custom_call_target="tpu_custom_call" | custom-call | flops 4294967296 | bytes 12582912 | tf_op jit(solution)/shard_map/d_proj/pallas_call | solution.py:483
  110.0 1.2 collective-permute-start.7
  111.2 2.9 %collective-permute-start.8 = (bf16[1040,512]{1,0:T(8,128)(2,1)}, bf16[1040,512]{1,0:T(8,128)(2,1)S(1)}, u32[]{:S(2)}, u32[]{:S(2)}) collective-permute-start(bf16[1040,512]{1,0:T(8,128)(2,1)} %get-tuple-element.49), channel_id=1, source_target_pairs={{0,16},{1,5},{2,18},{3,7},{4,20},{5,1},{6,22},{7,3},{8,24},{9,13},... | collective-permute-start | bytes 3194888 | tf_op jit(solution)/shard_map/ppermute | solution.py:566
  114.1 1.4 collective-permute-start.9
  115.4 24.5 %attention_backward.1 = (bf16[512,1024]{1,0:T(8,128)(2,1)}, bf16[2048,1024]{1,0:T(8,128)(2,1)}, bf16[2048,1024]{1,0:T(8,128)(2,1)}, bf16[768,1024]{1,0:T(8,128)(2,1)}, bf16[512,1024]{1,0:T(8,128)(2,1)}) custom-call(s32[8]{0:T(128)} %get-tuple-element.84.offset_ref, s32[8]{0:T(128)} %get-tuple-element.83.short_ref, s32[64,128]{1,0:T(8,128)} %pad_bitcast_fusion.span_ref, ...), custom_call_target="tpu_custom_call" | custom-call | flops 4345298944 | bytes 41943040 | tf_op jit(solution)/shard_map/attention_backward/pallas_call | solution.py:264
  140.0 1.0 copy-done.2
  141.7 3.4 %first_sum.1 = (bf16[1088,128]{1,0:T(8,128)(2,1)}, bf16[1088,128]{1,0:T(8,128)(2,1)}, bf16[1088,128]{1,0:T(8,128)(2,1)}, bf16[1088,128]{1,0:T(8,128)(2,1)}) custom-call(bf16[1040,512]{1,0:T(8,128)(2,1)} %get-tuple-element.57.after_ref.refs_0_, bf16[1040,512]{1,0:T(8,128)(2,1)} %copy-done.2, bf16[1040,512]{1,0:T(8,128)(2,1)} %copy-done.3, ...), custom_call_target="tpu_custom_call" | custom-call | tf_op jit(solution)/shard_map/first_sum/pallas_call | solution.py:603
  145.3 2.8 %collective-permute-start.11 = (bf16[1088,128]{1,0:T(8,128)(2,1)}, bf16[1088,128]{1,0:T(8,128)(2,1)S(1)}, u32[]{:S(2)}, u32[]{:S(2)}) collective-permute-start(bf16[1088,128]{1,0:T(8,128)(2,1)} %get-tuple-element.63), channel_id=1, source_target_pairs={{0,4},{1,17},{2,6},{3,19},{4,0},{5,21},{6,2},{7,23},{8,12},{9,25},... | collective-permute-start | bytes 835592 | tf_op jit(solution)/shard_map/ppermute | solution.py:566
  148.1 1.4 collective-permute-start.12
  149.5 6.6 %collective-permute-done.10.refs_1_ = bf16[1088,128]{1,0:T(8,128)(2,1)S(1)} collective-permute-done((bf16[1088,128]{1,0:T(8,128)(2,1)}, bf16[1088,128]{1,0:T(8,128)(2,1)S(1)}, u32[]{:S(2)}, u32[]{:S(2)}) %collective-permute-start.10) | collective-permute-done | bytes 278560 | tf_op jit(solution)/shard_map/ppermute | solution.py:566
  156.1 0.9 collective-permute-done.12.refs_3_
  157.0 1.3 collective-permute-start.14
  158.2 3.1 %collective-permute-start.13 = (bf16[512,1024]{1,0:T(8,128)(2,1)}, bf16[512,1024]{1,0:T(8,128)(2,1)S(1)}, u32[]{:S(2)}, u32[]{:S(2)}) collective-permute-start(bf16[512,1024]{1,0:T(8,128)(2,1)} %get-tuple-element.67), channel_id=1, source_target_pairs={{0,1},{1,2},{2,3},{3,4},{4,5},{5,6},{6,7},{7,8},{8,9},{9,10},{10,1... | collective-permute-start | bytes 3145736 | tf_op jit(solution)/shard_map/ppermute | solution.py:743
  161.4 2.2 %second_sum.1 = (bf16[320,128]{1,0:T(8,128)(2,1)}, bf16[320,128]{1,0:T(8,128)(2,1)}, bf16[320,128]{1,0:T(8,128)(2,1)}, bf16[320,128]{1,0:T(8,128)(2,1)}) custom-call(s32[4]{0:T(128)} %pad_add_fusion.1.place_ref, bf16[1088,128]{1,0:T(8,128)(2,1)} %get-tuple-element.71.refs_0_, bf16[1088,128]{1,0:T(8,128)(2,1)} %copy-done.6, bf16[1088,128]{1,0:T(8,128)(2,1)} %copy-done.7, ...), custom_call_target="tpu_custom_call" | custom-call | tf_op jit(solution)/shard_map/second_sum/pallas_call | solution.py:628
  163.6 1.5 collective-permute-start.15
  165.1 2.8 %collective-permute-start.16 = (bf16[320,128]{1,0:T(8,128)(2,1)}, bf16[320,128]{1,0:T(8,128)(2,1)S(1)}, u32[]{:S(2)}, u32[]{:S(2)}) collective-permute-start(bf16[320,128]{1,0:T(8,128)(2,1)} %get-tuple-element.77), channel_id=1, source_target_pairs={{0,64},{32,96},{64,0},{96,32},{1,65},{33,97},{65,1},{97,33},{2,66}... | collective-permute-start | bytes 245768 | tf_op jit(solution)/shard_map/ppermute | solution.py:686
  167.9 1.4 collective-permute-start.17
  169.3 0.7 collective-permute-done.15.refs_1_
  170.0 2.8 %collective-permute-done.16.refs_2_ = bf16[320,128]{1,0:T(8,128)(2,1)S(1)} collective-permute-done((bf16[320,128]{1,0:T(8,128)(2,1)}, bf16[320,128]{1,0:T(8,128)(2,1)S(1)}, u32[]{:S(2)}, u32[]{:S(2)}) %collective-permute-start.16) | collective-permute-done | bytes 81952 | tf_op jit(solution)/shard_map/ppermute | solution.py:686
  173.4 1.7 last_sum.1
  175.1 2.4 %collective-permute-start.20 = (bf16[256,128]{1,0:T(8,128)(2,1)}, bf16[256,128]{1,0:T(8,128)(2,1)S(1)}, u32[]{:S(2)}, u32[]{:S(2)}) collective-permute-start(bf16[256,128]{1,0:T(8,128)(2,1)} %get-tuple-element.79.refs_0_), channel_id=1, source_target_pairs={{0,96},{32,0},{64,32},{96,64},{1,97},{33,1},{65,33},{97,65},{2,98}... | collective-permute-start | bytes 196616 | tf_op jit(solution)/shard_map/ppermute | solution.py:686
  177.5 1.0 collective-permute-start.19
  178.5 0.7 collective-permute-start.18
  179.2 0.8 collective-permute-done.20.refs_3_
  180.0 3.4 %collective-permute-done.19.refs_2_ = bf16[256,128]{1,0:T(8,128)(2,1)S(1)} collective-permute-done((bf16[256,128]{1,0:T(8,128)(2,1)}, bf16[256,128]{1,0:T(8,128)(2,1)S(1)}, u32[]{:S(2)}, u32[]{:S(2)}) %collective-permute-start.19) | collective-permute-done | bytes 65568 | tf_op jit(solution)/shard_map/ppermute | solution.py:686
  183.4 0.7 collective-permute-done.18.refs_1_
  184.8 1.9 d_proj_rows.1
  186.7 1.0 copy-done.5
  188.2 3.8 %rims.1 = (bf16[2048,1024]{1,0:T(8,128)(2,1)}, bf16[2048,1024]{1,0:T(8,128)(2,1)}) custom-call(bf16[2048,1024]{1,0:T(8,128)(2,1)} %get-tuple-element.55.key_in, bf16[2048,1024]{1,0:T(8,128)(2,1)} %get-tuple-element.56.value_in, bf16[512,1024]{1,0:T(8,128)(2,1)} %copy-done.5, bf16[768,1024]{1,0:T(8,128)(2,1)} %copy-done.1), custom_call_target="tpu_custom_call", output_to_operand_aliasing={{0}: (0, {}), {1}: (1, {})} | custom-call | tf_op jit(solution)/shard_map/rims/pallas_call | solution.py:535
  (73 shorter events, 8.7 us)
Async XLA Ops:
  7.2 66.2 %all-gather.2.cloned.1.call-start = ((), (), s32[]{:S(2)}) async-start(), calls=%async_computation | async-start | bytes 8650752 | tf_op jit(solution)/shard_map/all_gather | solution.py:708
  8.6 15.7 %collective-permute-start.1 = (s32[256]{0:T(256)S(1)}, s32[256]{0:T(256)S(1)}, u32[]{:S(2)}, u32[]{:S(2)}) collective-permute-start(s32[256]{0:T(256)S(1)} %bitcast.54), channel_id=1, source_target_pairs={{1,0},{2,1},{3,2},{4,3},{5,4},{6,5},{7,6},{8,7},{9,8},{10,9},{11,1... | collective-permute-start | bytes 3080 | tf_op jit(solution)/shard_map/ppermute | solution.py:704
  10.6 13.7 %collective-permute-start = (s32[384]{0:T(512)S(1)}, s32[384]{0:T(512)S(1)}, u32[]{:S(2)}, u32[]{:S(2)}) collective-permute-start(s32[384]{0:T(512)S(1)} %slice_reduce_fusion), channel_id=1, source_target_pairs={{0,1},{1,2},{2,3},{3,4},{4,5},{5,6},{6,7},{7,8},{8,9},{9,10},{10,1... | collective-permute-start | bytes 4616 | tf_op jit(solution)/shard_map/ppermute | solution.py:703
  15.9 6.9 %copy-start.16 = (s32[1,512]{1,0:T(1,128)S(1)}, s32[1,512]{1,0:T(1,128)}, u32[]{:S(2)}) copy-start(s32[1,512]{1,0:T(1,128)} %param.12) | copy-start | bytes 6148
  15.9 8.4 %copy-start.15 = (s32[1,2048]{1,0:T(1,128)S(1)}, s32[1,2048]{1,0:T(1,128)}, u32[]{:S(2)}) copy-start(s32[1,2048]{1,0:T(1,128)} %param.10) | copy-start | bytes 24580
  15.9 12.7 %collective-permute-start.3 = (bf16[512,1024]{1,0:T(8,128)(2,1)}, bf16[512,1024]{1,0:T(8,128)(2,1)}, u32[]{:S(2)}, u32[]{:S(2)}) collective-permute-start(bf16[512,1024]{1,0:T(8,128)(2,1)} %pad_maximum_fusion.1), channel_id=1, source_target_pairs={{1,0},{2,1},{3,2},{4,3},{5,4},{6,5},{7,6},{8,7},{9,8},{10,9},{11,1... | collective-permute-start | bytes 3145736 | tf_op jit(solution)/shard_map/ppermute | solution.py:707
  19.0 9.6 %collective-permute-start.2 = (bf16[768,1024]{1,0:T(8,128)(2,1)S(1)}, bf16[768,1024]{1,0:T(8,128)(2,1)S(1)}, u32[]{:S(2)}, u32[]{:S(2)}) collective-permute-start(bf16[768,1024]{1,0:T(8,128)(2,1)S(1)} %pad_maximum_fusion), channel_id=1, source_target_pairs={{0,1},{1,2},{2,3},{3,4},{4,5},{5,6},{6,7},{7,8},{8,9},{9,10},{10,1... | collective-permute-start | bytes 4718600 | tf_op jit(solution)/shard_map/ppermute | solution.py:707
  28.6 1.1 copy-start
  73.4 19.7 %copy-start.18 = (bf16[512,1024]{1,0:T(8,128)(2,1)S(1)}, bf16[512,1024]{1,0:T(8,128)(2,1)}, u32[]{:S(2)}) copy-start(bf16[512,1024]{1,0:T(8,128)(2,1)} %get-tuple-element.43.attended_ref) | copy-start | bytes 3145732
  92.6 6.4 %collective-permute-start.4 = (bf16[512,2048]{1,0:T(8,128)(2,1)}, bf16[512,2048]{1,0:T(8,128)(2,1)S(1)}, u32[]{:S(2)}, u32[]{:S(2)}) collective-permute-start(bf16[512,2048]{1,0:T(8,128)(2,1)} %get-tuple-element.45), channel_id=1, source_target_pairs={{0,1},{1,0},{2,3},{3,2},{4,5},{5,4},{6,7},{7,6},{8,9},{9,8},{10,11... | collective-permute-start | bytes 6291464 | tf_op jit(solution)/shard_map/ppermute | solution.py:561
  93.1 5.9 %collective-permute-start.5 = (bf16[512,1024]{1,0:T(8,128)(2,1)S(1)}, bf16[512,1024]{1,0:T(8,128)(2,1)S(1)}, u32[]{:S(2)}, u32[]{:S(2)}) collective-permute-start(bf16[512,1024]{1,0:T(8,128)(2,1)S(1)} %copy-done.18), channel_id=1, source_target_pairs={{0,1},{1,0},{2,3},{3,2},{4,5},{5,4},{6,7},{7,6},{8,9},{9,8},{10,11... | collective-permute-start | bytes 3145736 | tf_op jit(solution)/shard_map/ppermute | solution.py:561
  94.3 4.1 %collective-permute-start.6 = (f32[8,512]{1,0:T(8,128)S(1)}, f32[8,512]{1,0:T(8,128)S(1)}, u32[]{:S(2)}, u32[]{:S(2)}) collective-permute-start(f32[8,512]{1,0:T(8,128)S(1)} %bitcast.45), channel_id=1, source_target_pairs={{0,1},{1,0},{2,3},{3,2},{4,5},{5,4},{6,7},{7,6},{8,9},{9,8},{10,11... | collective-permute-start | bytes 49160 | tf_op jit(solution)/shard_map/ppermute | solution.py:561
  99.0 1.0 copy-start.19
  100.0 1.3 copy-start.17
  110.0 30.0 %collective-permute-start.7 = (bf16[1040,512]{1,0:T(8,128)(2,1)}, bf16[1040,512]{1,0:T(8,128)(2,1)S(1)}, u32[]{:S(2)}, u32[]{:S(2)}) collective-permute-start(bf16[1040,512]{1,0:T(8,128)(2,1)} %get-tuple-element.48), channel_id=1, source_target_pairs={{0,8},{1,3},{2,10},{3,5},{4,12},{5,7},{6,14},{7,1},{8,16},{9,11},{... | collective-permute-start | bytes 3194888 | tf_op jit(solution)/shard_map/ppermute | solution.py:566
  111.2 28.8 %collective-permute-start.8 = (bf16[1040,512]{1,0:T(8,128)(2,1)}, bf16[1040,512]{1,0:T(8,128)(2,1)S(1)}, u32[]{:S(2)}, u32[]{:S(2)}) collective-permute-start(bf16[1040,512]{1,0:T(8,128)(2,1)} %get-tuple-element.49), channel_id=1, source_target_pairs={{0,16},{1,5},{2,18},{3,7},{4,20},{5,1},{6,22},{7,3},{8,24},{9,13},... | collective-permute-start | bytes 3194888 | tf_op jit(solution)/shard_map/ppermute | solution.py:566
  114.1 25.9 %collective-permute-start.9 = (bf16[1040,512]{1,0:T(8,128)(2,1)}, bf16[1040,512]{1,0:T(8,128)(2,1)S(1)}, u32[]{:S(2)}, u32[]{:S(2)}) collective-permute-start(bf16[1040,512]{1,0:T(8,128)(2,1)} %get-tuple-element.50), channel_id=1, source_target_pairs={{0,24},{1,7},{2,26},{3,1},{4,28},{5,3},{6,30},{7,5},{8,0},{9,15},{... | collective-permute-start | bytes 3194888 | tf_op jit(solution)/shard_map/ppermute | solution.py:566
  140.0 1.0 copy-start.2
  140.0 1.3 copy-start.3
  140.0 1.7 copy-start.4
  145.1 11.0 %collective-permute-start.10 = (bf16[1088,128]{1,0:T(8,128)(2,1)}, bf16[1088,128]{1,0:T(8,128)(2,1)S(1)}, u32[]{:S(2)}, u32[]{:S(2)}) collective-permute-start(bf16[1088,128]{1,0:T(8,128)(2,1)} %get-tuple-element.62), channel_id=1, source_target_pairs={{0,2},{1,9},{2,4},{3,11},{4,6},{5,13},{6,0},{7,15},{8,10},{9,17},{... | collective-permute-start | bytes 835592 | tf_op jit(solution)/shard_map/ppermute | solution.py:566
  145.3 10.8 %collective-permute-start.11 = (bf16[1088,128]{1,0:T(8,128)(2,1)}, bf16[1088,128]{1,0:T(8,128)(2,1)S(1)}, u32[]{:S(2)}, u32[]{:S(2)}) collective-permute-start(bf16[1088,128]{1,0:T(8,128)(2,1)} %get-tuple-element.63), channel_id=1, source_target_pairs={{0,4},{1,17},{2,6},{3,19},{4,0},{5,21},{6,2},{7,23},{8,12},{9,25},... | collective-permute-start | bytes 835592 | tf_op jit(solution)/shard_map/ppermute | solution.py:566
  148.1 8.9 %collective-permute-start.12 = (bf16[1088,128]{1,0:T(8,128)(2,1)}, bf16[1088,128]{1,0:T(8,128)(2,1)S(1)}, u32[]{:S(2)}, u32[]{:S(2)}) collective-permute-start(bf16[1088,128]{1,0:T(8,128)(2,1)} %get-tuple-element.64), channel_id=1, source_target_pairs={{0,6},{1,25},{2,0},{3,27},{4,2},{5,29},{6,4},{7,31},{8,14},{9,1},{... | collective-permute-start | bytes 835592 | tf_op jit(solution)/shard_map/ppermute | solution.py:566
  156.1 5.3 %copy-start.6 = (bf16[1088,128]{1,0:T(8,128)(2,1)}, bf16[1088,128]{1,0:T(8,128)(2,1)S(1)}, u32[]{:S(2)}) copy-start(bf16[1088,128]{1,0:T(8,128)(2,1)S(1)} %collective-permute-done.10.refs_1_) | copy-start | bytes 835588
  156.1 5.3 %copy-start.7 = (bf16[1088,128]{1,0:T(8,128)(2,1)}, bf16[1088,128]{1,0:T(8,128)(2,1)S(1)}, u32[]{:S(2)}) copy-start(bf16[1088,128]{1,0:T(8,128)(2,1)S(1)} %collective-permute-done.11.refs_2_) | copy-start | bytes 835588
  157.0 4.4 %copy-start.8 = (bf16[1088,128]{1,0:T(8,128)(2,1)}, bf16[1088,128]{1,0:T(8,128)(2,1)S(1)}, u32[]{:S(2)}) copy-start(bf16[1088,128]{1,0:T(8,128)(2,1)S(1)} %collective-permute-done.12.refs_3_) | copy-start | bytes 835588
  157.0 29.7 %collective-permute-start.14 = (bf16[768,1024]{1,0:T(8,128)(2,1)}, bf16[768,1024]{1,0:T(8,128)(2,1)S(1)}, u32[]{:S(2)}, u32[]{:S(2)}) collective-permute-start(bf16[768,1024]{1,0:T(8,128)(2,1)} %get-tuple-element.68), channel_id=1, source_target_pairs={{1,0},{2,1},{3,2},{4,3},{5,4},{6,5},{7,6},{8,7},{9,8},{10,9},{11,1... | collective-permute-start | bytes 4718600 | tf_op jit(solution)/shard_map/ppermute | solution.py:742
  158.2 28.4 %collective-permute-start.13 = (bf16[512,1024]{1,0:T(8,128)(2,1)}, bf16[512,1024]{1,0:T(8,128)(2,1)S(1)}, u32[]{:S(2)}, u32[]{:S(2)}) collective-permute-start(bf16[512,1024]{1,0:T(8,128)(2,1)} %get-tuple-element.67), channel_id=1, source_target_pairs={{0,1},{1,2},{2,3},{3,4},{4,5},{5,6},{6,7},{7,8},{8,9},{9,10},{10,1... | collective-permute-start | bytes 3145736 | tf_op jit(solution)/shard_map/ppermute | solution.py:743
  163.6 6.4 %collective-permute-start.15 = (bf16[320,128]{1,0:T(8,128)(2,1)}, bf16[320,128]{1,0:T(8,128)(2,1)S(1)}, u32[]{:S(2)}, u32[]{:S(2)}) collective-permute-start(bf16[320,128]{1,0:T(8,128)(2,1)} %get-tuple-element.76), channel_id=1, source_target_pairs={{0,32},{32,64},{64,96},{96,0},{1,33},{33,65},{65,97},{97,1},{2,34}... | collective-permute-start | bytes 245768 | tf_op jit(solution)/shard_map/ppermute | solution.py:686
  165.1 7.7 %collective-permute-start.16 = (bf16[320,128]{1,0:T(8,128)(2,1)}, bf16[320,128]{1,0:T(8,128)(2,1)S(1)}, u32[]{:S(2)}, u32[]{:S(2)}) collective-permute-start(bf16[320,128]{1,0:T(8,128)(2,1)} %get-tuple-element.77), channel_id=1, source_target_pairs={{0,64},{32,96},{64,0},{96,32},{1,65},{33,97},{65,1},{97,33},{2,66}... | collective-permute-start | bytes 245768 | tf_op jit(solution)/shard_map/ppermute | solution.py:686
  167.9 4.9 %collective-permute-start.17 = (bf16[320,128]{1,0:T(8,128)(2,1)}, bf16[320,128]{1,0:T(8,128)(2,1)S(1)}, u32[]{:S(2)}, u32[]{:S(2)}) collective-permute-start(bf16[320,128]{1,0:T(8,128)(2,1)} %get-tuple-element.78), channel_id=1, source_target_pairs={{0,96},{32,0},{64,32},{96,64},{1,97},{33,1},{65,33},{97,65},{2,98}... | collective-permute-start | bytes 245768 | tf_op jit(solution)/shard_map/ppermute | solution.py:686
  170.0 2.8 %copy-start.9 = (bf16[320,128]{1,0:T(8,128)(2,1)}, bf16[320,128]{1,0:T(8,128)(2,1)S(1)}, u32[]{:S(2)}) copy-start(bf16[320,128]{1,0:T(8,128)(2,1)S(1)} %collective-permute-done.15.refs_1_) | copy-start | bytes 245764
  172.8 0.6 copy-start.10
  172.8 0.7 copy-start.11
  175.1 4.9 %collective-permute-start.20 = (bf16[256,128]{1,0:T(8,128)(2,1)}, bf16[256,128]{1,0:T(8,128)(2,1)S(1)}, u32[]{:S(2)}, u32[]{:S(2)}) collective-permute-start(bf16[256,128]{1,0:T(8,128)(2,1)} %get-tuple-element.79.refs_0_), channel_id=1, source_target_pairs={{0,96},{32,0},{64,32},{96,64},{1,97},{33,1},{65,33},{97,65},{2,98}... | collective-permute-start | bytes 196616 | tf_op jit(solution)/shard_map/ppermute | solution.py:686
  177.5 6.0 %collective-permute-start.19 = (bf16[256,128]{1,0:T(8,128)(2,1)}, bf16[256,128]{1,0:T(8,128)(2,1)S(1)}, u32[]{:S(2)}, u32[]{:S(2)}) collective-permute-start(bf16[256,128]{1,0:T(8,128)(2,1)} %get-tuple-element.79.refs_0_), channel_id=1, source_target_pairs={{0,64},{32,96},{64,0},{96,32},{1,65},{33,97},{65,1},{97,33},{2,66}... | collective-permute-start | bytes 196616 | tf_op jit(solution)/shard_map/ppermute | solution.py:686
  178.5 5.7 %collective-permute-start.18 = (bf16[256,128]{1,0:T(8,128)(2,1)}, bf16[256,128]{1,0:T(8,128)(2,1)S(1)}, u32[]{:S(2)}, u32[]{:S(2)}) collective-permute-start(bf16[256,128]{1,0:T(8,128)(2,1)} %get-tuple-element.79.refs_0_), channel_id=1, source_target_pairs={{0,32},{32,64},{64,96},{96,0},{1,33},{33,65},{65,97},{97,1},{2,34}... | collective-permute-start | bytes 196616 | tf_op jit(solution)/shard_map/ppermute | solution.py:686
  180.0 4.1 %copy-start.12 = (bf16[256,128]{1,0:T(8,128)(2,1)}, bf16[256,128]{1,0:T(8,128)(2,1)S(1)}, u32[]{:S(2)}) copy-start(bf16[256,128]{1,0:T(8,128)(2,1)S(1)} %collective-permute-done.20.refs_3_) | copy-start | bytes 196612
  183.4 0.7 copy-start.13
  184.2 0.6 copy-start.14
  186.7 1.0 copy-start.5
  186.7 1.5 copy-start.1
Sparse Core Ops, SparseCore 0:
  10.3 63.0 all-gather.1
